TPU v7x, 256 devices: a whole 4x4x8 slice. The times are simulated.
256 devices in a mesh: col: 128 (over x, y, z), rep: 2 (over core).
Axes of the slice: x: 4, y: 4, z: 8, core: 2. Of those that a mesh axis runs over, the one named last changes fastest.
Arguments:
- features: bfloat16 [32768, 256], P('col'), may hold values from -6 to 6
- src_norm: bfloat16 [32768], P('col'), may hold values from 0.049804688 to 1
- dst_norm: float32 [524288], P('col'), may hold values from 0.05 to 1
- src_block: int32 [128, 2, 128], P('col', 'rep'), may hold values from 0 to 255, as said below
- dst_block: int32 [128, 2, 128], P('col', 'rep'), may hold values from 0 to 31
- counts: int32 [128, 2, 128, 128, 128], P('col', 'rep'), may hold values from 0 to 3, as said below
- weight: bfloat16 [256, 256], replicated, may hold values from -0.375 to 0.375
- out_bias: bfloat16 [256], replicated, may hold values from -3 to 3
Outputs:
- activated: bfloat16 [524288, 256], P(('col', 'rep'))
Inputs may be any that keep to these rules, and one draw needn't show every extreme that they name: For each (c, r) and each index p of col, the entries src_block[c, r, :] that lie in [p * 2, (p + 1) * 2) are all equal: a device's blocks name at most one source block of each index of col. `counts`: most entries are zero.
All inputs are finite; a program needn't handle non-finite values.
Results may differ from a plain program's by a relative error of at most 0.0055.
Values may be sent and summed in bfloat16 or wider, within the bound.
No kernel may reach another device: no remote copies, remote signals or barrier semaphores. Data moves between devices by JAX's collectives and lax.ppermute only.
A program may use at most 128 MiB of HBM per device.

v0:
```python
import jax
import jax.numpy as jnp
from jax import lax
from jax.sharding import PartitionSpec as P

BLOCK = 128
DST_BLK = 32


def body(features, src_norm, dst_norm, src_block, dst_block, counts, weight, out_bias):
    width = features.shape[1]
    src_ids = src_block.reshape(-1)
    dst_ids = dst_block.reshape(-1)
    rep_index = lax.axis_index("rep")
    all_feat, all_norm = (
        lax.all_gather(features, "col", axis=0, tiled=True),
        lax.all_gather(src_norm, "col", axis=0, tiled=True),
    )
    gathered = all_feat.reshape(-1, BLOCK, width)[src_ids]
    norm_vals = all_norm.reshape(-1, BLOCK)[src_ids]
    tile_vals = (
        counts.reshape(-1, BLOCK, BLOCK).astype(jnp.float32)
        * norm_vals.astype(jnp.float32)[:, None, :]
    ).astype(jnp.bfloat16)
    products = jnp.einsum("bij,bjf->bif", tile_vals, gathered, preferred_element_type=jnp.float32)
    summed = jax.ops.segment_sum(products, dst_ids, num_segments=DST_BLK)
    partial_rows = summed.reshape(DST_BLK * BLOCK, width)
    half_rows = partial_rows.shape[0] // 2
    own_norm_rows = lax.dynamic_slice_in_dim(dst_norm, rep_index * half_rows, half_rows, 0)
    combined = lax.psum(partial_rows, "rep")
    own_rows = lax.dynamic_slice_in_dim(combined, rep_index * half_rows, half_rows, 0)
    aggregate = own_rows * own_norm_rows[:, None]
    hidden = aggregate.astype(jnp.bfloat16)
    result = jnp.dot(hidden, weight, preferred_element_type=jnp.float32) + out_bias.astype(
        jnp.float32
    )
    return jax.nn.relu(result).astype(jnp.bfloat16)


def solution(mesh):
    placed = (
        P("col", None),
        P("col"),
        P("col"),
        P("col", "rep", None),
        P("col", "rep", None),
        P("col", "rep", None, None, None),
        P(),
        P(),
    )
    return jax.shard_map(
        body, mesh=mesh, in_specs=placed, out_specs=P(("col", "rep"), None), check_vma=False
    )
```

profile of v0, /device:TPU:1, one launch (start us, length us, event | category | flops | bytes accessed | tf_op | source)
XLA Modules:
  0.0 465.6 jit_solution(3929812493721058903)
XLA Ops:
  6.5 0.0 copy-start
  6.5 0.0 all-gather.3.cloned.1.call-start
  6.5 0.7 all-gather.3.cloned.1.call-update
  7.3 0.0 all-reduce.2.cloned.1.call-start
  7.3 0.7 reshape.76
  8.0 293.8 %all-gather = bf16[128,1,256]{2,1,0:T(2,128)(2,1)S(1)} all-gather(bf16[1,1,256]{2,1,0:T(2,128)(2,1)S(1)} %reshape.76), channel_id=1, replica_groups=mesh['col'=128,'rep'=2] {'col'}, dimensions={0}, use_global_device_ids=true | all-gather | bytes 66048 | tf_op jit(solution)/shard_map/all_gather | solution.py:17
  301.8 0.4 reduce
  302.2 0.7 fusion.7
  302.9 0.7 gather_fusion
  303.6 0.0 all-gather.3.cloned.1.call-done
  303.6 12.3 %gather_fusion.1 = bf16[128,128,256]{2,1,0:T(8,128)(2,1)} fusion(bf16[256,128,256]{2,1,0:T(8,128)(2,1)} %bitcast.15, s32[1024]{0:T(1024)S(1)} %pad_clamp_fusion), kind=kCustom, calls=%fused_computation.1 | custom fusion | bytes 16777728 | tf_op jit(solution)/shard_map/gather | solution.py:19
  316.0 0.0 copy-start.2
  316.0 13.8 %fusion.1 = f32[128,128,256]{2,1,0:T(8,128)} fusion(bf16[128,128,256]{2,1,0:T(8,128)(2,1)} %gather_fusion.1, s32[1,1,128,128,128]{4,3,2,1,0:T(8,128)} %param.13, f32[128,128]{1,0:T(8,128)S(1)} %convert_element_type.27), kind=kOutput, calls=%fused_computation.5 | convolution fusion | flops 1080033280 | bytes 33619968 | tf_op jit(solution)/shard_map/bij,bjf->bif/dot_general | solution.py:25
  329.8 2.4 broadcast_in_dim.2
  332.2 0.0 copy-done.2
  332.2 0.0 copy-start.3
  332.2 0.0 copy-start.1
  332.2 37.0 %scatter_fusion = f32[32,128,256]{2,1,0:T(8,128)} fusion(f32[32,128,256]{2,1,0:T(8,128)} %broadcast_in_dim.2, s32[128]{0:T(128)S(1)} %bitcast.16, f32[128,128,256]{2,1,0:T(8,128)} %fusion.1), kind=kCustom, calls=%fused_computation.2 | custom fusion | flops 4194304 | bytes 50332160 | tf_op jit(solution)/shard_map/scatter-add | solution.py:26
  369.2 0.0 all-reduce.2.cloned.1.call-update
  369.3 0.0 copy-done.3
  369.3 0.0 copy-done.1
  369.3 86.3 %all-reduce.2.cloned.1.call-done = f32[4096,256]{1,0:T(8,128)} async-done(((f32[4096,256]{1,0:T(8,128)}), f32[4096,256]{1,0:T(8,128)}) %all-reduce.2.cloned.1.call-update) | async-done | bytes 4194320 | tf_op jit(solution)/shard_map/psum | solution.py:30
  455.7 0.0 copy-done
  455.7 3.1 fusion.5
  (5 shorter events, 0.1 us)
Async XLA Ops:
  6.5 449.1 %copy-start = (bf16[256,256]{1,0:T(8,128)(2,1)S(1)}, bf16[256,256]{1,0:T(8,128)(2,1)}, u32[]{:S(2)}) copy-start(bf16[256,256]{1,0:T(8,128)(2,1)} %param.14) | copy-start | bytes 393220
  6.5 297.1 %all-gather.3.cloned.1.call-start = ((), (), s32[]{:S(2)}) async-start(), calls=%async_computation | async-start | bytes 16908288 | tf_op jit(solution)/shard_map/all_gather | solution.py:16
  7.3 448.4 %all-reduce.2.cloned.1.call-start = ((), (), s32[]{:S(2)}) async-start(), calls=%async_computation.1 | async-start | bytes 8388608 | tf_op jit(solution)/shard_map/psum | solution.py:30
  316.0 16.3 %copy-start.2 = (s32[1,1,128]{2,1,0:T(1,128)S(1)}, s32[1,1,128]{2,1,0:T(1,128)}, u32[]{:S(2)}) copy-start(s32[1,1,128]{2,1,0:T(1,128)} %param.12) | copy-start | bytes 1540
  332.2 37.0 %copy-start.3 = (bf16[256]{0:T(256)(128)(2,1)S(1)}, bf16[256]{0:T(256)(128)(2,1)}, u32[]{:S(2)}) copy-start(bf16[256]{0:T(256)(128)(2,1)} %param.15) | copy-start | bytes 1540
  332.2 37.1 %copy-start.1 = (f32[4096]{0:T(1024)S(1)}, f32[4096]{0:T(1024)}, u32[]{:S(2)}) copy-start(f32[4096]{0:T(1024)} %param.10) | copy-start | bytes 49156
Sparse Core Ops, SparseCore 0:
  11.0 154.2 all-gather.2
  369.4 86.2 all-reduce.1
where the time goes:
time: 466 us
  blocking collectives  294 us (63%)
  waiting for transfers between devices  87.1 us (19%)
  other arithmetic  38.1 us (8%)
  matrix products  16.9 us (4%)
  local copies, waits for them, and re-layouts  16.2 us (3%)
  between operations  13.5 us (3%)
    all_gather x1, blocking collectives, body(): lax.all_gather(src_norm, 'col', axis=0, tiled=True)  294 us
    psum x1, waiting for transfers between devices, body(): combined = lax.psum(partial_rows, 'rep')  86.3 us
    scatter-add x1, other arithmetic, body(): summed = jax.ops.segment_sum(products, dst_ids, num_segments=DST_BLK)  37 us
    dot_general x1, matrix products, body(): jnp.einsum('bij,bjf->bif', tile_vals, gathered, preferred_element_type=jn...  13.8 us
    gather x1, local copies, waits for them, and re-layouts, body(): gathered = all_feat.reshape(-1, BLOCK, width)[src_ids]  12.3 us
  transfers between devices with their start and end apart: 2, of which 1 were waited for; matrix products, arithmetic and copies ran while one was open for 1% of the time, Pallas kernels for 0%

commit v1 on v0

v1 whole, which is shorter than its diff:
```python
import jax
import jax.numpy as jnp
from jax import lax
from jax.experimental import pallas as pl
from jax.experimental.pallas import tpu as pltpu
from jax.sharding import PartitionSpec as P

BLOCK = 128
DST_BLK = 32
WIDTH = 256
NX, NY, NZ = 4, 4, 8
GROUP = 4
HALF_ROWS = 16 * BLOCK + 16
MAX_GROUPS = 256 // GROUP + DST_BLK
SLOTS = MAX_GROUPS * GROUP
MIB = 1024 * 1024


def device(x, y, z, r):
    return (((x % NX) * NY + (y % NY)) * NZ + (z % NZ)) * 2 + r


def from_z(step):
    return [
        (device(x, y, z + step, r), device(x, y, z, r))
        for x in range(NX) for y in range(NY) for z in range(NZ) for r in range(2)
    ]


def from_second(step):
    return [
        (device(x, y + step, z, 0) if r == 0 else device(x + step, y, z, 1), device(x, y, z, r))
        for x in range(NX) for y in range(NY) for z in range(NZ) for r in range(2)
    ]


def from_third(step):
    return [
        (device(x + step, y, z, 0) if r == 0 else device(x, y + step, z, 1), device(x, y, z, r))
        for x in range(NX) for y in range(NY) for z in range(NZ) for r in range(2)
    ]


def move(value, pairs):
    return lax.ppermute(value, ("col", "rep"), pairs)


def sort_kernel(place, src, dst, start, tiles, blocks, norms, count, cursor):
    z, second, third, rep = place[0], place[1], place[2], place[3]

    def clear(k, carry):
        count[k] = 0
        return carry

    lax.fori_loop(0, DST_BLK, clear, 0)

    def blank(s, carry):
        tiles[s] = 0
        blocks[s] = 0
        norms[s] = 128
        return carry

    lax.fori_loop(0, SLOTS, blank, 0)

    def key_of(e):
        return (dst[e] + 16 * (1 - rep)) & 31

    def tally(e, carry):
        k = key_of(e)
        count[k] = count[k] + jnp.where((src[e] & 1) == rep, 1, 0)
        return carry

    lax.fori_loop(0, 256, tally, 0)

    def offsets(k, at):
        start[k] = at
        cursor[k] = at * GROUP
        return at + ((count[k] + (GROUP - 1)) >> 2)

    start[DST_BLK] = lax.fori_loop(0, DST_BLK, offsets, 0)

    def put(e, carry):
        block = src[e]

        @pl.when((block & 1) == rep)
        def _():
            k = key_of(e)
            s = cursor[k]
            cursor[k] = s + 1
            p = block >> 1
            px, py, pz = p >> 5, (p >> 3) & 3, p & 7
            pa = jnp.where(rep == 0, py, px)
            pb = jnp.where(rep == 0, px, py)
            dz, da, db = (pz - z) & 7, (pa - second) & 3, (pb - third) & 3
            index = db * 32 + da * 8 + dz
            tiles[s] = e
            blocks[s] = index
            norms[s] = index

        return carry

    lax.fori_loop(0, 256, put, 0)


def sort_blocks(place, src, dst):
    smem = pl.BlockSpec(memory_space=pltpu.SMEM)
    slots = jax.ShapeDtypeStruct((SLOTS,), jnp.int32)
    return pl.pallas_call(
        sort_kernel,
        out_shape=(jax.ShapeDtypeStruct((DST_BLK + 1,), jnp.int32), slots, slots, slots),
        in_specs=[smem] * 3,
        out_specs=(smem,) * 4,
        scratch_shapes=[pltpu.SMEM((DST_BLK,), jnp.int32), pltpu.SMEM((DST_BLK,), jnp.int32)],
    )(place, src, dst)


def sum_kernel(start, tiles, blocks, norms, *refs):
    pieces, own_tiles, other_tiles = refs[:8], refs[8], refs[9]
    sent, kept = refs[10], refs[11]
    feat, tile, norm, sems = refs[12:]
    copies = [pltpu.make_async_copy(pieces[i], feat.at[i], sems.at[i]) for i in range(8)]
    copies.append(pltpu.make_async_copy(own_tiles, tile.at[pl.ds(0, 128)], sems.at[8]))
    copies.append(pltpu.make_async_copy(other_tiles, tile.at[pl.ds(128, 128)], sems.at[9]))
    for copy in copies:
        copy.start()
    for copy in copies:
        copy.wait()
    for i in range(8):
        norm[pl.ds(16 * i, 16), :] = feat[i, pl.ds(16 * BLOCK, 16), pl.ds(0, BLOCK)].astype(jnp.float32)
    norm[pl.ds(128, 8), :] = jnp.zeros((8, BLOCK), jnp.float32)

    def add_group(g, total):
        left, right = [], []
        for u in range(GROUP):
            s = g * GROUP + u
            index = blocks[s]
            scale = norm[pl.ds(norms[s], 1), :].astype(jnp.bfloat16)
            left.append(tile[tiles[s]] * scale)
            row = pl.multiple_of((index & 15) * BLOCK, BLOCK)
            right.append(feat[index >> 4, pl.ds(row, BLOCK), :])
        return total + jnp.dot(
            jnp.concatenate(left, axis=1), jnp.concatenate(right, axis=0),
            preferred_element_type=jnp.float32,
        )

    def make(out, base):
        def rows(d, carry):
            total = lax.fori_loop(
                start[base + d], start[base + d + 1], add_group, jnp.zeros((BLOCK, WIDTH), jnp.float32)
            )
            out[pl.ds(pl.multiple_of(d * BLOCK, BLOCK), BLOCK), :] = total.astype(out.dtype)
            return carry

        lax.fori_loop(0, DST_BLK // 2, rows, 0)

    make(sent, 0)
    make(kept, DST_BLK // 2)


def sum_tiles(lists, pieces, own_tiles, other_tiles):
    smem = pl.BlockSpec(memory_space=pltpu.SMEM)
    anywhere = pl.BlockSpec(memory_space=pl.ANY)
    vmem = pl.BlockSpec(memory_space=pltpu.VMEM)
    half = DST_BLK // 2 * BLOCK
    return pl.pallas_call(
        sum_kernel,
        out_shape=(
            jax.ShapeDtypeStruct((half, WIDTH), jnp.float32),
            jax.ShapeDtypeStruct((half, WIDTH), jnp.float32),
        ),
        in_specs=[smem] * 4 + [anywhere] * 10,
        out_specs=(vmem, vmem),
        scratch_shapes=[
            pltpu.VMEM((8, HALF_ROWS, WIDTH), jnp.bfloat16),
            pltpu.VMEM((256, BLOCK, BLOCK), jnp.bfloat16),
            pltpu.VMEM((136, BLOCK), jnp.float32),
            pltpu.SemaphoreType.DMA((10,)),
        ],
        compiler_params=pltpu.CompilerParams(vmem_limit_bytes=32 * MIB),
        cost_estimate=pl.CostEstimate(flops=2 * 10**9, bytes_accessed=20 * 10**6, transcendentals=0),
    )(*lists, *pieces, own_tiles, other_tiles)


def gather_features(features, src_norm, rep):
    mine = lax.dynamic_slice_in_dim(features, rep * BLOCK, BLOCK, 0)
    my_norm = lax.dynamic_slice_in_dim(src_norm, rep * BLOCK, BLOCK, 0)
    norm_rows = jnp.zeros((16, WIDTH), jnp.bfloat16).at[0, :BLOCK].set(my_norm)
    shard = jnp.concatenate([mine, norm_rows], axis=0)
    at = {0: shard}
    for step in (1, -1, 2, -2):
        at[step] = move(shard, from_z(step))
    far = move(jnp.concatenate([at[1], at[2]], axis=0), from_z(2))
    at[3], at[4] = far[:144], far[144:]
    at[-3] = move(at[-1], from_z(-2))
    line = [at[k] for k in (0, 1, 2, 3, 4, -3, -2, -1)]
    line = jnp.concatenate(
        [s[:BLOCK] for s in line] + [s[BLOCK : BLOCK + 1] for s in line]
        + [jnp.zeros((8, WIDTH), jnp.bfloat16)], axis=0
    )
    around = [line] + [move(line, from_second(step)) for step in (1, 2, 3)]
    cut = NZ * BLOCK
    halves = [
        jnp.concatenate([a[:cut], b[:cut], a[cut : cut + 8], b[cut : cut + 8]], axis=0)
        for a, b in (around[:2], around[2:])
    ]
    up_0 = move(halves[0], from_third(1))
    down_1 = move(halves[1], from_third(-1))
    up_1 = move(halves[1], from_third(1))
    down_0 = move(halves[0], from_third(-1))
    across_0 = move(up_0, from_third(1))
    across_1 = move(down_1, from_third(-1))
    return [halves[0], halves[1], up_0, up_1, across_0, across_1, down_0, down_1]


def body(features, src_norm, dst_norm, src_block, dst_block, counts, weight, out_bias):
    rep = lax.axis_index("rep")
    col = lax.axis_index("col")
    x, y, z = col // (NY * NZ), (col // NZ) % NY, col % NZ
    swap = [(0, 1), (1, 0)]
    ids = jnp.concatenate([src_block.reshape(1, -1), dst_block.reshape(1, -1)], axis=0)
    other_ids = lax.ppermute(ids, "rep", swap)
    place = jnp.stack([z, jnp.where(rep == 0, y, x), jnp.where(rep == 0, x, y), rep]).astype(jnp.int32)
    lists = sort_blocks(
        place, jnp.concatenate([ids[0], other_ids[0]]), jnp.concatenate([ids[1], other_ids[1]])
    )
    own_tiles = counts.reshape(-1, BLOCK, BLOCK).astype(jnp.bfloat16)
    other_tiles = lax.ppermute(own_tiles, "rep", swap)
    pieces = gather_features(features, src_norm, rep)
    sent, kept = sum_tiles(lists, pieces, own_tiles, other_tiles)
    half_rows = kept.shape[0]
    own_norm = lax.dynamic_slice_in_dim(dst_norm, rep * half_rows, half_rows, 0)
    aggregate = (kept + lax.ppermute(sent, "rep", swap)) * own_norm[:, None]
    hidden = aggregate.astype(jnp.bfloat16)
    result = jnp.dot(hidden, weight, preferred_element_type=jnp.float32) + out_bias.astype(jnp.float32)
    return jax.nn.relu(result).astype(jnp.bfloat16)


def solution(mesh):
    placed = (
        P("col", None),
        P("col"),
        P("col"),
        P("col", "rep", None),
        P("col", "rep", None),
        P("col", "rep", None, None, None),
        P(),
        P(),
    )
    return jax.shard_map(
        body, mesh=mesh, in_specs=placed, out_specs=P(("col", "rep"), None), check_vma=False
    )
```

time: 466 us -> 126 us (0.27)
  the two profiles are of different devices: /device:TPU:1 before, /device:TPU:45 now
where the time goes in v1:
time: 126 us
  waiting for transfers between devices  43.8 us (35%)
  starting transfers between devices  31.3 us (25%)
  Pallas kernels  28.4 us (23%)
  local copies, waits for them, and re-layouts  11.3 us (9%)
  other arithmetic  7.81 us (6%)
  matrix products  3.11 us (2%)
    ppermute x15, waiting for transfers between devices, move(): return lax.ppermute(value, ('col', 'rep'), pairs)  39 us
    ppermute x15, starting transfers between devices, move(): return lax.ppermute(value, ('col', 'rep'), pairs)  18.6 us
    pallas_call x1, Pallas kernels, sum_tiles(): pl.pallas_call(sum_kernel, out_shape=(jax.ShapeDtypeStruct((half, WIDTH),...  16 us
    pallas_call x1, Pallas kernels, sort_blocks(): pl.pallas_call(sort_kernel, out_shape=(jax.ShapeDtypeStruct((DST_BLK + 1,...  12.4 us
    ppermute x1, starting transfers between devices, body(): aggregate = (kept + lax.ppermute(sent, 'rep', swap)) * own_norm[:, None]  7.65 us
    convert_element_type x1, other arithmetic, body(): own_tiles = counts.reshape(-1, BLOCK, BLOCK).astype(jnp.bfloat16)  6.51 us
    concatenate x1, local copies, waits for them, and re-layouts, gather_features(): jnp.concatenate([a[:cut], b[:cut], a[cut:cut + 8], b[cut:cut + 8]], axis=0)  6.18 us
    ppermute x1, starting transfers between devices, body(): other_ids = lax.ppermute(ids, 'rep', swap)  4.32 us
  transfers between devices with their start and end apart: 18, of which 10 were waited for; matrix products, arithmetic and copies ran while one was open for 7% of the time, Pallas kernels for 10%

profile of v1, /device:TPU:45, one launch (start us, length us, event | category | flops | bytes accessed | tf_op | source)
XLA Modules:
  0.0 126.0 jit_solution(11443710972755834753)
XLA Ops:
  0.0 6.5 %convert_bitcast_fusion.refs_8_ = bf16[128,128,128]{2,1,0:T(8,128)(2,1)} fusion(s32[1,1,128,128,128]{4,3,2,1,0:T(8,128)} %param.15), kind=kLoop, calls=%fused_computation | loop fusion | flops 2097152 | bytes 12582912 | tf_op jit(solution)/shard_map/convert_element_type | solution.py:226
  6.5 0.7 collective-permute-start.16
  7.2 0.1 dynamic-slice_bitcast_fusion
  7.3 0.1 collective-permute-start.1
  7.4 5.8 %collective-permute-start.2 = (bf16[144,256]{1,0:T(8,128)(2,1)S(1)}, bf16[144,256]{1,0:T(8,128)(2,1)S(1)}, u32[]{:S(2)}, u32[]{:S(2)}) collective-permute-start(bf16[144,256]{1,0:T(8,128)(2,1)S(1)} %pad_maximum_fusion.2), channel_id=1, source_target_pairs={{4,0},{5,1},{6,2},{7,3},{8,4},{9,5},{10,6},{11,7},{12,8},{13,9},{1... | collective-permute-start | bytes 221192 | tf_op jit(solution)/shard_map/ppermute | solution.py:45
  13.2 0.7 collective-permute-start.4
  14.0 0.0 collective-permute-done.1
  14.0 2.3 %collective-permute-done.2 = bf16[144,256]{1,0:T(8,128)(2,1)S(1)} collective-permute-done((bf16[144,256]{1,0:T(8,128)(2,1)S(1)}, bf16[144,256]{1,0:T(8,128)(2,1)S(1)}, u32[]{:S(2)}, u32[]{:S(2)}) %collective-permute-start.2) | collective-permute-done | bytes 73760 | tf_op jit(solution)/shard_map/ppermute | solution.py:45
  16.3 4.5 %collective-permute-start.3 = (bf16[288,256]{1,0:T(8,128)(2,1)S(1)}, bf16[288,256]{1,0:T(8,128)(2,1)S(1)}, u32[]{:S(2)}, u32[]{:S(2)}) collective-permute-start(bf16[288,256]{1,0:T(8,128)(2,1)S(1)} %pad_maximum_fusion.1), channel_id=1, source_target_pairs={{4,0},{5,1},{6,2},{7,3},{8,4},{9,5},{10,6},{11,7},{12,8},{13,9},{1... | collective-permute-start | bytes 442376 | tf_op jit(solution)/shard_map/ppermute | solution.py:45
  20.8 0.0 collective-permute-start.6
  20.8 1.9 %collective-permute-start.5 = (bf16[144,256]{1,0:T(8,128)(2,1)S(1)}, bf16[144,256]{1,0:T(8,128)(2,1)S(1)}, u32[]{:S(2)}, u32[]{:S(2)}) collective-permute-start(bf16[144,256]{1,0:T(8,128)(2,1)S(1)} %collective-permute-done.4), channel_id=1, source_target_pairs={{12,0},{13,1},{14,2},{15,3},{0,4},{1,5},{2,6},{3,7},{4,8},{5,9},{6... | collective-permute-start | bytes 221192 | tf_op jit(solution)/shard_map/ppermute | solution.py:45
  22.7 3.8 %collective-permute-done.6 = bf16[144,256]{1,0:T(8,128)(2,1)S(1)} collective-permute-done((bf16[144,256]{1,0:T(8,128)(2,1)S(1)}, bf16[144,256]{1,0:T(8,128)(2,1)S(1)}, u32[]{:S(2)}, u32[]{:S(2)}) %collective-permute-start.6) | collective-permute-done | bytes 73760 | tf_op jit(solution)/shard_map/ppermute | solution.py:45
  26.6 4.3 %collective-permute-done.5 = bf16[144,256]{1,0:T(8,128)(2,1)S(1)} collective-permute-done((bf16[144,256]{1,0:T(8,128)(2,1)S(1)}, bf16[144,256]{1,0:T(8,128)(2,1)S(1)}, u32[]{:S(2)}, u32[]{:S(2)}) %collective-permute-start.5) | collective-permute-done | bytes 73760 | tf_op jit(solution)/shard_map/ppermute | solution.py:45
  30.9 0.1 concatenate.36
  31.0 0.3 collective-permute-start.8
  31.3 1.8 %collective-permute-start.9 = (bf16[1040,256]{1,0:T(8,128)(2,1)S(1)}, bf16[1040,256]{1,0:T(8,128)(2,1)S(1)}, u32[]{:S(2)}, u32[]{:S(2)}) collective-permute-start(bf16[1040,256]{1,0:T(8,128)(2,1)S(1)} %concatenate.36), channel_id=1, source_target_pairs={{48,0},{193,1},{50,2},{195,3},{52,4},{197,5},{54,6},{199,7},{56,8}... | collective-permute-start | bytes 1597448 | tf_op jit(solution)/shard_map/ppermute | solution.py:45
  33.1 0.1 collective-permute-start.7
  33.2 7.9 %collective-permute-done.8 = bf16[1040,256]{1,0:T(8,128)(2,1)S(1)} collective-permute-done((bf16[1040,256]{1,0:T(8,128)(2,1)S(1)}, bf16[1040,256]{1,0:T(8,128)(2,1)S(1)}, u32[]{:S(2)}, u32[]{:S(2)}) %collective-permute-start.8) | collective-permute-done | bytes 532512 | tf_op jit(solution)/shard_map/ppermute | solution.py:45
  41.1 4.7 %collective-permute-done.9 = bf16[1040,256]{1,0:T(8,128)(2,1)S(1)} collective-permute-done((bf16[1040,256]{1,0:T(8,128)(2,1)S(1)}, bf16[1040,256]{1,0:T(8,128)(2,1)S(1)}, u32[]{:S(2)}, u32[]{:S(2)}) %collective-permute-start.9) | collective-permute-done | bytes 532512 | tf_op jit(solution)/shard_map/ppermute | solution.py:45
  45.9 0.1 pad_maximum_fusion.refs_1_
  46.0 0.0 copy-start.13
  46.0 0.0 copy-start.14
  46.0 1.4 %collective-permute-start.13 = (bf16[2064,256]{1,0:T(8,128)(2,1)S(1)}, bf16[2064,256]{1,0:T(8,128)(2,1)S(1)}, u32[]{:S(2)}, u32[]{:S(2)}) collective-permute-start(bf16[2064,256]{1,0:T(8,128)(2,1)S(1)} %pad_maximum_fusion.refs_1_), channel_id=1, source_target_pairs={{192,0},{49,1},{194,2},{51,3},{196,4},{53,5},{198,6},{55,7},{200,8... | collective-permute-start | bytes 3170312 | tf_op jit(solution)/shard_map/ppermute | solution.py:45
  47.4 0.0 collective-permute-done.7
  47.4 0.8 slice.132
  48.3 6.2 %concatenate.37.refs_0_ = bf16[2064,256]{1,0:T(8,128)(2,1)S(1)} concatenate(bf16[128,256]{1,0:T(8,128)(2,1)S(1)} %constant_dynamic-slice_fusion, bf16[128,256]{1,0:T(8,128)(2,1)S(1)} %slice.118, bf16[128,256]{1,0:T(8,128)(2,1)S(1)} %slice.119, bf16[128,256]{1,0:T(8,128)(2,1)} %copy-done.10, bf16[128,256]{1,0:T(8,128)(2,1)} %copy-done.9, bf16[128,256]{1,0:T(8,128)(2,1)} %copy-done.8, ...), dimensions={0} | concatenate | bytes 2113536 | tf_op jit(solution)/shard_map/concatenate | solution.py:203
  54.4 0.2 collective-permute-start.10
  54.7 4.3 %collective-permute-start = (s32[2,128]{1,0:T(2,128)S(1)}, s32[2,128]{1,0:T(2,128)S(1)}, u32[]{:S(2)}, u32[]{:S(2)}) collective-permute-start(s32[2,128]{1,0:T(2,128)S(1)} %pad_add_fusion), channel_id=1, source_target_pairs={{0,1},{1,0},{2,3},{3,2},{4,5},{5,4},{6,7},{7,6},{8,9},{9,8},{10,11... | collective-permute-start | bytes 3080 | tf_op jit(solution)/shard_map/ppermute | solution.py:221
  59.0 0.0 collective-permute-start.11
  59.0 0.8 collective-permute-done
  59.8 0.7 collective-permute-start.15
  60.5 1.0 collective-permute-start.14
  61.5 7.2 %collective-permute-done.10.refs_2_ = bf16[2064,256]{1,0:T(8,128)(2,1)} collective-permute-done((bf16[2064,256]{1,0:T(8,128)(2,1)S(1)}, bf16[2064,256]{1,0:T(8,128)(2,1)}, u32[]{:S(2)}, u32[]{:S(2)}) %collective-permute-start.10) | collective-permute-done | bytes 1056800 | tf_op jit(solution)/shard_map/ppermute | solution.py:45
  68.6 0.2 collective-permute-start.12
  68.8 0.6 pad_add_fusion.3.place
  69.4 0.6 pad_add_fusion.1
  70.0 12.4 %shard_map.82 = (s32[33]{0:T(128)}, s32[384]{0:T(512)}, s32[384]{0:T(512)}, s32[384]{0:T(512)}) custom-call(s32[4]{0:T(128)} %pad_add_fusion.3.place, s32[256]{0:T(256)} %get-tuple-element.35.src, s32[256]{0:T(256)} %get-tuple-element.36.dst), custom_call_target="tpu_custom_call" | custom-call | tf_op jit(solution)/shard_map/pallas_call | solution.py:108
  82.5 2.8 %collective-permute-done.14.refs_5_ = bf16[2064,256]{1,0:T(8,128)(2,1)} collective-permute-done((bf16[2064,256]{1,0:T(8,128)(2,1)S(1)}, bf16[2064,256]{1,0:T(8,128)(2,1)}, u32[]{:S(2)}, u32[]{:S(2)}) %collective-permute-start.14) | collective-permute-done | bytes 1056800 | tf_op jit(solution)/shard_map/ppermute | solution.py:45
  85.3 6.0 %collective-permute-done.12.refs_4_ = bf16[2064,256]{1,0:T(8,128)(2,1)} collective-permute-done((bf16[2064,256]{1,0:T(8,128)(2,1)}, bf16[2064,256]{1,0:T(8,128)(2,1)}, u32[]{:S(2)}, u32[]{:S(2)}) %collective-permute-start.12) | collective-permute-done | bytes 1056800 | tf_op jit(solution)/shard_map/ppermute | solution.py:45
  91.3 0.7 copy-done.2
  92.0 0.7 copy-done.3
  92.7 0.7 copy-done.4
  93.3 0.6 copy-done.5
  93.9 16.0 %shard_map.83 = (f32[2048,256]{1,0:T(8,128)}, f32[2048,256]{1,0:T(8,128)S(1)}) custom-call(s32[33]{0:T(128)S(1)} %copy-done.5, s32[384]{0:T(512)S(1)} %copy-done.2, s32[384]{0:T(512)S(1)} %copy-done.3, s32[384]{0:T(512)S(1)} %copy-done.4, bf16[2064,256]{1,0:T(8,128)(2,1)S(1)} %concatenate.37.refs_0_, bf16[2064,256]{1,0:T(8,128)(2,1)S(1)} %pad_maximum_fusion.refs_1_, ...), custom_call_target="tpu_custom_call" | custom-call | flops 2000000000 | bytes 20000000 | tf_op jit(solution)/shard_map/pallas_call | solution.py:165
  109.9 1.3 %copy-done.1 = f32[2048,256]{1,0:T(8,128)} copy-done((f32[2048,256]{1,0:T(8,128)}, f32[2048,256]{1,0:T(8,128)S(1)}, u32[]{:S(2)}) %copy-start.1) | copy-done | bytes 2097176
  111.3 7.7 %collective-permute-start.17 = (f32[2048,256]{1,0:T(8,128)}, f32[2048,256]{1,0:T(8,128)S(1)}, u32[]{:S(2)}, u32[]{:S(2)}) collective-permute-start(f32[2048,256]{1,0:T(8,128)} %get-tuple-element.28), channel_id=1, source_target_pairs={{0,1},{1,0},{2,3},{3,2},{4,5},{5,4},{6,7},{7,6},{8,9},{9,8},{10,11... | collective-permute-start | bytes 6291464 | tf_op jit(solution)/shard_map/ppermute | solution.py:232
  119.0 4.0 %collective-permute-done.17 = f32[2048,256]{1,0:T(8,128)S(1)} collective-permute-done((f32[2048,256]{1,0:T(8,128)}, f32[2048,256]{1,0:T(8,128)S(1)}, u32[]{:S(2)}, u32[]{:S(2)}) %collective-permute-start.17) | collective-permute-done | bytes 2097184 | tf_op jit(solution)/shard_map/ppermute | solution.py:232
  122.9 3.1 %fusion.1 = bf16[2048,256]{1,0:T(8,128)(2,1)} fusion(bf16[256,256]{1,0:T(8,128)(2,1)S(1)} %copy-done, f32[2048,256]{1,0:T(8,128)} %copy-done.1, f32[2048,256]{1,0:T(8,128)S(1)} %collective-permute-done.17, f32[256]{0:T(256)S(1)} %convert_element_type.17, f32[2048]{0:T(1024)S(1)} %dynamic_slice.11), kind=kOutput, calls=%fused_computation.3 | convolution fusion | flops 271581184 | bytes 5383168 | tf_op jit(solution)/shard_map/dot_general | solution.py:234
  (60 shorter events, 0.3 us)
Async XLA Ops:
  0.0 122.9 %copy-start = (bf16[256,256]{1,0:T(8,128)(2,1)S(1)}, bf16[256,256]{1,0:T(8,128)(2,1)}, u32[]{:S(2)}) copy-start(bf16[256,256]{1,0:T(8,128)(2,1)} %param.16) | copy-start | bytes 393220
  0.0 7.2 %copy-start.15 = (bf16[256]{0:T(256)(128)(2,1)S(1)}, bf16[256]{0:T(256)(128)(2,1)}, u32[]{:S(2)}) copy-start(bf16[256]{0:T(256)(128)(2,1)} %param.11) | copy-start | bytes 1540
  0.0 7.3 %copy-start.11 = (bf16[256,256]{1,0:T(8,128)(2,1)S(1)}, bf16[256,256]{1,0:T(8,128)(2,1)}, u32[]{:S(2)}) copy-start(bf16[256,256]{1,0:T(8,128)(2,1)} %param.10) | copy-start | bytes 393220
  6.5 84.8 %collective-permute-start.16 = (bf16[128,128,128]{2,1,0:T(8,128)(2,1)}, bf16[128,128,128]{2,1,0:T(8,128)(2,1)}, u32[]{:S(2)}, u32[]{:S(2)}) collective-permute-start(bf16[128,128,128]{2,1,0:T(8,128)(2,1)} %convert_bitcast_fusion.refs_8_), channel_id=1, source_target_pairs={{0,1},{1,0},{2,3},{3,2},{4,5},{5,4},{6,7},{7,6},{8,9},{9,8},{10,11... | collective-permute-start | bytes 12582920 | tf_op jit(solution)/shard_map/ppermute | solution.py:227
  7.3 6.7 %collective-permute-start.1 = (bf16[144,256]{1,0:T(8,128)(2,1)S(1)}, bf16[144,256]{1,0:T(8,128)(2,1)S(1)}, u32[]{:S(2)}, u32[]{:S(2)}) collective-permute-start(bf16[144,256]{1,0:T(8,128)(2,1)S(1)} %pad_maximum_fusion.2), channel_id=1, source_target_pairs={{2,0},{3,1},{4,2},{5,3},{6,4},{7,5},{8,6},{9,7},{10,8},{11,9},{12,... | collective-permute-start | bytes 221192 | tf_op jit(solution)/shard_map/ppermute | solution.py:45
  7.4 8.8 %collective-permute-start.2 = (bf16[144,256]{1,0:T(8,128)(2,1)S(1)}, bf16[144,256]{1,0:T(8,128)(2,1)S(1)}, u32[]{:S(2)}, u32[]{:S(2)}) collective-permute-start(bf16[144,256]{1,0:T(8,128)(2,1)S(1)} %pad_maximum_fusion.2), channel_id=1, source_target_pairs={{4,0},{5,1},{6,2},{7,3},{8,4},{9,5},{10,6},{11,7},{12,8},{13,9},{1... | collective-permute-start | bytes 221192 | tf_op jit(solution)/shard_map/ppermute | solution.py:45
  13.2 7.6 %collective-permute-start.4 = (bf16[144,256]{1,0:T(8,128)(2,1)S(1)}, bf16[144,256]{1,0:T(8,128)(2,1)S(1)}, u32[]{:S(2)}, u32[]{:S(2)}) collective-permute-start(bf16[144,256]{1,0:T(8,128)(2,1)S(1)} %pad_maximum_fusion.2), channel_id=1, source_target_pairs={{14,0},{15,1},{0,2},{1,3},{2,4},{3,5},{4,6},{5,7},{6,8},{7,9},{8,1... | collective-permute-start | bytes 221192 | tf_op jit(solution)/shard_map/ppermute | solution.py:45
  16.3 14.6 %collective-permute-start.3 = (bf16[288,256]{1,0:T(8,128)(2,1)S(1)}, bf16[288,256]{1,0:T(8,128)(2,1)S(1)}, u32[]{:S(2)}, u32[]{:S(2)}) collective-permute-start(bf16[288,256]{1,0:T(8,128)(2,1)S(1)} %pad_maximum_fusion.1), channel_id=1, source_target_pairs={{4,0},{5,1},{6,2},{7,3},{8,4},{9,5},{10,6},{11,7},{12,8},{13,9},{1... | collective-permute-start | bytes 442376 | tf_op jit(solution)/shard_map/ppermute | solution.py:45
  20.8 5.8 %collective-permute-start.6 = (bf16[144,256]{1,0:T(8,128)(2,1)S(1)}, bf16[144,256]{1,0:T(8,128)(2,1)S(1)}, u32[]{:S(2)}, u32[]{:S(2)}) collective-permute-start(bf16[144,256]{1,0:T(8,128)(2,1)S(1)} %pad_maximum_fusion.2), channel_id=1, source_target_pairs={{12,0},{13,1},{14,2},{15,3},{0,4},{1,5},{2,6},{3,7},{4,8},{5,9},{6... | collective-permute-start | bytes 221192 | tf_op jit(solution)/shard_map/ppermute | solution.py:45
  20.8 10.0 %collective-permute-start.5 = (bf16[144,256]{1,0:T(8,128)(2,1)S(1)}, bf16[144,256]{1,0:T(8,128)(2,1)S(1)}, u32[]{:S(2)}, u32[]{:S(2)}) collective-permute-start(bf16[144,256]{1,0:T(8,128)(2,1)S(1)} %collective-permute-done.4), channel_id=1, source_target_pairs={{12,0},{13,1},{14,2},{15,3},{0,4},{1,5},{2,6},{3,7},{4,8},{5,9},{6... | collective-permute-start | bytes 221192 | tf_op jit(solution)/shard_map/ppermute | solution.py:45
  22.7 23.2 %copy-start.6 = (bf16[128,256]{1,0:T(8,128)(2,1)}, bf16[128,256]{1,0:T(8,128)(2,1)S(1)}, u32[]{:S(2)}) copy-start(bf16[128,256]{1,0:T(8,128)(2,1)S(1)} %slice.124) | copy-start | bytes 196612
  26.5 19.3 %copy-start.7 = (bf16[128,256]{1,0:T(8,128)(2,1)}, bf16[128,256]{1,0:T(8,128)(2,1)S(1)}, u32[]{:S(2)}) copy-start(bf16[128,256]{1,0:T(8,128)(2,1)S(1)} %slice.123) | copy-start | bytes 196612
  30.8 15.1 %copy-start.8 = (bf16[128,256]{1,0:T(8,128)(2,1)}, bf16[128,256]{1,0:T(8,128)(2,1)S(1)}, u32[]{:S(2)}) copy-start(bf16[128,256]{1,0:T(8,128)(2,1)S(1)} %slice.122) | copy-start | bytes 196612
  30.9 15.0 %copy-start.9 = (bf16[128,256]{1,0:T(8,128)(2,1)}, bf16[128,256]{1,0:T(8,128)(2,1)S(1)}, u32[]{:S(2)}) copy-start(bf16[128,256]{1,0:T(8,128)(2,1)S(1)} %get-tuple-element.31) | copy-start | bytes 196612
  30.9 15.0 %copy-start.10 = (bf16[128,256]{1,0:T(8,128)(2,1)}, bf16[128,256]{1,0:T(8,128)(2,1)S(1)}, u32[]{:S(2)}) copy-start(bf16[128,256]{1,0:T(8,128)(2,1)S(1)} %get-tuple-element.32) | copy-start | bytes 196612
  31.0 10.1 %collective-permute-start.8 = (bf16[1040,256]{1,0:T(8,128)(2,1)S(1)}, bf16[1040,256]{1,0:T(8,128)(2,1)S(1)}, u32[]{:S(2)}, u32[]{:S(2)}) collective-permute-start(bf16[1040,256]{1,0:T(8,128)(2,1)S(1)} %concatenate.36), channel_id=1, source_target_pairs={{32,0},{129,1},{34,2},{131,3},{36,4},{133,5},{38,6},{135,7},{40,8}... | collective-permute-start | bytes 1597448 | tf_op jit(solution)/shard_map/ppermute | solution.py:45
  31.3 14.5 %collective-permute-start.9 = (bf16[1040,256]{1,0:T(8,128)(2,1)S(1)}, bf16[1040,256]{1,0:T(8,128)(2,1)S(1)}, u32[]{:S(2)}, u32[]{:S(2)}) collective-permute-start(bf16[1040,256]{1,0:T(8,128)(2,1)S(1)} %concatenate.36), channel_id=1, source_target_pairs={{48,0},{193,1},{50,2},{195,3},{52,4},{197,5},{54,6},{199,7},{56,8}... | collective-permute-start | bytes 1597448 | tf_op jit(solution)/shard_map/ppermute | solution.py:45
  33.1 14.3 %collective-permute-start.7 = (bf16[1040,256]{1,0:T(8,128)(2,1)S(1)}, bf16[1040,256]{1,0:T(8,128)(2,1)S(1)}, u32[]{:S(2)}, u32[]{:S(2)}) collective-permute-start(bf16[1040,256]{1,0:T(8,128)(2,1)S(1)} %concatenate.36), channel_id=1, source_target_pairs={{16,0},{65,1},{18,2},{67,3},{20,4},{69,5},{22,6},{71,7},{24,8},{73... | collective-permute-start | bytes 1597448 | tf_op jit(solution)/shard_map/ppermute | solution.py:45
  46.0 8.7 %copy-start.13 = (s32[1,1,128]{2,1,0:T(1,128)S(1)}, s32[1,1,128]{2,1,0:T(1,128)}, u32[]{:S(2)}) copy-start(s32[1,1,128]{2,1,0:T(1,128)} %param.14) | copy-start | bytes 1540
  46.0 8.7 %copy-start.14 = (s32[1,1,128]{2,1,0:T(1,128)S(1)}, s32[1,1,128]{2,1,0:T(1,128)}, u32[]{:S(2)}) copy-start(s32[1,1,128]{2,1,0:T(1,128)} %param.13) | copy-start | bytes 1540
  46.0 14.4 %collective-permute-start.13 = (bf16[2064,256]{1,0:T(8,128)(2,1)S(1)}, bf16[2064,256]{1,0:T(8,128)(2,1)S(1)}, u32[]{:S(2)}, u32[]{:S(2)}) collective-permute-start(bf16[2064,256]{1,0:T(8,128)(2,1)S(1)} %pad_maximum_fusion.refs_1_), channel_id=1, source_target_pairs={{192,0},{49,1},{194,2},{51,3},{196,4},{53,5},{198,6},{55,7},{200,8... | collective-permute-start | bytes 3170312 | tf_op jit(solution)/shard_map/ppermute | solution.py:45
  54.4 14.2 %collective-permute-start.10 = (bf16[2064,256]{1,0:T(8,128)(2,1)S(1)}, bf16[2064,256]{1,0:T(8,128)(2,1)}, u32[]{:S(2)}, u32[]{:S(2)}) collective-permute-start(bf16[2064,256]{1,0:T(8,128)(2,1)S(1)} %concatenate.37.refs_0_), channel_id=1, source_target_pairs={{64,0},{17,1},{66,2},{19,3},{68,4},{21,5},{70,6},{23,7},{72,8},{25... | collective-permute-start | bytes 3170312 | tf_op jit(solution)/shard_map/ppermute | solution.py:45
  54.7 5.1 %collective-permute-start = (s32[2,128]{1,0:T(2,128)S(1)}, s32[2,128]{1,0:T(2,128)S(1)}, u32[]{:S(2)}, u32[]{:S(2)}) collective-permute-start(s32[2,128]{1,0:T(2,128)S(1)} %pad_add_fusion), channel_id=1, source_target_pairs={{0,1},{1,0},{2,3},{3,2},{4,5},{5,4},{6,7},{7,6},{8,9},{9,8},{10,11... | collective-permute-start | bytes 3080 | tf_op jit(solution)/shard_map/ppermute | solution.py:221
  59.0 23.4 %collective-permute-start.11 = (bf16[2064,256]{1,0:T(8,128)(2,1)S(1)}, bf16[2064,256]{1,0:T(8,128)(2,1)}, u32[]{:S(2)}, u32[]{:S(2)}) collective-permute-start(bf16[2064,256]{1,0:T(8,128)(2,1)S(1)} %pad_maximum_fusion.refs_1_), channel_id=1, source_target_pairs={{64,0},{17,1},{66,2},{19,3},{68,4},{21,5},{70,6},{23,7},{72,8},{25... | collective-permute-start | bytes 3170312 | tf_op jit(solution)/shard_map/ppermute | solution.py:45
  59.8 22.6 %collective-permute-start.15 = (bf16[2064,256]{1,0:T(8,128)(2,1)S(1)}, bf16[2064,256]{1,0:T(8,128)(2,1)}, u32[]{:S(2)}, u32[]{:S(2)}) collective-permute-start(bf16[2064,256]{1,0:T(8,128)(2,1)S(1)} %concatenate.37.refs_0_), channel_id=1, source_target_pairs={{192,0},{49,1},{194,2},{51,3},{196,4},{53,5},{198,6},{55,7},{200,8... | collective-permute-start | bytes 3170312 | tf_op jit(solution)/shard_map/ppermute | solution.py:45
  60.5 24.8 %collective-permute-start.14 = (bf16[2064,256]{1,0:T(8,128)(2,1)S(1)}, bf16[2064,256]{1,0:T(8,128)(2,1)}, u32[]{:S(2)}, u32[]{:S(2)}) collective-permute-start(bf16[2064,256]{1,0:T(8,128)(2,1)S(1)} %collective-permute-done.13.refs_7_), channel_id=1, source_target_pairs={{192,0},{49,1},{194,2},{51,3},{196,4},{53,5},{198,6},{55,7},{200,8... | collective-permute-start | bytes 3170312 | tf_op jit(solution)/shard_map/ppermute | solution.py:45
  68.6 22.6 %collective-permute-start.12 = (bf16[2064,256]{1,0:T(8,128)(2,1)}, bf16[2064,256]{1,0:T(8,128)(2,1)}, u32[]{:S(2)}, u32[]{:S(2)}) collective-permute-start(bf16[2064,256]{1,0:T(8,128)(2,1)} %collective-permute-done.10.refs_2_), channel_id=1, source_target_pairs={{64,0},{17,1},{66,2},{19,3},{68,4},{21,5},{70,6},{23,7},{72,8},{25... | collective-permute-start | bytes 3170312 | tf_op jit(solution)/shard_map/ppermute | solution.py:45
  91.3 0.7 copy-start.2
  92.0 0.7 copy-start.3
  92.7 0.7 copy-start.4
  93.3 0.6 copy-start.5
  93.9 25.0 %copy-start.16 = (bf16[256]{0:T(256)(128)(2,1)S(1)}, bf16[256]{0:T(256)(128)(2,1)}, u32[]{:S(2)}) copy-start(bf16[256]{0:T(256)(128)(2,1)} %param.17) | copy-start | bytes 1540
  93.9 25.0 %copy-start.12 = (f32[4096]{0:T(1024)S(1)}, f32[4096]{0:T(1024)}, u32[]{:S(2)}) copy-start(f32[4096]{0:T(1024)} %param.12) | copy-start | bytes 49156
  109.9 1.4 %copy-start.1 = (f32[2048,256]{1,0:T(8,128)}, f32[2048,256]{1,0:T(8,128)S(1)}, u32[]{:S(2)}) copy-start(f32[2048,256]{1,0:T(8,128)S(1)} %get-tuple-element.27) | copy-start | bytes 6291460
  111.3 11.6 %collective-permute-start.17 = (f32[2048,256]{1,0:T(8,128)}, f32[2048,256]{1,0:T(8,128)S(1)}, u32[]{:S(2)}, u32[]{:S(2)}) collective-permute-start(f32[2048,256]{1,0:T(8,128)} %get-tuple-element.28), channel_id=1, source_target_pairs={{0,1},{1,0},{2,3},{3,2},{4,5},{5,4},{6,7},{7,6},{8,9},{9,8},{10,11... | collective-permute-start | bytes 6291464 | tf_op jit(solution)/shard_map/ppermute | solution.py:232

commit v2 on v0

v2 whole, which is shorter than its diff:
```python
import functools

import jax
import jax.numpy as jnp
from jax import lax
from jax.experimental import pallas as pl
from jax.experimental.pallas import tpu as pltpu
from jax.sharding import PartitionSpec as P

BLOCK = 128
DST_BLK = 32
WIDTH = 256
NX, NY, NZ = 4, 4, 8
SHARD = 2 * BLOCK + 16
LINE = 8 * BLOCK + 16
DEPTH = 64
UNROLL = 4
SEGMENTS = 8
SEG_SLOTS = 2 * BLOCK + UNROLL
PACKED = 2 * BLOCK + SEGMENTS * (UNROLL - 1)
DST_ROWS = DST_BLK * BLOCK
HALF = DST_ROWS // 2
MIB = 1024 * 1024


def device(x, y, z, r):
    return (((x % NX) * NY + (y % NY)) * NZ + (z % NZ)) * 2 + r


def from_z(step):
    return [
        (device(x, y, z - step if r else z + step % 4, r), device(x, y, z, r))
        for x in range(NX) for y in range(NY) for z in range(NZ) for r in range(2)
    ]


def from_second(step):
    return [
        (device(x, y + step, z, 0) if r == 0 else device(x + step, y, z, 1), device(x, y, z, r))
        for x in range(NX) for y in range(NY) for z in range(NZ) for r in range(2)
    ]


def from_third(step):
    return [
        (device(x + step, y, z, 0) if r == 0 else device(x, y + step, z, 1), device(x, y, z, r))
        for x in range(NX) for y in range(NY) for z in range(NZ) for r in range(2)
    ]


def move(value, pairs):
    return lax.ppermute(value, ("col", "rep"), pairs)


def line_kernel(a, b, c, d, own, slots, line):
    cut = 2 * BLOCK
    norms = []
    for k, shard in enumerate((a, b, c, d)):
        line[pl.ds(k * cut, cut), :] = shard[pl.ds(0, cut), :]
        norms.append(shard[pl.ds(cut, 16), :][:1].astype(jnp.float32))
    rows = jnp.concatenate(norms + [jnp.zeros((12, WIDTH), jnp.float32)], axis=0)
    line[pl.ds(8 * BLOCK, 16), :] = rows.astype(jnp.bfloat16)


def make_line(shards, own, slots):
    vmem = pl.BlockSpec(memory_space=pltpu.VMEM)
    return pl.pallas_call(
        line_kernel,
        out_shape=jax.ShapeDtypeStruct((LINE, WIDTH), jnp.bfloat16),
        in_specs=[vmem] * 4 + [pl.BlockSpec(memory_space=pltpu.HBM), pl.BlockSpec(memory_space=pl.ANY)],
        out_specs=vmem,
        compiler_params=pltpu.CompilerParams(vmem_limit_bytes=4 * MIB),
    )(*shards, own, slots)


def sort_kernel(codes, base, slots, count, listed):
    def clear(k, carry):
        count[k] = 0
        return carry

    lax.fori_loop(0, SEGMENTS, clear, 0)

    def put(i, carry):
        for u in range(4):
            code = codes[4 * i + u]
            segment = (code >> 26) & 15
            at = count[segment]
            listed[segment * SEG_SLOTS + at] = code
            count[segment] = at + (code >> 30)
        return carry

    lax.fori_loop(0, 64, put, 0)

    def squeeze(k, at):
        base[k] = at
        size = count[k]
        for u in range(UNROLL - 1):
            listed[k * SEG_SLOTS + size + u] = 4 << 21
        groups = (size + (UNROLL - 1)) >> 2

        def copy(g, carry):
            for u in range(UNROLL):
                slots[(at + g) * UNROLL + u] = listed[k * SEG_SLOTS + g * UNROLL + u]
            return carry

        lax.fori_loop(0, groups, copy, 0)
        return at + groups

    base[SEGMENTS] = lax.fori_loop(0, SEGMENTS, squeeze, 0)


def sort_codes(codes):
    smem = pl.BlockSpec(memory_space=pltpu.SMEM)
    return pl.pallas_call(
        sort_kernel,
        out_shape=(
            jax.ShapeDtypeStruct((SEGMENTS + 1,), jnp.int32),
            jax.ShapeDtypeStruct((PACKED,), jnp.int32),
        ),
        in_specs=[smem],
        out_specs=(smem, smem),
        scratch_shapes=[
            pltpu.SMEM((SEGMENTS,), jnp.int32),
            pltpu.SMEM((SEGMENTS * SEG_SLOTS,), jnp.int32),
        ],
        compiler_params=pltpu.CompilerParams(vmem_limit_bytes=2 * MIB),
    )(codes)


def pack_kernel(base, slots, own, other, packed, tile, in_sem):
    total = base[SEGMENTS]

    def fetch(g):
        slot = lax.rem(g, DEPTH // UNROLL)
        for u in range(UNROLL):
            e = slots[g * UNROLL + u] & 255

            @pl.when(e < BLOCK)
            def _():
                pltpu.make_async_copy(own.at[e], tile.at[slot, u], in_sem.at[slot, u]).start()

            @pl.when(e >= BLOCK)
            def _():
                pltpu.make_async_copy(other.at[e - BLOCK], tile.at[slot, u], in_sem.at[slot, u]).start()

    def begin(g, carry):
        fetch(g)
        return carry

    ahead = DEPTH // UNROLL - 1
    lax.fori_loop(0, jnp.minimum(total, ahead), begin, 0)

    def step(g, carry):
        slot = lax.rem(g, DEPTH // UNROLL)

        @pl.when(g + ahead < total)
        def _():
            fetch(g + ahead)

        for u in range(UNROLL):
            pltpu.make_async_copy(own.at[0], tile.at[slot, u], in_sem.at[slot, u]).wait()

        packed[g] = tile[slot].astype(jnp.float32).astype(jnp.bfloat16)
        return carry

    lax.fori_loop(0, total, step, 0)


def pack_tiles(lists, own, other):
    smem = pl.BlockSpec(memory_space=pltpu.SMEM)
    hbm = pl.BlockSpec(memory_space=pltpu.HBM)
    ring = (DEPTH // UNROLL, UNROLL, BLOCK, BLOCK)
    return pl.pallas_call(
        pack_kernel,
        out_shape=jax.ShapeDtypeStruct((PACKED // UNROLL, UNROLL, BLOCK, BLOCK), jnp.bfloat16),
        in_specs=[smem, smem, hbm, hbm],
        out_specs=pl.BlockSpec(memory_space=pltpu.VMEM),
        scratch_shapes=[pltpu.VMEM(ring, jnp.int32), pltpu.SemaphoreType.DMA(ring[:2])],
        compiler_params=pltpu.CompilerParams(vmem_limit_bytes=16 * MIB),
        cost_estimate=pl.CostEstimate(flops=10**6, bytes_accessed=20 * 10**6, transcendentals=0),
    )(*lists, own, other)


def halves_kernel(a, b, c, d, packed, low, high):
    for out, lines in ((low, (a, b)), (high, (c, d))):
        for k, line in enumerate(lines):
            out[pl.ds(k * LINE, LINE), :] = line[...]


def make_halves(lines, packed):
    vmem = pl.BlockSpec(memory_space=pltpu.VMEM)
    half = jax.ShapeDtypeStruct((2 * LINE, WIDTH), jnp.bfloat16)
    return pl.pallas_call(
        halves_kernel,
        out_shape=(half, half),
        in_specs=[vmem] * 4 + [pl.BlockSpec(memory_space=pl.ANY)],
        out_specs=(vmem, vmem),
        compiler_params=pltpu.CompilerParams(vmem_limit_bytes=8 * MIB),
    )(*lines, packed)


def sum_kernel(ids, before, *refs):
    base, slots, packed = refs[:3]
    pieces = refs[3 : 3 + len(ids)]
    refs = refs[3 + len(ids) :]
    if before:
        earlier, refs = refs[0], refs[1:]
    if len(refs) > 2:
        sent, kept, norm, total = refs
    else:
        total, norm = refs
    if before:
        total[...] = earlier[...]
    else:
        total[...] = jnp.zeros_like(total)
    for i, piece in enumerate(pieces):
        for line in range(2):
            for half in range(2):
                rows = piece[pl.ds(line * LINE + 8 * BLOCK, 16), pl.ds(half * BLOCK, BLOCK)]
                norm[pl.ds(32 * i + 16 * half + 8 * line, 8), :] = rows.astype(jnp.float32)[:8]
    for i, (k, piece) in enumerate(zip(ids, pieces)):
        first, last = base[k], base[k + 1]

        def add(g, groups, i=i, piece=piece):
            found = []
            for u in range(UNROLL * groups):
                code = slots[UNROLL * g + u]
                scale = norm[pl.ds(32 * i + ((code >> 21) & 31), 1), :]
                row = pl.multiple_of(((code >> 13) & 255) * 16, 16)
                found.append((
                    pl.multiple_of(((code >> 8) & 31) * BLOCK, BLOCK),
                    jnp.dot(
                        packed[g + u // UNROLL, u % UNROLL] * scale.astype(jnp.bfloat16),
                        piece[pl.ds(row, BLOCK), :], preferred_element_type=jnp.float32,
                    ),
                ))
            for at, product in found:
                total[pl.ds(at, BLOCK), :] += product

        def pair(j, carry, first=first, add=add):
            add(first + 2 * j, 2)
            return carry

        lax.fori_loop(0, (last - first) >> 1, pair, 0)

        @pl.when(((last - first) & 1) == 1)
        def _(last=last, add=add):
            add(last - 1, 1)

    if len(refs) > 2:
        sent[...] = total[pl.ds(0, HALF), :].astype(sent.dtype)
        kept[...] = total[pl.ds(HALF, HALF), :]


def sum_tiles(lists, pieces, earlier=None, last=False):
    smem = pl.BlockSpec(memory_space=pltpu.SMEM)
    vmem = pl.BlockSpec(memory_space=pltpu.VMEM)
    ids = tuple(pieces)
    before = [] if earlier is None else [earlier]
    whole = jax.ShapeDtypeStruct((DST_ROWS, WIDTH), jnp.float32)
    ends = tuple(jax.ShapeDtypeStruct((HALF, WIDTH), t) for t in (jnp.bfloat16, jnp.float32))
    norm = pltpu.VMEM((32 * len(ids), BLOCK), jnp.float32)
    return pl.pallas_call(
        functools.partial(sum_kernel, ids, bool(before)),
        out_shape=ends if last else whole,
        in_specs=[smem] * 2 + [vmem] * (1 + len(ids) + len(before)),
        out_specs=(vmem, vmem) if last else vmem,
        scratch_shapes=[norm] + ([pltpu.VMEM(whole.shape, whole.dtype)] if last else []),
        compiler_params=pltpu.CompilerParams(vmem_limit_bytes=8 * MIB),
        cost_estimate=pl.CostEstimate(flops=4 * 10**8, bytes_accessed=8 * 10**6, transcendentals=0),
    )(*lists, *pieces.values(), *before)


def finish_kernel(kept, received, scale, weight, bias, out, buffer, sems):
    step = HALF // 8
    copies = []
    for i in range(8):
        rows = pl.ds(i * step, step)
        factor = jnp.concatenate([scale[rows, :]] * 2, axis=1)
        aggregate = (kept[rows, :] + received[rows, :].astype(jnp.float32)) * factor
        result = jnp.dot(
            aggregate.astype(jnp.bfloat16), weight[...], preferred_element_type=jnp.float32
        ) + bias[...]
        buffer[rows, :] = jnp.maximum(result, 0.0).astype(jnp.bfloat16)
        copies.append(pltpu.make_async_copy(buffer.at[rows], out.at[rows], sems.at[i]))
        copies[-1].start()
    for copy in copies:
        copy.wait()


def finish(kept, received, scale, weight, bias):
    vmem = pl.BlockSpec(memory_space=pltpu.VMEM)
    return pl.pallas_call(
        finish_kernel,
        out_shape=jax.ShapeDtypeStruct((HALF, WIDTH), jnp.bfloat16),
        in_specs=[vmem] * 5,
        out_specs=pl.BlockSpec(memory_space=pl.ANY),
        scratch_shapes=[pltpu.VMEM((HALF, WIDTH), jnp.bfloat16), pltpu.SemaphoreType.DMA((8,))],
        compiler_params=pltpu.CompilerParams(vmem_limit_bytes=12 * MIB),
        cost_estimate=pl.CostEstimate(flops=3 * 10**8, bytes_accessed=6 * 10**6, transcendentals=0),
    )(kept, received, scale, weight, bias)


def encode(src, dst, place):
    z, second, third, rep = place
    entry = jnp.arange(2 * BLOCK, dtype=jnp.int32)
    p = src >> 1
    dz = ((p & 7) - z) & 7
    px, py = p >> 5, (p >> 3) & 3
    pa = jnp.where(rep == 0, py, px)
    pb = jnp.where(rep == 0, px, py)
    shard = jnp.where(rep == 0, dz, 8 - dz) & 3
    da, db = (pa - second) & 3, (pb - third) & 3
    line = da & 1
    d = (dst + 16 * (1 - rep)) & 31
    segment = db * 2 + (da >> 1)
    row16 = line * (LINE // 16) + shard * 16 + (src & 1) * 8
    scale = (src & 1) * 16 + line * 8 + shard
    valid = jnp.where((dz >> 2) == rep, 1, 0)
    return entry | (d << 8) | (row16 << 13) | (scale << 21) | (segment << 26) | (valid << 30)


def gather_shards(features, src_norm):
    norm_rows = jnp.zeros((16, WIDTH), jnp.bfloat16).at[0].set(src_norm)
    shard = jnp.concatenate([features, norm_rows], axis=0)
    return [move(shard, from_z(step)) for step in (4, 1, 2, 3)]


def body(features, src_norm, dst_norm, src_block, dst_block, counts, weight, out_bias):
    rep = lax.axis_index("rep")
    col = lax.axis_index("col")
    x, y, z = col // (NY * NZ), (col // NZ) % NY, col % NZ
    swap = [(0, 1), (1, 0)]
    own = counts.reshape(-1, BLOCK, BLOCK)
    other = lax.ppermute(own, "rep", swap)
    ids = jnp.concatenate([src_block.reshape(1, -1), dst_block.reshape(1, -1)], axis=0)
    all_ids = lax.all_gather(ids, "rep")
    both = jnp.concatenate([ids, jnp.where(rep == 0, all_ids[1], all_ids[0])], axis=1)
    place = (z, jnp.where(rep == 0, y, x), jnp.where(rep == 0, x, y), rep)
    base, slots = sort_codes(encode(both[0], both[1], place))
    line_0 = make_line(gather_shards(features, src_norm), other, slots)
    lines = [line_0] + [move(line_0, from_second(step)) for step in (1, 2, 3)]
    packed = pack_tiles((base, slots), own, other)
    lists = (base, slots, packed)
    half_0, half_1 = make_halves(lines, packed)
    up_0 = move(half_0, from_third(1))
    down_1 = move(half_1, from_third(-1))
    up_1 = move(half_1, from_third(1))
    down_0 = move(half_0, from_third(-1))
    across_0 = move(up_0, from_third(1))
    across_1 = move(down_1, from_third(-1))
    total = sum_tiles(lists, {0: half_0, 1: half_1})
    total = sum_tiles(lists, {2: up_0, 7: down_1, 3: up_1, 6: down_0}, total)
    sent, kept = sum_tiles(lists, {4: across_0, 5: across_1}, total, True)
    received = lax.ppermute(sent, "rep", swap)
    own_norm = lax.dynamic_slice_in_dim(dst_norm, rep * HALF, HALF, 0)
    scale = jnp.broadcast_to(own_norm[:, None], (HALF, BLOCK))
    return finish(kept, received, scale, weight, out_bias.astype(jnp.float32).reshape(1, -1))


def solution(mesh):
    placed = (
        P("col", None),
        P("col"),
        P("col"),
        P("col", "rep", None),
        P("col", "rep", None),
        P("col", "rep", None, None, None),
        P(),
        P(),
    )
    return jax.shard_map(
        body, mesh=mesh, in_specs=placed, out_specs=P(("col", "rep"), None), check_vma=False
    )
```

time: 466 us -> 88.7 us (0.19)
  blocking collectives: 294 us -> 1.77 us
  waiting for transfers between devices: 87.1 us -> 34.5 us
  other arithmetic: 38.1 us -> 2.33 us
  Pallas kernels: 0 us -> 24.9 us
  starting transfers between devices: 0.04 us -> 23.4 us
  matrix products: 16.9 us -> 0 us
  local copies, waits for them, and re-layouts: 16.2 us -> 1.01 us
  between operations: 13.5 us -> 0.31 us
    all_gather x1, blocking collectives: 294 us -> 1.77 us  [body(): all_ids = lax.all_gather(ids, 'rep')]
    psum x1 -> x0, waiting for transfers between devices: 86.3 us -> none  [body(): combined = lax.psum(partial_rows, 'rep')]
    scatter-add x1 -> x0, other arithmetic: 37 us -> none  [body(): summed = jax.ops.segment_sum(products, dst_ids, num_segments=DST_BLK)]
    ppermute x0 -> x15, waiting for transfers between devices: none -> 34.5 us  [the longest x13 31.9 us: move(): return lax.ppermute(value, ('col', 'rep'), pairs)]
    pallas_call x0 -> x8, Pallas kernels: none -> 24.9 us  [the longest x1 10.6 us: pack_tiles(): pl.pallas_call(pack_kernel, out_shape=jax.ShapeDtypeStruct((PACKED // UNR...]
    ppermute x0 -> x15, starting transfers between devices: none -> 23.4 us  [the longest x13 19.9 us: move(): return lax.ppermute(value, ('col', 'rep'), pairs)]
    dot_general x2 -> x0, matrix products: 16.9 us -> none  [the longest x1 13.8 us: body(): jnp.einsum('bij,bjf->bif', tile_vals, gathered, preferred_element_type=jn...]
    gather x2 -> x0, local copies, waits for them, and re-layouts: 13 us -> none  [the longest x1 12.3 us: body(): gathered = all_feat.reshape(-1, BLOCK, width)[src_ids]]
  transfers between devices with their start and end apart: 2 -> 15, of which waited for: 1 -> 8; matrix products, arithmetic and copies ran while one was open for 1% -> 3% of each run, Pallas kernels for 0% -> 22%
where the time goes in v2:
time: 88.7 us; the launch traced here: 88.2 us
  waiting for transfers between devices  34.5 us (39%)
  Pallas kernels  24.9 us (28%)
  starting transfers between devices  23.4 us (26%)
  other arithmetic  2.33 us (3%)
  blocking collectives  1.77 us (2%)
  local copies, waits for them, and re-layouts  1.01 us (1%)
    ppermute x13, waiting for transfers between devices, move(): return lax.ppermute(value, ('col', 'rep'), pairs)  31.9 us
    ppermute x13, starting transfers between devices, move(): return lax.ppermute(value, ('col', 'rep'), pairs)  19.9 us
    pallas_call x1, Pallas kernels, pack_tiles(): pl.pallas_call(pack_kernel, out_shape=jax.ShapeDtypeStruct((PACKED // UNR...  10.6 us
    pallas_call x3, Pallas kernels, sum_tiles(): pl.pallas_call(functools.partial(sum_kernel, ids, bool(before)), out_shap...  9.72 us
    ppermute x1, starting transfers between devices, body(): other = lax.ppermute(own, 'rep', swap)  3.24 us
    pallas_call x1, Pallas kernels, sort_codes(): pl.pallas_call(sort_kernel, out_shape=(jax.ShapeDtypeStruct((SEGMENTS + 1...  3.14 us
    ppermute x1, waiting for transfers between devices, body(): received = lax.ppermute(sent, 'rep', swap)  2.54 us
  transfers between devices with their start and end apart: 15, of which 8 were waited for; matrix products, arithmetic and copies ran while one was open for 3% of the time, Pallas kernels for 22%

profile of v2, /device:TPU:1, one launch (start us, length us, event | category | flops | bytes accessed | tf_op | source)
XLA Modules:
  0.0 88.2 jit_solution(7027875764680369427)
XLA Ops:
  0.0 3.2 %collective-permute-start = (s32[128,128,128]{2,1,0:T(8,128)}, s32[128,128,128]{2,1,0:T(8,128)}, u32[]{:S(2)}, u32[]{:S(2)}) collective-permute-start(s32[128,128,128]{2,1,0:T(8,128)} %bitcast.14), channel_id=1, source_target_pairs={{0,1},{1,0},{2,3},{3,2},{4,5},{5,4},{6,7},{7,6},{8,9},{9,8},{10,11... | collective-permute-start | bytes 25165832 | tf_op jit(solution)/shard_map/ppermute | solution.py:335
  3.2 0.7 reshape.78
  3.9 0.9 %fusion.1 = bf16[272,256]{1,0:T(8,128)(2,1)S(1)} fusion(bf16[1,256]{1,0:T(2,128)(2,1)S(1)} %reshape.78, bf16[256,256]{1,0:T(8,128)(2,1)} %param.10), kind=kLoop, calls=%fused_computation.2 | loop fusion | flops 417792 | bytes 270848 | tf_op jit(solution)/shard_map/concatenate | solution.py:325
  4.8 7.1 %collective-permute-start.1 = (bf16[272,256]{1,0:T(8,128)(2,1)S(1)}, bf16[272,256]{1,0:T(8,128)(2,1)S(1)}, u32[]{:S(2)}, u32[]{:S(2)}) collective-permute-start(bf16[272,256]{1,0:T(8,128)(2,1)S(1)} %fusion.1), channel_id=1, source_target_pairs={{0,0},{9,1},{2,2},{11,3},{4,4},{13,5},{6,6},{15,7},{8,8},{1,9},{10... | collective-permute-start | bytes 417800 | tf_op jit(solution)/shard_map/ppermute | solution.py:52
  11.9 0.8 collective-permute-start.2
  12.7 1.2 %collective-permute-start.3 = (bf16[272,256]{1,0:T(8,128)(2,1)S(1)}, bf16[272,256]{1,0:T(8,128)(2,1)S(1)}, u32[]{:S(2)}, u32[]{:S(2)}) collective-permute-start(bf16[272,256]{1,0:T(8,128)(2,1)S(1)} %fusion.1), channel_id=1, source_target_pairs={{4,0},{13,1},{6,2},{15,3},{8,4},{1,5},{10,6},{3,7},{12,8},{5,9},{1... | collective-permute-start | bytes 417800 | tf_op jit(solution)/shard_map/ppermute | solution.py:52
  13.9 0.0 collective-permute-start.4
  13.9 0.7 add_bitcast_fusion
  14.6 1.8 %all-gather.1 = s32[2,2,128]{2,1,0:T(2,128)S(1)} all-gather(s32[1,2,128]{2,1,0:T(2,128)S(1)} %add_bitcast_fusion), channel_id=2, replica_groups=mesh['col'=128,'rep'=2] {'rep'}, dimensions={0}, use_global_device_ids=true | all-gather | bytes 3072 | tf_op jit(solution)/shard_map/all_gather | solution.py:337
  16.4 0.7 pad_add_fusion
  17.1 3.1 %shard_map.82 = (s32[9]{0:T(128)S(1)}, s32[280]{0:T(512)S(1)}) custom-call(s32[256]{0:T(256)S(1)} %fusion.8.codes), custom_call_target="tpu_custom_call" | custom-call | tf_op jit(solution)/shard_map/pallas_call | solution.py:114
  20.3 0.0 collective-permute-done.1.a
  20.3 0.0 collective-permute-done.2.b
  20.3 0.0 collective-permute-done.3.c
  20.3 3.2 %collective-permute-done.4.d = bf16[272,256]{1,0:T(8,128)(2,1)S(1)} collective-permute-done((bf16[272,256]{1,0:T(8,128)(2,1)S(1)}, bf16[272,256]{1,0:T(8,128)(2,1)S(1)}, u32[]{:S(2)}, u32[]{:S(2)}) %collective-permute-start.4) | collective-permute-done | bytes 139296 | tf_op jit(solution)/shard_map/ppermute | solution.py:52
  23.5 0.0 collective-permute-done.other.own
  23.6 2.5 %collective-permute-start.5 = (bf16[1040,256]{1,0:T(8,128)(2,1)S(1)}, bf16[1040,256]{1,0:T(8,128)(2,1)S(1)}, u32[]{:S(2)}, u32[]{:S(2)}) collective-permute-start(bf16[1040,256]{1,0:T(8,128)(2,1)S(1)} %shard_map.84.a), channel_id=1, source_target_pairs={{16,0},{65,1},{18,2},{67,3},{20,4},{69,5},{22,6},{71,7},{24,8},{73... | collective-permute-start | bytes 1597448 | tf_op jit(solution)/shard_map/ppermute | solution.py:52
  26.1 0.5 collective-permute-start.6
  26.6 0.6 collective-permute-start.7
  27.2 0.0 copy-done
  27.2 10.6 %shard_map.83.packed.refs_2_ = bf16[70,4,128,128]{3,2,1,0:T(8,128)(2,1)S(1)} custom-call(s32[9]{0:T(128)S(1)} %get-tuple-element.23.base.refs_0_, s32[280]{0:T(512)S(1)} %get-tuple-element.24.slots.refs_1_, s32[128,128,128]{2,1,0:T(8,128)S(1)} %bitcast.15, s32[128,128,128]{2,1,0:T(8,128)} %collective-permute-done.other.own), custom_call_target="tpu_custom_call" | custom-call | flops 1000000 | bytes 20000000 | tf_op jit(solution)/shard_map/pallas_call | solution.py:173
  37.8 0.2 collective-permute-done.5.b
  38.0 0.0 collective-permute-done.6.c
  38.0 3.4 %collective-permute-done.7.d = bf16[1040,256]{1,0:T(8,128)(2,1)S(1)} collective-permute-done((bf16[1040,256]{1,0:T(8,128)(2,1)S(1)}, bf16[1040,256]{1,0:T(8,128)(2,1)S(1)}, u32[]{:S(2)}, u32[]{:S(2)}) %collective-permute-start.7) | collective-permute-done | bytes 532512 | tf_op jit(solution)/shard_map/ppermute | solution.py:52
  41.4 0.1 shard_map.85
  41.6 1.4 %collective-permute-start.10 = (bf16[2080,256]{1,0:T(8,128)(2,1)S(1)}, bf16[2080,256]{1,0:T(8,128)(2,1)S(1)}, u32[]{:S(2)}, u32[]{:S(2)}) collective-permute-start(bf16[2080,256]{1,0:T(8,128)(2,1)S(1)} %get-tuple-element.26.refs_4_), channel_id=1, source_target_pairs={{192,0},{49,1},{194,2},{51,3},{196,4},{53,5},{198,6},{55,7},{200,8... | collective-permute-start | bytes 3194888 | tf_op jit(solution)/shard_map/ppermute | solution.py:52
  42.9 1.5 %collective-permute-start.8 = (bf16[2080,256]{1,0:T(8,128)(2,1)S(1)}, bf16[2080,256]{1,0:T(8,128)(2,1)S(1)}, u32[]{:S(2)}, u32[]{:S(2)}) collective-permute-start(bf16[2080,256]{1,0:T(8,128)(2,1)S(1)} %get-tuple-element.25.refs_3_), channel_id=1, source_target_pairs={{64,0},{17,1},{66,2},{19,3},{68,4},{21,5},{70,6},{23,7},{72,8},{25... | collective-permute-start | bytes 3194888 | tf_op jit(solution)/shard_map/ppermute | solution.py:52
  44.5 1.4 %collective-permute-start.12 = (bf16[2080,256]{1,0:T(8,128)(2,1)S(1)}, bf16[2080,256]{1,0:T(8,128)(2,1)S(1)}, u32[]{:S(2)}, u32[]{:S(2)}) collective-permute-start(bf16[2080,256]{1,0:T(8,128)(2,1)S(1)} %get-tuple-element.26.refs_4_), channel_id=1, source_target_pairs={{64,0},{17,1},{66,2},{19,3},{68,4},{21,5},{70,6},{23,7},{72,8},{25... | collective-permute-start | bytes 3194888 | tf_op jit(solution)/shard_map/ppermute | solution.py:52
  45.8 0.1 collective-permute-start.13
  45.9 11.1 %collective-permute-done.10.refs_4_ = bf16[2080,256]{1,0:T(8,128)(2,1)S(1)} collective-permute-done((bf16[2080,256]{1,0:T(8,128)(2,1)S(1)}, bf16[2080,256]{1,0:T(8,128)(2,1)S(1)}, u32[]{:S(2)}, u32[]{:S(2)}) %collective-permute-start.10) | collective-permute-done | bytes 1064992 | tf_op jit(solution)/shard_map/ppermute | solution.py:52
  57.0 0.0 collective-permute-start.11
  57.1 0.0 collective-permute-done.8.refs_3_
  57.1 2.7 %collective-permute-start.9 = (bf16[2080,256]{1,0:T(8,128)(2,1)S(1)}, bf16[2080,256]{1,0:T(8,128)(2,1)S(1)}, u32[]{:S(2)}, u32[]{:S(2)}) collective-permute-start(bf16[2080,256]{1,0:T(8,128)(2,1)S(1)} %collective-permute-done.8.refs_3_), channel_id=1, source_target_pairs={{64,0},{17,1},{66,2},{19,3},{68,4},{21,5},{70,6},{23,7},{72,8},{25... | collective-permute-start | bytes 3194888 | tf_op jit(solution)/shard_map/ppermute | solution.py:52
  59.8 2.0 %shard_map.86.refs_7_ = f32[4096,256]{1,0:T(8,128)S(1)} custom-call(s32[9]{0:T(128)S(1)} %get-tuple-element.23.base.refs_0_, s32[280]{0:T(512)S(1)} %get-tuple-element.24.slots.refs_1_, bf16[70,4,128,128]{3,2,1,0:T(8,128)(2,1)S(1)} %shard_map.83.packed.refs_2_, bf16[2080,256]{1,0:T(8,128)(2,1)S(1)} %get-tuple-element.25.refs_3_, ...), custom_call_target="tpu_custom_call" | custom-call | flops 400000000 | bytes 8000000 | tf_op jit(solution)/shard_map/pallas_call | solution.py:263
  61.8 6.7 %collective-permute-done.12.refs_5_ = bf16[2080,256]{1,0:T(8,128)(2,1)S(1)} collective-permute-done((bf16[2080,256]{1,0:T(8,128)(2,1)S(1)}, bf16[2080,256]{1,0:T(8,128)(2,1)S(1)}, u32[]{:S(2)}, u32[]{:S(2)}) %collective-permute-start.12) | collective-permute-done | bytes 1064992 | tf_op jit(solution)/shard_map/ppermute | solution.py:52
  68.5 0.0 collective-permute-done.13.refs_6_
  68.5 4.1 %shard_map.87.refs_5_ = f32[4096,256]{1,0:T(8,128)S(1)} custom-call(s32[9]{0:T(128)S(1)} %get-tuple-element.23.base.refs_0_, s32[280]{0:T(512)S(1)} %get-tuple-element.24.slots.refs_1_, bf16[70,4,128,128]{3,2,1,0:T(8,128)(2,1)S(1)} %shard_map.83.packed.refs_2_, bf16[2080,256]{1,0:T(8,128)(2,1)S(1)} %collective-permute-done.8.refs_3_, ...), custom_call_target="tpu_custom_call" | custom-call | flops 400000000 | bytes 8000000 | tf_op jit(solution)/shard_map/pallas_call | solution.py:263
  72.5 0.0 copy-start.3
  72.6 0.0 copy-start.2
  72.6 7.2 %collective-permute-done.11.refs_4_ = bf16[2080,256]{1,0:T(8,128)(2,1)S(1)} collective-permute-done((bf16[2080,256]{1,0:T(8,128)(2,1)S(1)}, bf16[2080,256]{1,0:T(8,128)(2,1)S(1)}, u32[]{:S(2)}, u32[]{:S(2)}) %collective-permute-start.11) | collective-permute-done | bytes 1064992 | tf_op jit(solution)/shard_map/ppermute | solution.py:52
  79.7 0.1 collective-permute-done.9.refs_3_
  79.9 3.7 %shard_map.88 = (bf16[2048,256]{1,0:T(8,128)(2,1)}, f32[2048,256]{1,0:T(8,128)S(1)}) custom-call(s32[9]{0:T(128)S(1)} %get-tuple-element.23.base.refs_0_, s32[280]{0:T(512)S(1)} %get-tuple-element.24.slots.refs_1_, bf16[70,4,128,128]{3,2,1,0:T(8,128)(2,1)S(1)} %shard_map.83.packed.refs_2_, bf16[2080,256]{1,0:T(8,128)(2,1)S(1)} %collective-permute-done.9.refs_3_, ...), custom_call_target="tpu_custom_call" | custom-call | flops 400000000 | bytes 8000000 | tf_op jit(solution)/shard_map/pallas_call | solution.py:263
  83.5 0.3 collective-permute-start.14
  83.8 0.0 copy-done.3
  83.9 0.0 copy-done.2
  83.9 2.5 %collective-permute-done.14.received = bf16[2048,256]{1,0:T(8,128)(2,1)S(1)} collective-permute-done((bf16[2048,256]{1,0:T(8,128)(2,1)}, bf16[2048,256]{1,0:T(8,128)(2,1)S(1)}, u32[]{:S(2)}, u32[]{:S(2)}) %collective-permute-start.14) | collective-permute-done | bytes 1048608 | tf_op jit(solution)/shard_map/ppermute | solution.py:355
  86.4 0.3 broadcast_in_dim.14.scale
  86.8 1.3 %shard_map.89 = bf16[2048,256]{1,0:T(8,128)(2,1)} custom-call(f32[2048,256]{1,0:T(8,128)S(1)} %get-tuple-element.27.kept, bf16[2048,256]{1,0:T(8,128)(2,1)S(1)} %collective-permute-done.14.received, f32[2048,128]{1,0:T(8,128)S(1)} %broadcast_in_dim.14.scale, bf16[256,256]{1,0:T(8,128)(2,1)S(1)} %copy-done.1, f32[1,256]{1,0:T(1,128)S(1)} %bitcast.16), custom_call_target="tpu_custom_call" | custom-call | flops 300000000 | bytes 6000000 | tf_op jit(solution)/shard_map/pallas_call | solution.py:293
  (10 shorter events, 0.1 us)
Async XLA Ops:
  0.0 23.5 %collective-permute-start = (s32[128,128,128]{2,1,0:T(8,128)}, s32[128,128,128]{2,1,0:T(8,128)}, u32[]{:S(2)}, u32[]{:S(2)}) collective-permute-start(s32[128,128,128]{2,1,0:T(8,128)} %bitcast.14), channel_id=1, source_target_pairs={{0,1},{1,0},{2,3},{3,2},{4,5},{5,4},{6,7},{7,6},{8,9},{9,8},{10,11... | collective-permute-start | bytes 25165832 | tf_op jit(solution)/shard_map/ppermute | solution.py:335
  4.8 15.5 %collective-permute-start.1 = (bf16[272,256]{1,0:T(8,128)(2,1)S(1)}, bf16[272,256]{1,0:T(8,128)(2,1)S(1)}, u32[]{:S(2)}, u32[]{:S(2)}) collective-permute-start(bf16[272,256]{1,0:T(8,128)(2,1)S(1)} %fusion.1), channel_id=1, source_target_pairs={{0,0},{9,1},{2,2},{11,3},{4,4},{13,5},{6,6},{15,7},{8,8},{1,9},{10... | collective-permute-start | bytes 417800 | tf_op jit(solution)/shard_map/ppermute | solution.py:52
  11.9 8.4 %collective-permute-start.2 = (bf16[272,256]{1,0:T(8,128)(2,1)S(1)}, bf16[272,256]{1,0:T(8,128)(2,1)S(1)}, u32[]{:S(2)}, u32[]{:S(2)}) collective-permute-start(bf16[272,256]{1,0:T(8,128)(2,1)S(1)} %fusion.1), channel_id=1, source_target_pairs={{2,0},{15,1},{4,2},{1,3},{6,4},{3,5},{8,6},{5,7},{10,8},{7,9},{12,... | collective-permute-start | bytes 417800 | tf_op jit(solution)/shard_map/ppermute | solution.py:52
  12.7 7.6 %collective-permute-start.3 = (bf16[272,256]{1,0:T(8,128)(2,1)S(1)}, bf16[272,256]{1,0:T(8,128)(2,1)S(1)}, u32[]{:S(2)}, u32[]{:S(2)}) collective-permute-start(bf16[272,256]{1,0:T(8,128)(2,1)S(1)} %fusion.1), channel_id=1, source_target_pairs={{4,0},{13,1},{6,2},{15,3},{8,4},{1,5},{10,6},{3,7},{12,8},{5,9},{1... | collective-permute-start | bytes 417800 | tf_op jit(solution)/shard_map/ppermute | solution.py:52
  13.9 9.6 %collective-permute-start.4 = (bf16[272,256]{1,0:T(8,128)(2,1)S(1)}, bf16[272,256]{1,0:T(8,128)(2,1)S(1)}, u32[]{:S(2)}, u32[]{:S(2)}) collective-permute-start(bf16[272,256]{1,0:T(8,128)(2,1)S(1)} %fusion.1), channel_id=1, source_target_pairs={{6,0},{11,1},{8,2},{13,3},{10,4},{15,5},{12,6},{1,7},{14,8},{3,9},... | collective-permute-start | bytes 417800 | tf_op jit(solution)/shard_map/ppermute | solution.py:52
  23.5 3.7 %copy-start = (s32[1,1,128,128,128]{4,3,2,1,0:T(8,128)S(1)}, s32[1,1,128,128,128]{4,3,2,1,0:T(8,128)}, u32[]{:S(2)}) copy-start(s32[1,1,128,128,128]{4,3,2,1,0:T(8,128)} %param.15) | copy-start | bytes 25165828
  23.6 14.4 %collective-permute-start.5 = (bf16[1040,256]{1,0:T(8,128)(2,1)S(1)}, bf16[1040,256]{1,0:T(8,128)(2,1)S(1)}, u32[]{:S(2)}, u32[]{:S(2)}) collective-permute-start(bf16[1040,256]{1,0:T(8,128)(2,1)S(1)} %shard_map.84.a), channel_id=1, source_target_pairs={{16,0},{65,1},{18,2},{67,3},{20,4},{69,5},{22,6},{71,7},{24,8},{73... | collective-permute-start | bytes 1597448 | tf_op jit(solution)/shard_map/ppermute | solution.py:52
  26.1 11.9 %collective-permute-start.6 = (bf16[1040,256]{1,0:T(8,128)(2,1)S(1)}, bf16[1040,256]{1,0:T(8,128)(2,1)S(1)}, u32[]{:S(2)}, u32[]{:S(2)}) collective-permute-start(bf16[1040,256]{1,0:T(8,128)(2,1)S(1)} %shard_map.84.a), channel_id=1, source_target_pairs={{32,0},{129,1},{34,2},{131,3},{36,4},{133,5},{38,6},{135,7},{40,8}... | collective-permute-start | bytes 1597448 | tf_op jit(solution)/shard_map/ppermute | solution.py:52
  26.6 14.8 %collective-permute-start.7 = (bf16[1040,256]{1,0:T(8,128)(2,1)S(1)}, bf16[1040,256]{1,0:T(8,128)(2,1)S(1)}, u32[]{:S(2)}, u32[]{:S(2)}) collective-permute-start(bf16[1040,256]{1,0:T(8,128)(2,1)S(1)} %shard_map.84.a), channel_id=1, source_target_pairs={{48,0},{193,1},{50,2},{195,3},{52,4},{197,5},{54,6},{199,7},{56,8}... | collective-permute-start | bytes 1597448 | tf_op jit(solution)/shard_map/ppermute | solution.py:52
  41.6 15.5 %collective-permute-start.10 = (bf16[2080,256]{1,0:T(8,128)(2,1)S(1)}, bf16[2080,256]{1,0:T(8,128)(2,1)S(1)}, u32[]{:S(2)}, u32[]{:S(2)}) collective-permute-start(bf16[2080,256]{1,0:T(8,128)(2,1)S(1)} %get-tuple-element.26.refs_4_), channel_id=1, source_target_pairs={{192,0},{49,1},{194,2},{51,3},{196,4},{53,5},{198,6},{55,7},{200,8... | collective-permute-start | bytes 3194888 | tf_op jit(solution)/shard_map/ppermute | solution.py:52
  42.9 14.1 %collective-permute-start.8 = (bf16[2080,256]{1,0:T(8,128)(2,1)S(1)}, bf16[2080,256]{1,0:T(8,128)(2,1)S(1)}, u32[]{:S(2)}, u32[]{:S(2)}) collective-permute-start(bf16[2080,256]{1,0:T(8,128)(2,1)S(1)} %get-tuple-element.25.refs_3_), channel_id=1, source_target_pairs={{64,0},{17,1},{66,2},{19,3},{68,4},{21,5},{70,6},{23,7},{72,8},{25... | collective-permute-start | bytes 3194888 | tf_op jit(solution)/shard_map/ppermute | solution.py:52
  44.5 24.0 %collective-permute-start.12 = (bf16[2080,256]{1,0:T(8,128)(2,1)S(1)}, bf16[2080,256]{1,0:T(8,128)(2,1)S(1)}, u32[]{:S(2)}, u32[]{:S(2)}) collective-permute-start(bf16[2080,256]{1,0:T(8,128)(2,1)S(1)} %get-tuple-element.26.refs_4_), channel_id=1, source_target_pairs={{64,0},{17,1},{66,2},{19,3},{68,4},{21,5},{70,6},{23,7},{72,8},{25... | collective-permute-start | bytes 3194888 | tf_op jit(solution)/shard_map/ppermute | solution.py:52
  45.8 22.6 %collective-permute-start.13 = (bf16[2080,256]{1,0:T(8,128)(2,1)S(1)}, bf16[2080,256]{1,0:T(8,128)(2,1)S(1)}, u32[]{:S(2)}, u32[]{:S(2)}) collective-permute-start(bf16[2080,256]{1,0:T(8,128)(2,1)S(1)} %get-tuple-element.25.refs_3_), channel_id=1, source_target_pairs={{192,0},{49,1},{194,2},{51,3},{196,4},{53,5},{198,6},{55,7},{200,8... | collective-permute-start | bytes 3194888 | tf_op jit(solution)/shard_map/ppermute | solution.py:52
  57.0 22.7 %collective-permute-start.11 = (bf16[2080,256]{1,0:T(8,128)(2,1)S(1)}, bf16[2080,256]{1,0:T(8,128)(2,1)S(1)}, u32[]{:S(2)}, u32[]{:S(2)}) collective-permute-start(bf16[2080,256]{1,0:T(8,128)(2,1)S(1)} %collective-permute-done.10.refs_4_), channel_id=1, source_target_pairs={{192,0},{49,1},{194,2},{51,3},{196,4},{53,5},{198,6},{55,7},{200,8... | collective-permute-start | bytes 3194888 | tf_op jit(solution)/shard_map/ppermute | solution.py:52
  57.1 22.8 %collective-permute-start.9 = (bf16[2080,256]{1,0:T(8,128)(2,1)S(1)}, bf16[2080,256]{1,0:T(8,128)(2,1)S(1)}, u32[]{:S(2)}, u32[]{:S(2)}) collective-permute-start(bf16[2080,256]{1,0:T(8,128)(2,1)S(1)} %collective-permute-done.8.refs_3_), channel_id=1, source_target_pairs={{64,0},{17,1},{66,2},{19,3},{68,4},{21,5},{70,6},{23,7},{72,8},{25... | collective-permute-start | bytes 3194888 | tf_op jit(solution)/shard_map/ppermute | solution.py:52
  72.5 11.3 %copy-start.3 = (bf16[256]{0:T(256)(128)(2,1)S(1)}, bf16[256]{0:T(256)(128)(2,1)}, u32[]{:S(2)}) copy-start(bf16[256]{0:T(256)(128)(2,1)} %param.17) | copy-start | bytes 1540
  72.6 11.3 %copy-start.2 = (f32[4096]{0:T(1024)S(1)}, f32[4096]{0:T(1024)}, u32[]{:S(2)}) copy-start(f32[4096]{0:T(1024)} %param.12) | copy-start | bytes 49156
  83.5 3.2 %copy-start.1 = (bf16[256,256]{1,0:T(8,128)(2,1)S(1)}, bf16[256,256]{1,0:T(8,128)(2,1)}, u32[]{:S(2)}) copy-start(bf16[256,256]{1,0:T(8,128)(2,1)} %weight.1) | copy-start | bytes 393220
  83.5 2.9 %collective-permute-start.14 = (bf16[2048,256]{1,0:T(8,128)(2,1)}, bf16[2048,256]{1,0:T(8,128)(2,1)S(1)}, u32[]{:S(2)}, u32[]{:S(2)}) collective-permute-start(bf16[2048,256]{1,0:T(8,128)(2,1)} %get-tuple-element.28), channel_id=1, source_target_pairs={{0,1},{1,0},{2,3},{3,2},{4,5},{5,4},{6,7},{7,6},{8,9},{9,8},{10,11... | collective-permute-start | bytes 3145736 | tf_op jit(solution)/shard_map/ppermute | solution.py:355

commit v3 on v2

--- a/solution.py
+++ b/solution.py
@@ -15,7 +15,7 @@
 LINE = 8 * BLOCK + 16
 DEPTH = 64
 UNROLL = 4
-SEGMENTS = 8
+SEGMENTS = 16
 SEG_SLOTS = 2 * BLOCK + UNROLL
 PACKED = 2 * BLOCK + SEGMENTS * (UNROLL - 1)
 DST_ROWS = DST_BLK * BLOCK
@@ -29,7 +29,15 @@
 
 def from_z(step):
     return [
-        (device(x, y, z - step if r else z + step % 4, r), device(x, y, z, r))
+        (device(x, y, 4 * r + (z + step) % 4, z // 4), device(x, y, z, r))
+        for x in range(NX) for y in range(NY) for z in range(NZ) for r in range(2)
+        if step or r != z // 4
+    ]
+
+
+def from_beside(step):
+    return [
+        (device(x, y, z - step if r else z + step, r), device(x, y, z, r))
         for x in range(NX) for y in range(NY) for z in range(NZ) for r in range(2)
     ]
 
@@ -52,28 +60,33 @@
     return lax.ppermute(value, ("col", "rep"), pairs)
 
 
-def line_kernel(a, b, c, d, own, slots, line):
+def line_kernel(keep, own, b, c, d, a, swapped, codes, line):
     cut = 2 * BLOCK
     norms = []
     for k, shard in enumerate((a, b, c, d)):
-        line[pl.ds(k * cut, cut), :] = shard[pl.ds(0, cut), :]
-        norms.append(shard[pl.ds(cut, 16), :][:1].astype(jnp.float32))
+        rows, norm = shard[pl.ds(0, cut), :], shard[pl.ds(cut, 16), :]
+        if k == 0:
+            rows = jnp.where(keep[0] != 0, own[pl.ds(0, cut), :], rows)
+            norm = jnp.where(keep[0] != 0, own[pl.ds(cut, 16), :], norm)
+        line[pl.ds(k * cut, cut), :] = rows
+        norms.append(norm[:1].astype(jnp.float32))
     rows = jnp.concatenate(norms + [jnp.zeros((12, WIDTH), jnp.float32)], axis=0)
     line[pl.ds(8 * BLOCK, 16), :] = rows.astype(jnp.bfloat16)
 
 
-def make_line(shards, own, slots):
+def make_line(keep, shards, own, slots):
     vmem = pl.BlockSpec(memory_space=pltpu.VMEM)
     return pl.pallas_call(
         line_kernel,
         out_shape=jax.ShapeDtypeStruct((LINE, WIDTH), jnp.bfloat16),
-        in_specs=[vmem] * 4 + [pl.BlockSpec(memory_space=pltpu.HBM), pl.BlockSpec(memory_space=pl.ANY)],
+        in_specs=[pl.BlockSpec(memory_space=pltpu.SMEM)] + [vmem] * 5
+        + [pl.BlockSpec(memory_space=pltpu.HBM), pl.BlockSpec(memory_space=pl.ANY)],
         out_specs=vmem,
         compiler_params=pltpu.CompilerParams(vmem_limit_bytes=4 * MIB),
-    )(*shards, own, slots)
-
-
-def sort_kernel(codes, base, slots, count, listed):
+    )(keep, *shards, own, slots)
+
+
+def sort_codes(codes, base, slots, count, listed):
     def clear(k, carry):
         count[k] = 0
         return carry
@@ -109,25 +122,8 @@
     base[SEGMENTS] = lax.fori_loop(0, SEGMENTS, squeeze, 0)
 
 
-def sort_codes(codes):
-    smem = pl.BlockSpec(memory_space=pltpu.SMEM)
-    return pl.pallas_call(
-        sort_kernel,
-        out_shape=(
-            jax.ShapeDtypeStruct((SEGMENTS + 1,), jnp.int32),
-            jax.ShapeDtypeStruct((PACKED,), jnp.int32),
-        ),
-        in_specs=[smem],
-        out_specs=(smem, smem),
-        scratch_shapes=[
-            pltpu.SMEM((SEGMENTS,), jnp.int32),
-            pltpu.SMEM((SEGMENTS * SEG_SLOTS,), jnp.int32),
-        ],
-        compiler_params=pltpu.CompilerParams(vmem_limit_bytes=2 * MIB),
-    )(codes)
-
-
-def pack_kernel(base, slots, own, other, packed, tile, in_sem):
+def pack_kernel(codes, own, other, base, slots, packed, count, listed, tile, in_sem):
+    sort_codes(codes, base, slots, count, listed)
     total = base[SEGMENTS]
 
     def fetch(g):
@@ -166,37 +162,52 @@
     lax.fori_loop(0, total, step, 0)
 
 
-def pack_tiles(lists, own, other):
+def pack_tiles(codes, own, other):
     smem = pl.BlockSpec(memory_space=pltpu.SMEM)
     hbm = pl.BlockSpec(memory_space=pltpu.HBM)
     ring = (DEPTH // UNROLL, UNROLL, BLOCK, BLOCK)
     return pl.pallas_call(
         pack_kernel,
-        out_shape=jax.ShapeDtypeStruct((PACKED // UNROLL, UNROLL, BLOCK, BLOCK), jnp.bfloat16),
-        in_specs=[smem, smem, hbm, hbm],
-        out_specs=pl.BlockSpec(memory_space=pltpu.VMEM),
-        scratch_shapes=[pltpu.VMEM(ring, jnp.int32), pltpu.SemaphoreType.DMA(ring[:2])],
-        compiler_params=pltpu.CompilerParams(vmem_limit_bytes=16 * MIB),
+        out_shape=(
+            jax.ShapeDtypeStruct((SEGMENTS + 1,), jnp.int32),
+            jax.ShapeDtypeStruct((PACKED,), jnp.int32),
+            jax.ShapeDtypeStruct((PACKED // UNROLL, UNROLL, BLOCK, BLOCK), jnp.bfloat16),
+        ),
+        in_specs=[smem, hbm, hbm],
+        out_specs=(smem, smem, pl.BlockSpec(memory_space=pltpu.VMEM)),
+        scratch_shapes=[
+            pltpu.SMEM((SEGMENTS,), jnp.int32),
+            pltpu.SMEM((SEGMENTS * SEG_SLOTS,), jnp.int32),
+            pltpu.VMEM(ring, jnp.int32),
+            pltpu.SemaphoreType.DMA(ring[:2]),
+        ],
+        compiler_params=pltpu.CompilerParams(vmem_limit_bytes=20 * MIB),
         cost_estimate=pl.CostEstimate(flops=10**6, bytes_accessed=20 * 10**6, transcendentals=0),
-    )(*lists, own, other)
-
-
-def halves_kernel(a, b, c, d, packed, low, high):
-    for out, lines in ((low, (a, b)), (high, (c, d))):
-        for k, line in enumerate(lines):
-            out[pl.ds(k * LINE, LINE), :] = line[...]
-
-
-def make_halves(lines, packed):
+    )(codes, own, other)
+
+
+def join_kernel(odd, a, b, c, d, packed, single, double):
+    double[pl.ds(0, LINE), :] = b[...]
+    double[pl.ds(LINE, LINE), :] = c[...]
+
+    @pl.when(odd[0] == 0)
+    def _():
+        single[...] = a[...]
+
+    @pl.when(odd[0] != 0)
+    def _():
+        single[...] = d[...]
+
+
+def join_lines(odd, lines, packed):
     vmem = pl.BlockSpec(memory_space=pltpu.VMEM)
-    half = jax.ShapeDtypeStruct((2 * LINE, WIDTH), jnp.bfloat16)
     return pl.pallas_call(
-        halves_kernel,
-        out_shape=(half, half),
-        in_specs=[vmem] * 4 + [pl.BlockSpec(memory_space=pl.ANY)],
+        join_kernel,
+        out_shape=tuple(jax.ShapeDtypeStruct((n * LINE, WIDTH), jnp.bfloat16) for n in (1, 2)),
+        in_specs=[pl.BlockSpec(memory_space=pltpu.SMEM)] + [vmem] * 4 + [pl.BlockSpec(memory_space=pl.ANY)],
         out_specs=(vmem, vmem),
         compiler_params=pltpu.CompilerParams(vmem_limit_bytes=8 * MIB),
-    )(*lines, packed)
+    )(odd, *lines, packed)
 
 
 def sum_kernel(ids, before, *refs):
@@ -214,7 +225,7 @@
     else:
         total[...] = jnp.zeros_like(total)
     for i, piece in enumerate(pieces):
-        for line in range(2):
+        for line in range(piece.shape[0] // LINE):
             for half in range(2):
                 rows = piece[pl.ds(line * LINE + 8 * BLOCK, 16), pl.ds(half * BLOCK, BLOCK)]
                 norm[pl.ds(32 * i + 16 * half + 8 * line, 8), :] = rows.astype(jnp.float32)[:8]
@@ -301,29 +312,40 @@
     )(kept, received, scale, weight, bias)
 
 
+OWN_0, OWN_12, OWN_3 = 0, 1, 2
+UP, UP_12, UP_Z = 4, 5, 6
+FAR, FAR_12, FAR_Z = 8, 9, 10
+DOWN, DOWN_12, DOWN_Z = 12, 13, 14
+
+
 def encode(src, dst, place):
     z, second, third, rep = place
     entry = jnp.arange(2 * BLOCK, dtype=jnp.int32)
     p = src >> 1
-    dz = ((p & 7) - z) & 7
-    px, py = p >> 5, (p >> 3) & 3
+    px, py, pz = p >> 5, (p >> 3) & 3, p & 7
     pa = jnp.where(rep == 0, py, px)
     pb = jnp.where(rep == 0, px, py)
-    shard = jnp.where(rep == 0, dz, 8 - dz) & 3
     da, db = (pa - second) & 3, (pb - third) & 3
-    line = da & 1
+    double = (da == 1) | (da == 2)
+    beside = (db != 0) & (da == jnp.where((z & 1) == 0, 3, 0))
+    own_kind = jnp.where(double, 1, jnp.where(da == 0, 0, 2))
+    far_kind = jnp.where(double, 1, jnp.where(beside, 2, 0))
+    segment = db * 4 + jnp.where(db == 0, own_kind, far_kind)
+    line = jnp.where(da == 2, 1, 0)
+    z_of = jnp.where(beside, jnp.where((rep == 0) == (db != 3), z + 1, z - 1), z)
+    shard = (pz - z_of) & 3
     d = (dst + 16 * (1 - rep)) & 31
-    segment = db * 2 + (da >> 1)
     row16 = line * (LINE // 16) + shard * 16 + (src & 1) * 8
     scale = (src & 1) * 16 + line * 8 + shard
-    valid = jnp.where((dz >> 2) == rep, 1, 0)
+    valid = jnp.where((pz >> 2) == rep, 1, 0)
     return entry | (d << 8) | (row16 << 13) | (scale << 21) | (segment << 26) | (valid << 30)
 
 
 def gather_shards(features, src_norm):
-    norm_rows = jnp.zeros((16, WIDTH), jnp.bfloat16).at[0].set(src_norm)
+    norm_rows = jnp.broadcast_to(src_norm, (16, WIDTH))
     shard = jnp.concatenate([features, norm_rows], axis=0)
-    return [move(shard, from_z(step)) for step in (4, 1, 2, 3)]
+    near = [move(shard, from_z(step)) for step in (1, 2, 3)]
+    return [shard, *near, move(shard, from_z(0))]
 
 
 def body(features, src_norm, dst_norm, src_block, dst_block, counts, weight, out_bias):
@@ -337,21 +359,25 @@
     all_ids = lax.all_gather(ids, "rep")
     both = jnp.concatenate([ids, jnp.where(rep == 0, all_ids[1], all_ids[0])], axis=1)
     place = (z, jnp.where(rep == 0, y, x), jnp.where(rep == 0, x, y), rep)
-    base, slots = sort_codes(encode(both[0], both[1], place))
-    line_0 = make_line(gather_shards(features, src_norm), other, slots)
+    codes = encode(both[0], both[1], place)
+    line_0 = make_line(
+        jnp.where(z // 4 == rep, 1, 0).astype(jnp.int32).reshape(1), gather_shards(features, src_norm), other, codes)
     lines = [line_0] + [move(line_0, from_second(step)) for step in (1, 2, 3)]
-    packed = pack_tiles((base, slots), own, other)
-    lists = (base, slots, packed)
-    half_0, half_1 = make_halves(lines, packed)
-    up_0 = move(half_0, from_third(1))
-    down_1 = move(half_1, from_third(-1))
-    up_1 = move(half_1, from_third(1))
-    down_0 = move(half_0, from_third(-1))
-    across_0 = move(up_0, from_third(1))
-    across_1 = move(down_1, from_third(-1))
-    total = sum_tiles(lists, {0: half_0, 1: half_1})
-    total = sum_tiles(lists, {2: up_0, 7: down_1, 3: up_1, 6: down_0}, total)
-    sent, kept = sum_tiles(lists, {4: across_0, 5: across_1}, total, True)
+    lists = pack_tiles(codes, own, other)
+    single, double = join_lines((z & 1).astype(jnp.int32).reshape(1), lines, lists[2])
+    up = move(single, from_third(1))
+    down_12 = move(double, from_third(-1))
+    up_12 = move(double, from_third(1))
+    down = move(single, from_third(-1))
+    up_z = move(up, from_beside(1))
+    down_z = move(down, from_beside(-1))
+    far = move(up, from_third(1))
+    far_12 = move(down_12, from_third(-1))
+    far_z = move(up_z, from_third(1))
+    total = sum_tiles(lists, {OWN_0: lines[0], OWN_12: double, OWN_3: lines[3]})
+    near = {UP: up, UP_Z: up_z, DOWN_12: down_12, DOWN: down, UP_12: up_12, FAR: far}
+    total = sum_tiles(lists, near, total)
+    sent, kept = sum_tiles(lists, {FAR_12: far_12, FAR_Z: far_z, DOWN_Z: down_z}, total, True)
     received = lax.ppermute(sent, "rep", swap)
     own_norm = lax.dynamic_slice_in_dim(dst_norm, rep * HALF, HALF, 0)
     scale = jnp.broadcast_to(own_norm[:, None], (HALF, BLOCK))

time: 88.7 us -> 84.9 us (0.957)
  waiting for transfers between devices: 34.5 us -> 25.3 us
  starting transfers between devices: 23.4 us -> 28.7 us
    ppermute x13 -> x16, waiting for transfers between devices: 31.9 us -> 22.4 us  [move(): return lax.ppermute(value, ('col', 'rep'), pairs)]
    ppermute x13 -> x16, starting transfers between devices: 19.9 us -> 25.5 us  [move(): return lax.ppermute(value, ('col', 'rep'), pairs)]
    pallas_call x3 -> x2, Pallas kernels: 13.9 us -> 13.5 us  [the longest x1 13.4 us: pack_tiles(): pl.pallas_call(pack_kernel, out_shape=(jax.ShapeDtypeStruct((SEGMENTS + 1...]
  transfers between devices with their start and end apart: 15 -> 18, of which waited for: 8 -> 9; matrix products, arithmetic and copies ran while one was open for 3% -> 4% of each run, Pallas kernels for 22% -> 24%
where the time goes in v3:
time: 84.9 us; the launch traced here: 84.4 us
  starting transfers between devices  28.7 us (34%)
  waiting for transfers between devices  25.3 us (30%)
  Pallas kernels  24.9 us (29%)
  other arithmetic  2.33 us (3%)
  blocking collectives  1.77 us (2%)
  local copies, waits for them, and re-layouts  1.01 us (1%)
    ppermute x16, starting transfers between devices, move(): return lax.ppermute(value, ('col', 'rep'), pairs)  25.5 us
    ppermute x16, waiting for transfers between devices, move(): return lax.ppermute(value, ('col', 'rep'), pairs)  22.4 us
    pallas_call x1, Pallas kernels, pack_tiles(): pl.pallas_call(pack_kernel, out_shape=(jax.ShapeDtypeStruct((SEGMENTS + 1...  13.4 us
    pallas_call x3, Pallas kernels, sum_tiles(): pl.pallas_call(functools.partial(sum_kernel, ids, bool(before)), out_shap...  10 us
    ppermute x1, starting transfers between devices, body(): other = lax.ppermute(own, 'rep', swap)  3.24 us
    ppermute x1, waiting for transfers between devices, body(): received = lax.ppermute(sent, 'rep', swap)  2.83 us
    all_gather x1, blocking collectives, body(): all_ids = lax.all_gather(ids, 'rep')  1.77 us
  transfers between devices with their start and end apart: 18, of which 9 were waited for; matrix products, arithmetic and copies ran while one was open for 4% of the time, Pallas kernels for 24%

profile of v3, /device:TPU:1, one launch (start us, length us, event | category | flops | bytes accessed | tf_op | source)
XLA Modules:
  0.0 84.4 jit_solution(18066328253452051542)
XLA Ops:
  0.0 3.2 %collective-permute-start = (s32[128,128,128]{2,1,0:T(8,128)}, s32[128,128,128]{2,1,0:T(8,128)}, u32[]{:S(2)}, u32[]{:S(2)}) collective-permute-start(s32[128,128,128]{2,1,0:T(8,128)} %bitcast.15), channel_id=1, source_target_pairs={{0,1},{1,0},{2,3},{3,2},{4,5},{5,4},{6,7},{7,6},{8,9},{9,8},{10,11... | collective-permute-start | bytes 25165832 | tf_op jit(solution)/shard_map/ppermute | solution.py:357
  3.2 0.7 broadcast_in_dim.40
  3.9 0.9 %pad_maximum_fusion.own = bf16[272,256]{1,0:T(8,128)(2,1)S(1)} fusion(bf16[16,256]{1,0:T(8,128)(2,1)S(1)} %broadcast_in_dim.40, bf16[256,256]{1,0:T(8,128)(2,1)} %param.8), kind=kLoop, calls=%fused_computation | loop fusion | flops 278528 | bytes 278528 | tf_op jit(solution)/shard_map/concatenate | solution.py:346
  4.8 3.8 %collective-permute-start.1 = (bf16[272,256]{1,0:T(8,128)(2,1)S(1)}, bf16[272,256]{1,0:T(8,128)(2,1)S(1)}, u32[]{:S(2)}, u32[]{:S(2)}) collective-permute-start(bf16[272,256]{1,0:T(8,128)(2,1)S(1)} %pad_maximum_fusion.own), channel_id=1, source_target_pairs={{2,0},{10,1},{4,2},{12,3},{6,4},{14,5},{0,6},{8,7},{3,8},{11,9},{5... | collective-permute-start | bytes 417800 | tf_op jit(solution)/shard_map/ppermute | solution.py:60
  8.6 0.5 collective-permute-start.2
  9.2 4.7 %collective-permute-start.3 = (bf16[272,256]{1,0:T(8,128)(2,1)S(1)}, bf16[272,256]{1,0:T(8,128)(2,1)S(1)}, u32[]{:S(2)}, u32[]{:S(2)}) collective-permute-start(bf16[272,256]{1,0:T(8,128)(2,1)S(1)} %pad_maximum_fusion.own), channel_id=1, source_target_pairs={{6,0},{14,1},{0,2},{8,3},{2,4},{10,5},{4,6},{12,7},{7,8},{15,9},{1... | collective-permute-start | bytes 417800 | tf_op jit(solution)/shard_map/ppermute | solution.py:60
  13.8 2.8 %collective-permute-start.4 = (bf16[272,256]{1,0:T(8,128)(2,1)S(1)}, bf16[272,256]{1,0:T(8,128)(2,1)S(1)}, u32[]{:S(2)}, u32[]{:S(2)}) collective-permute-start(bf16[272,256]{1,0:T(8,128)(2,1)S(1)} %pad_maximum_fusion.own), channel_id=1, source_target_pairs={{8,1},{10,3},{12,5},{14,7},{1,8},{3,10},{5,12},{7,14},{24,17},{26,... | collective-permute-start | bytes 417800 | tf_op jit(solution)/shard_map/ppermute | solution.py:60
  16.7 0.7 add_bitcast_fusion
  17.4 1.8 %all-gather.1 = s32[2,2,128]{2,1,0:T(2,128)S(1)} all-gather(s32[1,2,128]{2,1,0:T(2,128)S(1)} %add_bitcast_fusion), channel_id=2, replica_groups=mesh['col'=128,'rep'=2] {'rep'}, dimensions={0}, use_global_device_ids=true | all-gather | bytes 3072 | tf_op jit(solution)/shard_map/all_gather | solution.py:359
  19.2 0.7 pad_add_fusion
  19.9 0.0 collective-permute-done.1.b
  19.9 0.0 collective-permute-done.2.c
  19.9 2.5 %collective-permute-done.3.d = bf16[272,256]{1,0:T(8,128)(2,1)S(1)} collective-permute-done((bf16[272,256]{1,0:T(8,128)(2,1)S(1)}, bf16[272,256]{1,0:T(8,128)(2,1)S(1)}, u32[]{:S(2)}, u32[]{:S(2)}) %collective-permute-start.3) | collective-permute-done | bytes 139296 | tf_op jit(solution)/shard_map/ppermute | solution.py:60
  22.4 2.3 %collective-permute-done.4.a = bf16[272,256]{1,0:T(8,128)(2,1)S(1)} collective-permute-done((bf16[272,256]{1,0:T(8,128)(2,1)S(1)}, bf16[272,256]{1,0:T(8,128)(2,1)S(1)}, u32[]{:S(2)}, u32[]{:S(2)}) %collective-permute-start.4) | collective-permute-done | bytes 139296 | tf_op jit(solution)/shard_map/ppermute | solution.py:60
  24.7 0.0 collective-permute-done.other.swapped
  24.7 2.6 %collective-permute-start.5 = (bf16[1040,256]{1,0:T(8,128)(2,1)S(1)}, bf16[1040,256]{1,0:T(8,128)(2,1)S(1)}, u32[]{:S(2)}, u32[]{:S(2)}) collective-permute-start(bf16[1040,256]{1,0:T(8,128)(2,1)S(1)} %shard_map.83.a.refs_3_), channel_id=1, source_target_pairs={{16,0},{65,1},{18,2},{67,3},{20,4},{69,5},{22,6},{71,7},{24,8},{73... | collective-permute-start | bytes 1597448 | tf_op jit(solution)/shard_map/ppermute | solution.py:60
  27.3 0.5 collective-permute-start.6
  27.8 0.6 collective-permute-start.7
  28.4 13.4 %shard_map.82 = (s32[17]{0:T(128)S(1)}, s32[304]{0:T(512)S(1)}, bf16[76,4,128,128]{3,2,1,0:T(8,128)(2,1)S(1)}) custom-call(s32[256]{0:T(256)S(1)} %or_or_fusion.codes, s32[128,128,128]{2,1,0:T(8,128)S(1)} %bitcast.16, s32[128,128,128]{2,1,0:T(8,128)} %collective-permute-done.other.swapped), custom_call_target="tpu_custom_call" | custom-call | flops 1000000 | bytes 20000000 | tf_op jit(solution)/shard_map/pallas_call | solution.py:169
  41.9 0.0 collective-permute-done.6.c
  41.9 0.7 collective-permute-done.7.d.refs_5_
  42.6 0.1 shard_map.84
  42.7 2.6 %collective-permute-start.8 = (bf16[2080,256]{1,0:T(8,128)(2,1)S(1)}, bf16[2080,256]{1,0:T(8,128)(2,1)S(1)}, u32[]{:S(2)}, u32[]{:S(2)}) collective-permute-start(bf16[2080,256]{1,0:T(8,128)(2,1)S(1)} %get-tuple-element.15.refs_4_), channel_id=1, source_target_pairs={{192,0},{49,1},{194,2},{51,3},{196,4},{53,5},{198,6},{55,7},{200,8... | collective-permute-start | bytes 3194888 | tf_op jit(solution)/shard_map/ppermute | solution.py:60
  45.3 0.4 collective-permute-start.10
  45.7 1.4 %collective-permute-start.15 = (bf16[2080,256]{1,0:T(8,128)(2,1)S(1)}, bf16[2080,256]{1,0:T(8,128)(2,1)S(1)}, u32[]{:S(2)}, u32[]{:S(2)}) collective-permute-start(bf16[2080,256]{1,0:T(8,128)(2,1)S(1)} %get-tuple-element.15.refs_4_), channel_id=1, source_target_pairs={{64,0},{17,1},{66,2},{19,3},{68,4},{21,5},{70,6},{23,7},{72,8},{25... | collective-permute-start | bytes 3194888 | tf_op jit(solution)/shard_map/ppermute | solution.py:60
  47.1 0.1 collective-permute-start.13
  47.2 6.5 %collective-permute-done.10.refs_3_ = bf16[1040,256]{1,0:T(8,128)(2,1)S(1)} collective-permute-done((bf16[1040,256]{1,0:T(8,128)(2,1)S(1)}, bf16[1040,256]{1,0:T(8,128)(2,1)S(1)}, u32[]{:S(2)}, u32[]{:S(2)}) %collective-permute-start.10) | collective-permute-done | bytes 532512 | tf_op jit(solution)/shard_map/ppermute | solution.py:60
  53.7 1.4 %collective-permute-start.11 = (bf16[1040,256]{1,0:T(8,128)(2,1)S(1)}, bf16[1040,256]{1,0:T(8,128)(2,1)S(1)}, u32[]{:S(2)}, u32[]{:S(2)}) collective-permute-start(bf16[1040,256]{1,0:T(8,128)(2,1)S(1)} %collective-permute-done.10.refs_3_), channel_id=1, source_target_pairs={{2,0},{15,1},{4,2},{1,3},{6,4},{3,5},{8,6},{5,7},{10,8},{7,9},{12,... | collective-permute-start | bytes 1597448 | tf_op jit(solution)/shard_map/ppermute | solution.py:60
  55.1 3.2 %collective-permute-done.8.refs_5_ = bf16[2080,256]{1,0:T(8,128)(2,1)S(1)} collective-permute-done((bf16[2080,256]{1,0:T(8,128)(2,1)S(1)}, bf16[2080,256]{1,0:T(8,128)(2,1)S(1)}, u32[]{:S(2)}, u32[]{:S(2)}) %collective-permute-start.8) | collective-permute-done | bytes 1064992 | tf_op jit(solution)/shard_map/ppermute | solution.py:60
  58.3 1.1 %collective-permute-start.9 = (bf16[2080,256]{1,0:T(8,128)(2,1)S(1)}, bf16[2080,256]{1,0:T(8,128)(2,1)S(1)}, u32[]{:S(2)}, u32[]{:S(2)}) collective-permute-start(bf16[2080,256]{1,0:T(8,128)(2,1)S(1)} %collective-permute-done.8.refs_5_), channel_id=1, source_target_pairs={{192,0},{49,1},{194,2},{51,3},{196,4},{53,5},{198,6},{55,7},{200,8... | collective-permute-start | bytes 3194888 | tf_op jit(solution)/shard_map/ppermute | solution.py:60
  59.4 1.5 %collective-permute-start.16 = (bf16[1040,256]{1,0:T(8,128)(2,1)S(1)}, bf16[1040,256]{1,0:T(8,128)(2,1)S(1)}, u32[]{:S(2)}, u32[]{:S(2)}) collective-permute-start(bf16[1040,256]{1,0:T(8,128)(2,1)S(1)} %collective-permute-done.10.refs_3_), channel_id=1, source_target_pairs={{64,0},{17,1},{66,2},{19,3},{68,4},{21,5},{70,6},{23,7},{72,8},{25... | collective-permute-start | bytes 1597448 | tf_op jit(solution)/shard_map/ppermute | solution.py:60
  61.0 3.0 %collective-permute-done.13.refs_6_ = bf16[1040,256]{1,0:T(8,128)(2,1)S(1)} collective-permute-done((bf16[1040,256]{1,0:T(8,128)(2,1)S(1)}, bf16[1040,256]{1,0:T(8,128)(2,1)S(1)}, u32[]{:S(2)}, u32[]{:S(2)}) %collective-permute-start.13) | collective-permute-done | bytes 532512 | tf_op jit(solution)/shard_map/ppermute | solution.py:60
  64.0 0.0 collective-permute-start.14
  64.0 0.0 collective-permute-done.11.refs_4_
  64.0 1.5 %collective-permute-start.12 = (bf16[1040,256]{1,0:T(8,128)(2,1)S(1)}, bf16[1040,256]{1,0:T(8,128)(2,1)S(1)}, u32[]{:S(2)}, u32[]{:S(2)}) collective-permute-start(bf16[1040,256]{1,0:T(8,128)(2,1)S(1)} %collective-permute-done.11.refs_4_), channel_id=1, source_target_pairs={{64,0},{17,1},{66,2},{19,3},{68,4},{21,5},{70,6},{23,7},{72,8},{25... | collective-permute-start | bytes 1597448 | tf_op jit(solution)/shard_map/ppermute | solution.py:60
  65.5 2.6 %shard_map.85.refs_9_ = f32[4096,256]{1,0:T(8,128)S(1)} custom-call(s32[17]{0:T(128)S(1)} %get-tuple-element.12.refs_0_, s32[304]{0:T(512)S(1)} %get-tuple-element.13.refs_1_, bf16[76,4,128,128]{3,2,1,0:T(8,128)(2,1)S(1)} %get-tuple-element.14.packed.refs_2_, bf16[1040,256]{1,0:T(8,128)(2,1)S(1)} %shard_map.83.a.refs_3_, ...), custom_call_target="tpu_custom_call" | custom-call | flops 400000000 | bytes 8000000 | tf_op jit(solution)/shard_map/pallas_call | solution.py:274
  68.0 2.8 %collective-permute-done.16.refs_8_ = bf16[1040,256]{1,0:T(8,128)(2,1)S(1)} collective-permute-done((bf16[1040,256]{1,0:T(8,128)(2,1)S(1)}, bf16[1040,256]{1,0:T(8,128)(2,1)S(1)}, u32[]{:S(2)}, u32[]{:S(2)}) %collective-permute-start.16) | collective-permute-done | bytes 532512 | tf_op jit(solution)/shard_map/ppermute | solution.py:60
  70.8 4.0 %shard_map.86.refs_6_ = f32[4096,256]{1,0:T(8,128)S(1)} custom-call(s32[17]{0:T(128)S(1)} %get-tuple-element.12.refs_0_, s32[304]{0:T(512)S(1)} %get-tuple-element.13.refs_1_, bf16[76,4,128,128]{3,2,1,0:T(8,128)(2,1)S(1)} %get-tuple-element.14.packed.refs_2_, bf16[1040,256]{1,0:T(8,128)(2,1)S(1)} %collective-permute-done.10.refs_3_, ...), custom_call_target="tpu_custom_call" | custom-call | flops 400000000 | bytes 8000000 | tf_op jit(solution)/shard_map/pallas_call | solution.py:274
  74.8 0.0 copy-start.3
  74.8 0.0 copy-start.2
  74.9 0.0 copy-start.1
  74.9 0.0 collective-permute-done.14.refs_5_
  74.9 1.4 %collective-permute-done.12.refs_4_ = bf16[1040,256]{1,0:T(8,128)(2,1)S(1)} collective-permute-done((bf16[1040,256]{1,0:T(8,128)(2,1)S(1)}, bf16[1040,256]{1,0:T(8,128)(2,1)S(1)}, u32[]{:S(2)}, u32[]{:S(2)}) %collective-permute-start.12) | collective-permute-done | bytes 532512 | tf_op jit(solution)/shard_map/ppermute | solution.py:60
  76.3 0.0 collective-permute-done.9.refs_3_
  76.3 3.5 %shard_map.87 = (bf16[2048,256]{1,0:T(8,128)(2,1)}, f32[2048,256]{1,0:T(8,128)S(1)}) custom-call(s32[17]{0:T(128)S(1)} %get-tuple-element.12.refs_0_, s32[304]{0:T(512)S(1)} %get-tuple-element.13.refs_1_, bf16[76,4,128,128]{3,2,1,0:T(8,128)(2,1)S(1)} %get-tuple-element.14.packed.refs_2_, bf16[2080,256]{1,0:T(8,128)(2,1)S(1)} %collective-permute-done.9.refs_3_, ...), custom_call_target="tpu_custom_call" | custom-call | flops 400000000 | bytes 8000000 | tf_op jit(solution)/shard_map/pallas_call | solution.py:274
  79.8 2.8 %collective-permute-done.17.received = bf16[2048,256]{1,0:T(8,128)(2,1)S(1)} collective-permute-done((bf16[2048,256]{1,0:T(8,128)(2,1)}, bf16[2048,256]{1,0:T(8,128)(2,1)S(1)}, u32[]{:S(2)}, u32[]{:S(2)}) %collective-permute-start.17) | collective-permute-done | bytes 1048608 | tf_op jit(solution)/shard_map/ppermute | solution.py:381
  82.6 0.3 broadcast_in_dim.41.scale
  83.0 1.3 %shard_map.88 = bf16[2048,256]{1,0:T(8,128)(2,1)} custom-call(f32[2048,256]{1,0:T(8,128)S(1)} %get-tuple-element.17.kept, bf16[2048,256]{1,0:T(8,128)(2,1)S(1)} %collective-permute-done.17.received, f32[2048,128]{1,0:T(8,128)S(1)} %broadcast_in_dim.41.scale, bf16[256,256]{1,0:T(8,128)(2,1)S(1)} %copy-done.1, f32[1,256]{1,0:T(1,128)S(1)} %bitcast.17), custom_call_target="tpu_custom_call" | custom-call | flops 300000000 | bytes 6000000 | tf_op jit(solution)/shard_map/pallas_call | solution.py:304
  (15 shorter events, 0.1 us)
Async XLA Ops:
  0.0 24.7 %collective-permute-start = (s32[128,128,128]{2,1,0:T(8,128)}, s32[128,128,128]{2,1,0:T(8,128)}, u32[]{:S(2)}, u32[]{:S(2)}) collective-permute-start(s32[128,128,128]{2,1,0:T(8,128)} %bitcast.15), channel_id=1, source_target_pairs={{0,1},{1,0},{2,3},{3,2},{4,5},{5,4},{6,7},{7,6},{8,9},{9,8},{10,11... | collective-permute-start | bytes 25165832 | tf_op jit(solution)/shard_map/ppermute | solution.py:357
  4.8 15.1 %collective-permute-start.1 = (bf16[272,256]{1,0:T(8,128)(2,1)S(1)}, bf16[272,256]{1,0:T(8,128)(2,1)S(1)}, u32[]{:S(2)}, u32[]{:S(2)}) collective-permute-start(bf16[272,256]{1,0:T(8,128)(2,1)S(1)} %pad_maximum_fusion.own), channel_id=1, source_target_pairs={{2,0},{10,1},{4,2},{12,3},{6,4},{14,5},{0,6},{8,7},{3,8},{11,9},{5... | collective-permute-start | bytes 417800 | tf_op jit(solution)/shard_map/ppermute | solution.py:60
  8.6 11.3 %collective-permute-start.2 = (bf16[272,256]{1,0:T(8,128)(2,1)S(1)}, bf16[272,256]{1,0:T(8,128)(2,1)S(1)}, u32[]{:S(2)}, u32[]{:S(2)}) collective-permute-start(bf16[272,256]{1,0:T(8,128)(2,1)S(1)} %pad_maximum_fusion.own), channel_id=1, source_target_pairs={{4,0},{12,1},{6,2},{14,3},{0,4},{8,5},{2,6},{10,7},{5,8},{13,9},{7... | collective-permute-start | bytes 417800 | tf_op jit(solution)/shard_map/ppermute | solution.py:60
  9.2 13.2 %collective-permute-start.3 = (bf16[272,256]{1,0:T(8,128)(2,1)S(1)}, bf16[272,256]{1,0:T(8,128)(2,1)S(1)}, u32[]{:S(2)}, u32[]{:S(2)}) collective-permute-start(bf16[272,256]{1,0:T(8,128)(2,1)S(1)} %pad_maximum_fusion.own), channel_id=1, source_target_pairs={{6,0},{14,1},{0,2},{8,3},{2,4},{10,5},{4,6},{12,7},{7,8},{15,9},{1... | collective-permute-start | bytes 417800 | tf_op jit(solution)/shard_map/ppermute | solution.py:60
  13.8 10.9 %collective-permute-start.4 = (bf16[272,256]{1,0:T(8,128)(2,1)S(1)}, bf16[272,256]{1,0:T(8,128)(2,1)S(1)}, u32[]{:S(2)}, u32[]{:S(2)}) collective-permute-start(bf16[272,256]{1,0:T(8,128)(2,1)S(1)} %pad_maximum_fusion.own), channel_id=1, source_target_pairs={{8,1},{10,3},{12,5},{14,7},{1,8},{3,10},{5,12},{7,14},{24,17},{26,... | collective-permute-start | bytes 417800 | tf_op jit(solution)/shard_map/ppermute | solution.py:60
  24.7 3.7 %copy-start = (s32[1,1,128,128,128]{4,3,2,1,0:T(8,128)S(1)}, s32[1,1,128,128,128]{4,3,2,1,0:T(8,128)}, u32[]{:S(2)}) copy-start(s32[1,1,128,128,128]{4,3,2,1,0:T(8,128)} %param.13) | copy-start | bytes 25165828
  24.7 17.1 %collective-permute-start.5 = (bf16[1040,256]{1,0:T(8,128)(2,1)S(1)}, bf16[1040,256]{1,0:T(8,128)(2,1)S(1)}, u32[]{:S(2)}, u32[]{:S(2)}) collective-permute-start(bf16[1040,256]{1,0:T(8,128)(2,1)S(1)} %shard_map.83.a.refs_3_), channel_id=1, source_target_pairs={{16,0},{65,1},{18,2},{67,3},{20,4},{69,5},{22,6},{71,7},{24,8},{73... | collective-permute-start | bytes 1597448 | tf_op jit(solution)/shard_map/ppermute | solution.py:60
  27.3 14.6 %collective-permute-start.6 = (bf16[1040,256]{1,0:T(8,128)(2,1)S(1)}, bf16[1040,256]{1,0:T(8,128)(2,1)S(1)}, u32[]{:S(2)}, u32[]{:S(2)}) collective-permute-start(bf16[1040,256]{1,0:T(8,128)(2,1)S(1)} %shard_map.83.a.refs_3_), channel_id=1, source_target_pairs={{32,0},{129,1},{34,2},{131,3},{36,4},{133,5},{38,6},{135,7},{40,8}... | collective-permute-start | bytes 1597448 | tf_op jit(solution)/shard_map/ppermute | solution.py:60
  27.8 14.8 %collective-permute-start.7 = (bf16[1040,256]{1,0:T(8,128)(2,1)S(1)}, bf16[1040,256]{1,0:T(8,128)(2,1)S(1)}, u32[]{:S(2)}, u32[]{:S(2)}) collective-permute-start(bf16[1040,256]{1,0:T(8,128)(2,1)S(1)} %shard_map.83.a.refs_3_), channel_id=1, source_target_pairs={{48,0},{193,1},{50,2},{195,3},{52,4},{197,5},{54,6},{199,7},{56,8}... | collective-permute-start | bytes 1597448 | tf_op jit(solution)/shard_map/ppermute | solution.py:60
  42.7 15.5 %collective-permute-start.8 = (bf16[2080,256]{1,0:T(8,128)(2,1)S(1)}, bf16[2080,256]{1,0:T(8,128)(2,1)S(1)}, u32[]{:S(2)}, u32[]{:S(2)}) collective-permute-start(bf16[2080,256]{1,0:T(8,128)(2,1)S(1)} %get-tuple-element.15.refs_4_), channel_id=1, source_target_pairs={{192,0},{49,1},{194,2},{51,3},{196,4},{53,5},{198,6},{55,7},{200,8... | collective-permute-start | bytes 3194888 | tf_op jit(solution)/shard_map/ppermute | solution.py:60
  45.3 8.4 %collective-permute-start.10 = (bf16[1040,256]{1,0:T(8,128)(2,1)S(1)}, bf16[1040,256]{1,0:T(8,128)(2,1)S(1)}, u32[]{:S(2)}, u32[]{:S(2)}) collective-permute-start(bf16[1040,256]{1,0:T(8,128)(2,1)S(1)} %get-tuple-element.16), channel_id=1, source_target_pairs={{64,0},{17,1},{66,2},{19,3},{68,4},{21,5},{70,6},{23,7},{72,8},{25... | collective-permute-start | bytes 1597448 | tf_op jit(solution)/shard_map/ppermute | solution.py:60
  45.7 25.1 %collective-permute-start.15 = (bf16[2080,256]{1,0:T(8,128)(2,1)S(1)}, bf16[2080,256]{1,0:T(8,128)(2,1)S(1)}, u32[]{:S(2)}, u32[]{:S(2)}) collective-permute-start(bf16[2080,256]{1,0:T(8,128)(2,1)S(1)} %get-tuple-element.15.refs_4_), channel_id=1, source_target_pairs={{64,0},{17,1},{66,2},{19,3},{68,4},{21,5},{70,6},{23,7},{72,8},{25... | collective-permute-start | bytes 3194888 | tf_op jit(solution)/shard_map/ppermute | solution.py:60
  47.1 16.9 %collective-permute-start.13 = (bf16[1040,256]{1,0:T(8,128)(2,1)S(1)}, bf16[1040,256]{1,0:T(8,128)(2,1)S(1)}, u32[]{:S(2)}, u32[]{:S(2)}) collective-permute-start(bf16[1040,256]{1,0:T(8,128)(2,1)S(1)} %get-tuple-element.16), channel_id=1, source_target_pairs={{192,0},{49,1},{194,2},{51,3},{196,4},{53,5},{198,6},{55,7},{200,8... | collective-permute-start | bytes 1597448 | tf_op jit(solution)/shard_map/ppermute | solution.py:60
  53.7 10.3 %collective-permute-start.11 = (bf16[1040,256]{1,0:T(8,128)(2,1)S(1)}, bf16[1040,256]{1,0:T(8,128)(2,1)S(1)}, u32[]{:S(2)}, u32[]{:S(2)}) collective-permute-start(bf16[1040,256]{1,0:T(8,128)(2,1)S(1)} %collective-permute-done.10.refs_3_), channel_id=1, source_target_pairs={{2,0},{15,1},{4,2},{1,3},{6,4},{3,5},{8,6},{5,7},{10,8},{7,9},{12,... | collective-permute-start | bytes 1597448 | tf_op jit(solution)/shard_map/ppermute | solution.py:60
  58.3 18.0 %collective-permute-start.9 = (bf16[2080,256]{1,0:T(8,128)(2,1)S(1)}, bf16[2080,256]{1,0:T(8,128)(2,1)S(1)}, u32[]{:S(2)}, u32[]{:S(2)}) collective-permute-start(bf16[2080,256]{1,0:T(8,128)(2,1)S(1)} %collective-permute-done.8.refs_5_), channel_id=1, source_target_pairs={{192,0},{49,1},{194,2},{51,3},{196,4},{53,5},{198,6},{55,7},{200,8... | collective-permute-start | bytes 3194888 | tf_op jit(solution)/shard_map/ppermute | solution.py:60
  59.4 11.4 %collective-permute-start.16 = (bf16[1040,256]{1,0:T(8,128)(2,1)S(1)}, bf16[1040,256]{1,0:T(8,128)(2,1)S(1)}, u32[]{:S(2)}, u32[]{:S(2)}) collective-permute-start(bf16[1040,256]{1,0:T(8,128)(2,1)S(1)} %collective-permute-done.10.refs_3_), channel_id=1, source_target_pairs={{64,0},{17,1},{66,2},{19,3},{68,4},{21,5},{70,6},{23,7},{72,8},{25... | collective-permute-start | bytes 1597448 | tf_op jit(solution)/shard_map/ppermute | solution.py:60
  64.0 10.9 %collective-permute-start.14 = (bf16[1040,256]{1,0:T(8,128)(2,1)S(1)}, bf16[1040,256]{1,0:T(8,128)(2,1)S(1)}, u32[]{:S(2)}, u32[]{:S(2)}) collective-permute-start(bf16[1040,256]{1,0:T(8,128)(2,1)S(1)} %collective-permute-done.13.refs_6_), channel_id=1, source_target_pairs={{14,0},{3,1},{0,2},{5,3},{2,4},{7,5},{4,6},{9,7},{6,8},{11,9},{8,1... | collective-permute-start | bytes 1597448 | tf_op jit(solution)/shard_map/ppermute | solution.py:60
  64.0 12.2 %collective-permute-start.12 = (bf16[1040,256]{1,0:T(8,128)(2,1)S(1)}, bf16[1040,256]{1,0:T(8,128)(2,1)S(1)}, u32[]{:S(2)}, u32[]{:S(2)}) collective-permute-start(bf16[1040,256]{1,0:T(8,128)(2,1)S(1)} %collective-permute-done.11.refs_4_), channel_id=1, source_target_pairs={{64,0},{17,1},{66,2},{19,3},{68,4},{21,5},{70,6},{23,7},{72,8},{25... | collective-permute-start | bytes 1597448 | tf_op jit(solution)/shard_map/ppermute | solution.py:60
  74.8 4.9 %copy-start.3 = (bf16[256]{0:T(256)(128)(2,1)S(1)}, bf16[256]{0:T(256)(128)(2,1)}, u32[]{:S(2)}) copy-start(bf16[256]{0:T(256)(128)(2,1)} %param.15) | copy-start | bytes 1540
  74.8 4.9 %copy-start.2 = (f32[4096]{0:T(1024)S(1)}, f32[4096]{0:T(1024)}, u32[]{:S(2)}) copy-start(f32[4096]{0:T(1024)} %param.10) | copy-start | bytes 49156
  74.9 8.1 %copy-start.1 = (bf16[256,256]{1,0:T(8,128)(2,1)S(1)}, bf16[256,256]{1,0:T(8,128)(2,1)}, u32[]{:S(2)}) copy-start(bf16[256,256]{1,0:T(8,128)(2,1)} %weight.1) | copy-start | bytes 393220
  79.8 2.9 %collective-permute-start.17 = (bf16[2048,256]{1,0:T(8,128)(2,1)}, bf16[2048,256]{1,0:T(8,128)(2,1)S(1)}, u32[]{:S(2)}, u32[]{:S(2)}) collective-permute-start(bf16[2048,256]{1,0:T(8,128)(2,1)} %get-tuple-element.18), channel_id=1, source_target_pairs={{0,1},{1,0},{2,3},{3,2},{4,5},{5,4},{6,7},{7,6},{8,9},{9,8},{10,11... | collective-permute-start | bytes 3145736 | tf_op jit(solution)/shard_map/ppermute | solution.py:381

commit v4 on v3

--- a/solution.py
+++ b/solution.py
@@ -60,7 +60,7 @@
     return lax.ppermute(value, ("col", "rep"), pairs)
 
 
-def line_kernel(keep, own, b, c, d, a, swapped, codes, line):
+def line_kernel(keep, own, c, d, b, a, swapped, slots, line):
     cut = 2 * BLOCK
     norms = []
     for k, shard in enumerate((a, b, c, d)):
@@ -86,7 +86,7 @@
     )(keep, *shards, own, slots)
 
 
-def sort_codes(codes, base, slots, count, listed):
+def sort_kernel(codes, base, slots, count, listed):
     def clear(k, carry):
         count[k] = 0
         return carry
@@ -122,8 +122,25 @@
     base[SEGMENTS] = lax.fori_loop(0, SEGMENTS, squeeze, 0)
 
 
-def pack_kernel(codes, own, other, base, slots, packed, count, listed, tile, in_sem):
-    sort_codes(codes, base, slots, count, listed)
+def sort_codes(codes):
+    smem = pl.BlockSpec(memory_space=pltpu.SMEM)
+    return pl.pallas_call(
+        sort_kernel,
+        out_shape=(
+            jax.ShapeDtypeStruct((SEGMENTS + 1,), jnp.int32),
+            jax.ShapeDtypeStruct((PACKED,), jnp.int32),
+        ),
+        in_specs=[smem],
+        out_specs=(smem, smem),
+        scratch_shapes=[
+            pltpu.SMEM((SEGMENTS,), jnp.int32),
+            pltpu.SMEM((SEGMENTS * SEG_SLOTS,), jnp.int32),
+        ],
+        compiler_params=pltpu.CompilerParams(vmem_limit_bytes=2 * MIB),
+    )(codes)
+
+
+def pack_kernel(base, slots, own, other, packed, tile, in_sem):
     total = base[SEGMENTS]
 
     def fetch(g):
@@ -133,11 +150,11 @@
 
             @pl.when(e < BLOCK)
             def _():
-                pltpu.make_async_copy(own.at[e], tile.at[slot, u], in_sem.at[slot, u]).start()
+                pltpu.make_async_copy(own.at[e], tile.at[slot, u], in_sem.at[slot]).start()
 
             @pl.when(e >= BLOCK)
             def _():
-                pltpu.make_async_copy(other.at[e - BLOCK], tile.at[slot, u], in_sem.at[slot, u]).start()
+                pltpu.make_async_copy(other.at[e - BLOCK], tile.at[slot, u], in_sem.at[slot]).start()
 
     def begin(g, carry):
         fetch(g)
@@ -153,8 +170,7 @@
         def _():
             fetch(g + ahead)
 
-        for u in range(UNROLL):
-            pltpu.make_async_copy(own.at[0], tile.at[slot, u], in_sem.at[slot, u]).wait()
+        pltpu.make_async_copy(own.at[pl.ds(0, UNROLL)], tile.at[slot], in_sem.at[slot]).wait()
 
         packed[g] = tile[slot].astype(jnp.float32).astype(jnp.bfloat16)
         return carry
@@ -162,31 +178,22 @@
     lax.fori_loop(0, total, step, 0)
 
 
-def pack_tiles(codes, own, other):
+def pack_tiles(lists, own, other):
     smem = pl.BlockSpec(memory_space=pltpu.SMEM)
     hbm = pl.BlockSpec(memory_space=pltpu.HBM)
     ring = (DEPTH // UNROLL, UNROLL, BLOCK, BLOCK)
     return pl.pallas_call(
         pack_kernel,
-        out_shape=(
-            jax.ShapeDtypeStruct((SEGMENTS + 1,), jnp.int32),
-            jax.ShapeDtypeStruct((PACKED,), jnp.int32),
-            jax.ShapeDtypeStruct((PACKED // UNROLL, UNROLL, BLOCK, BLOCK), jnp.bfloat16),
-        ),
-        in_specs=[smem, hbm, hbm],
-        out_specs=(smem, smem, pl.BlockSpec(memory_space=pltpu.VMEM)),
-        scratch_shapes=[
-            pltpu.SMEM((SEGMENTS,), jnp.int32),
-            pltpu.SMEM((SEGMENTS * SEG_SLOTS,), jnp.int32),
-            pltpu.VMEM(ring, jnp.int32),
-            pltpu.SemaphoreType.DMA(ring[:2]),
-        ],
+        out_shape=jax.ShapeDtypeStruct((PACKED // UNROLL, UNROLL, BLOCK, BLOCK), jnp.bfloat16),
+        in_specs=[smem, smem, hbm, hbm],
+        out_specs=pl.BlockSpec(memory_space=pltpu.VMEM),
+        scratch_shapes=[pltpu.VMEM(ring, jnp.int32), pltpu.SemaphoreType.DMA(ring[:1])],
         compiler_params=pltpu.CompilerParams(vmem_limit_bytes=20 * MIB),
         cost_estimate=pl.CostEstimate(flops=10**6, bytes_accessed=20 * 10**6, transcendentals=0),
-    )(codes, own, other)
-
-
-def join_kernel(odd, a, b, c, d, packed, single, double):
+    )(*lists, own, other)
+
+
+def join_kernel(odd, c, a, b, d, packed, single, double):
     double[pl.ds(0, LINE), :] = b[...]
     double[pl.ds(LINE, LINE), :] = c[...]
 
@@ -207,7 +214,7 @@
         in_specs=[pl.BlockSpec(memory_space=pltpu.SMEM)] + [vmem] * 4 + [pl.BlockSpec(memory_space=pl.ANY)],
         out_specs=(vmem, vmem),
         compiler_params=pltpu.CompilerParams(vmem_limit_bytes=8 * MIB),
-    )(odd, *lines, packed)
+    )(odd, lines[2], lines[0], lines[1], lines[3], packed)
 
 
 def sum_kernel(ids, before, *refs):
@@ -287,7 +294,11 @@
     copies = []
     for i in range(8):
         rows = pl.ds(i * step, step)
-        factor = jnp.concatenate([scale[rows, :]] * 2, axis=1)
+        tiles = [
+            jnp.broadcast_to(scale[pl.ds(i * step // BLOCK + k, 1), :], (BLOCK, BLOCK)).T
+            for k in range(step // BLOCK)
+        ]
+        factor = jnp.concatenate([jnp.concatenate(tiles, axis=0)] * 2, axis=1)
         aggregate = (kept[rows, :] + received[rows, :].astype(jnp.float32)) * factor
         result = jnp.dot(
             aggregate.astype(jnp.bfloat16), weight[...], preferred_element_type=jnp.float32
@@ -344,8 +355,7 @@
 def gather_shards(features, src_norm):
     norm_rows = jnp.broadcast_to(src_norm, (16, WIDTH))
     shard = jnp.concatenate([features, norm_rows], axis=0)
-    near = [move(shard, from_z(step)) for step in (1, 2, 3)]
-    return [shard, *near, move(shard, from_z(0))]
+    return [shard] + [move(shard, from_z(step)) for step in (2, 3, 1, 0)]
 
 
 def body(features, src_norm, dst_norm, src_block, dst_block, counts, weight, out_bias):
@@ -359,11 +369,11 @@
     all_ids = lax.all_gather(ids, "rep")
     both = jnp.concatenate([ids, jnp.where(rep == 0, all_ids[1], all_ids[0])], axis=1)
     place = (z, jnp.where(rep == 0, y, x), jnp.where(rep == 0, x, y), rep)
-    codes = encode(both[0], both[1], place)
+    base, slots = sort_codes(encode(both[0], both[1], place))
     line_0 = make_line(
-        jnp.where(z // 4 == rep, 1, 0).astype(jnp.int32).reshape(1), gather_shards(features, src_norm), other, codes)
+        jnp.where(z // 4 == rep, 1, 0).astype(jnp.int32).reshape(1), gather_shards(features, src_norm), other, slots)
     lines = [line_0] + [move(line_0, from_second(step)) for step in (1, 2, 3)]
-    lists = pack_tiles(codes, own, other)
+    lists = (base, slots, pack_tiles((base, slots), own, other))
     single, double = join_lines((z & 1).astype(jnp.int32).reshape(1), lines, lists[2])
     up = move(single, from_third(1))
     down_12 = move(double, from_third(-1))
@@ -380,7 +390,7 @@
     sent, kept = sum_tiles(lists, {FAR_12: far_12, FAR_Z: far_z, DOWN_Z: down_z}, total, True)
     received = lax.ppermute(sent, "rep", swap)
     own_norm = lax.dynamic_slice_in_dim(dst_norm, rep * HALF, HALF, 0)
-    scale = jnp.broadcast_to(own_norm[:, None], (HALF, BLOCK))
+    scale = own_norm.reshape(HALF // BLOCK, BLOCK)
     return finish(kept, received, scale, weight, out_bias.astype(jnp.float32).reshape(1, -1))
 
 

time: 84.9 us -> 81.8 us (0.963)
  waiting for transfers between devices: 25.3 us -> 19.6 us
  starting transfers between devices: 28.7 us -> 33.7 us
  Pallas kernels: 24.9 us -> 23 us
    ppermute x16, waiting for transfers between devices: 22.4 us -> 17.1 us  [move(): return lax.ppermute(value, ('col', 'rep'), pairs)]
    ppermute x16, starting transfers between devices: 25.5 us -> 28.5 us  [move(): return lax.ppermute(value, ('col', 'rep'), pairs)]
    ppermute x1, starting transfers between devices: 0.01 us -> 2.02 us  [body(): received = lax.ppermute(sent, 'rep', swap)]
    pallas_call x3, Pallas kernels: 10 us -> 8.94 us  [sum_tiles(): pl.pallas_call(functools.partial(sum_kernel, ids, bool(before)), out_shap...]
    pallas_call x1 -> x2, Pallas kernels: 13.4 us -> 12.5 us  [the longest x1 9.26 us: pack_tiles(): pl.pallas_call(pack_kernel, out_shape=jax.ShapeDtypeStruct((PACKED // UNR...]
  transfers between devices with their start and end apart: 18 -> 18, of which waited for: 9 -> 7; matrix products, arithmetic and copies ran while one was open for 4% -> 4% of each run, Pallas kernels for 24% -> 22%
where the time goes in v4:
time: 81.8 us; the launch traced here: 81.5 us
  starting transfers between devices  33.7 us (41%)
  Pallas kernels  23 us (28%)
  waiting for transfers between devices  19.6 us (24%)
  other arithmetic  2.33 us (3%)
  blocking collectives  1.77 us (2%)
    ppermute x16, starting transfers between devices, move(): return lax.ppermute(value, ('col', 'rep'), pairs)  28.5 us
    ppermute x16, waiting for transfers between devices, move(): return lax.ppermute(value, ('col', 'rep'), pairs)  17.1 us
    pallas_call x1, Pallas kernels, pack_tiles(): pl.pallas_call(pack_kernel, out_shape=jax.ShapeDtypeStruct((PACKED // UNR...  9.26 us
    pallas_call x3, Pallas kernels, sum_tiles(): pl.pallas_call(functools.partial(sum_kernel, ids, bool(before)), out_shap...  8.94 us
    pallas_call x1, Pallas kernels, sort_codes(): pl.pallas_call(sort_kernel, out_shape=(jax.ShapeDtypeStruct((SEGMENTS + 1...  3.27 us
    ppermute x1, starting transfers between devices, body(): other = lax.ppermute(own, 'rep', swap)  3.24 us
    ppermute x1, waiting for transfers between devices, body(): received = lax.ppermute(sent, 'rep', swap)  2.47 us
    ppermute x1, starting transfers between devices, body(): received = lax.ppermute(sent, 'rep', swap)  2.02 us
  transfers between devices with their start and end apart: 18, of which 7 were waited for; matrix products, arithmetic and copies ran while one was open for 4% of the time, Pallas kernels for 22%

profile of v4, /device:TPU:1, one launch (start us, length us, event | category | flops | bytes accessed | tf_op | source)
XLA Modules:
  0.0 81.5 jit_solution(4292948782208246796)
XLA Ops:
  0.0 3.2 %collective-permute-start = (s32[128,128,128]{2,1,0:T(8,128)}, s32[128,128,128]{2,1,0:T(8,128)}, u32[]{:S(2)}, u32[]{:S(2)}) collective-permute-start(s32[128,128,128]{2,1,0:T(8,128)} %bitcast.17), channel_id=1, source_target_pairs={{0,1},{1,0},{2,3},{3,2},{4,5},{5,4},{6,7},{7,6},{8,9},{9,8},{10,11... | collective-permute-start | bytes 25165832 | tf_op jit(solution)/shard_map/ppermute | solution.py:367
  3.2 0.7 broadcast_in_dim.34
  3.9 0.9 %pad_maximum_fusion.own = bf16[272,256]{1,0:T(8,128)(2,1)S(1)} fusion(bf16[16,256]{1,0:T(8,128)(2,1)S(1)} %broadcast_in_dim.34, bf16[256,256]{1,0:T(8,128)(2,1)} %param.8), kind=kLoop, calls=%fused_computation | loop fusion | flops 278528 | bytes 278528 | tf_op jit(solution)/shard_map/concatenate | solution.py:357
  4.8 4.3 %collective-permute-start.1 = (bf16[272,256]{1,0:T(8,128)(2,1)S(1)}, bf16[272,256]{1,0:T(8,128)(2,1)S(1)}, u32[]{:S(2)}, u32[]{:S(2)}) collective-permute-start(bf16[272,256]{1,0:T(8,128)(2,1)S(1)} %pad_maximum_fusion.own), channel_id=1, source_target_pairs={{4,0},{12,1},{6,2},{14,3},{0,4},{8,5},{2,6},{10,7},{5,8},{13,9},{7... | collective-permute-start | bytes 417800 | tf_op jit(solution)/shard_map/ppermute | solution.py:60
  9.1 1.1 %collective-permute-start.2 = (bf16[272,256]{1,0:T(8,128)(2,1)S(1)}, bf16[272,256]{1,0:T(8,128)(2,1)S(1)}, u32[]{:S(2)}, u32[]{:S(2)}) collective-permute-start(bf16[272,256]{1,0:T(8,128)(2,1)S(1)} %pad_maximum_fusion.own), channel_id=1, source_target_pairs={{6,0},{14,1},{0,2},{8,3},{2,4},{10,5},{4,6},{12,7},{7,8},{15,9},{1... | collective-permute-start | bytes 417800 | tf_op jit(solution)/shard_map/ppermute | solution.py:60
  10.2 1.9 %collective-permute-start.3 = (bf16[272,256]{1,0:T(8,128)(2,1)S(1)}, bf16[272,256]{1,0:T(8,128)(2,1)S(1)}, u32[]{:S(2)}, u32[]{:S(2)}) collective-permute-start(bf16[272,256]{1,0:T(8,128)(2,1)S(1)} %pad_maximum_fusion.own), channel_id=1, source_target_pairs={{2,0},{10,1},{4,2},{12,3},{6,4},{14,5},{0,6},{8,7},{3,8},{11,9},{5... | collective-permute-start | bytes 417800 | tf_op jit(solution)/shard_map/ppermute | solution.py:60
  12.0 4.2 %collective-permute-start.4 = (bf16[272,256]{1,0:T(8,128)(2,1)S(1)}, bf16[272,256]{1,0:T(8,128)(2,1)S(1)}, u32[]{:S(2)}, u32[]{:S(2)}) collective-permute-start(bf16[272,256]{1,0:T(8,128)(2,1)S(1)} %pad_maximum_fusion.own), channel_id=1, source_target_pairs={{8,1},{10,3},{12,5},{14,7},{1,8},{3,10},{5,12},{7,14},{24,17},{26,... | collective-permute-start | bytes 417800 | tf_op jit(solution)/shard_map/ppermute | solution.py:60
  16.3 0.7 add_bitcast_fusion
  17.0 1.8 %all-gather.1 = s32[2,2,128]{2,1,0:T(2,128)S(1)} all-gather(s32[1,2,128]{2,1,0:T(2,128)S(1)} %add_bitcast_fusion), channel_id=2, replica_groups=mesh['col'=128,'rep'=2] {'rep'}, dimensions={0}, use_global_device_ids=true | all-gather | bytes 3072 | tf_op jit(solution)/shard_map/all_gather | solution.py:369
  18.7 0.7 pad_add_fusion
  19.5 3.3 %shard_map.82 = (s32[17]{0:T(128)S(1)}, s32[304]{0:T(512)S(1)}) custom-call(s32[256]{0:T(256)S(1)} %or_or_fusion.codes), custom_call_target="tpu_custom_call" | custom-call | tf_op jit(solution)/shard_map/pallas_call | solution.py:127
  22.8 0.0 collective-permute-done.1.c
  22.8 0.0 collective-permute-done.2.d
  22.8 0.0 collective-permute-done.3.b
  22.8 1.0 %collective-permute-done.4.a = bf16[272,256]{1,0:T(8,128)(2,1)S(1)} collective-permute-done((bf16[272,256]{1,0:T(8,128)(2,1)S(1)}, bf16[272,256]{1,0:T(8,128)(2,1)S(1)}, u32[]{:S(2)}, u32[]{:S(2)}) %collective-permute-start.4) | collective-permute-done | bytes 139296 | tf_op jit(solution)/shard_map/ppermute | solution.py:60
  23.8 0.0 collective-permute-done.other.swapped
  23.8 2.8 %collective-permute-start.5 = (bf16[1040,256]{1,0:T(8,128)(2,1)S(1)}, bf16[1040,256]{1,0:T(8,128)(2,1)S(1)}, u32[]{:S(2)}, u32[]{:S(2)}) collective-permute-start(bf16[1040,256]{1,0:T(8,128)(2,1)S(1)} %shard_map.84.a.refs_3_), channel_id=1, source_target_pairs={{32,0},{129,1},{34,2},{131,3},{36,4},{133,5},{38,6},{135,7},{40,8}... | collective-permute-start | bytes 1597448 | tf_op jit(solution)/shard_map/ppermute | solution.py:60
  26.7 0.9 %collective-permute-start.6 = (bf16[1040,256]{1,0:T(8,128)(2,1)S(1)}, bf16[1040,256]{1,0:T(8,128)(2,1)S(1)}, u32[]{:S(2)}, u32[]{:S(2)}) collective-permute-start(bf16[1040,256]{1,0:T(8,128)(2,1)S(1)} %shard_map.84.a.refs_3_), channel_id=1, source_target_pairs={{16,0},{65,1},{18,2},{67,3},{20,4},{69,5},{22,6},{71,7},{24,8},{73... | collective-permute-start | bytes 1597448 | tf_op jit(solution)/shard_map/ppermute | solution.py:60
  27.5 0.6 collective-permute-start.7
  28.1 9.3 %shard_map.83.packed.refs_2_ = bf16[76,4,128,128]{3,2,1,0:T(8,128)(2,1)S(1)} custom-call(s32[17]{0:T(128)S(1)} %get-tuple-element.11.base.refs_0_, s32[304]{0:T(512)S(1)} %get-tuple-element.12.slots.refs_1_, s32[128,128,128]{2,1,0:T(8,128)S(1)} %bitcast.18, s32[128,128,128]{2,1,0:T(8,128)} %collective-permute-done.other.swapped), custom_call_target="tpu_custom_call" | custom-call | flops 1000000 | bytes 20000000 | tf_op jit(solution)/shard_map/pallas_call | solution.py:185
  37.4 0.0 collective-permute-done.5.c
  37.4 2.3 %collective-permute-done.6.b = bf16[1040,256]{1,0:T(8,128)(2,1)S(1)} collective-permute-done((bf16[1040,256]{1,0:T(8,128)(2,1)S(1)}, bf16[1040,256]{1,0:T(8,128)(2,1)S(1)}, u32[]{:S(2)}, u32[]{:S(2)}) %collective-permute-start.6) | collective-permute-done | bytes 532512 | tf_op jit(solution)/shard_map/ppermute | solution.py:60
  39.7 0.0 collective-permute-done.7.d.refs_5_
  39.7 0.1 shard_map.85
  39.8 1.1 %collective-permute-start.8 = (bf16[2080,256]{1,0:T(8,128)(2,1)S(1)}, bf16[2080,256]{1,0:T(8,128)(2,1)S(1)}, u32[]{:S(2)}, u32[]{:S(2)}) collective-permute-start(bf16[2080,256]{1,0:T(8,128)(2,1)S(1)} %get-tuple-element.13.refs_4_), channel_id=1, source_target_pairs={{192,0},{49,1},{194,2},{51,3},{196,4},{53,5},{198,6},{55,7},{200,8... | collective-permute-start | bytes 3194888 | tf_op jit(solution)/shard_map/ppermute | solution.py:60
  40.9 1.6 %collective-permute-start.10 = (bf16[1040,256]{1,0:T(8,128)(2,1)S(1)}, bf16[1040,256]{1,0:T(8,128)(2,1)S(1)}, u32[]{:S(2)}, u32[]{:S(2)}) collective-permute-start(bf16[1040,256]{1,0:T(8,128)(2,1)S(1)} %get-tuple-element.14), channel_id=1, source_target_pairs={{64,0},{17,1},{66,2},{19,3},{68,4},{21,5},{70,6},{23,7},{72,8},{25... | collective-permute-start | bytes 1597448 | tf_op jit(solution)/shard_map/ppermute | solution.py:60
  42.6 1.2 %collective-permute-start.15 = (bf16[2080,256]{1,0:T(8,128)(2,1)S(1)}, bf16[2080,256]{1,0:T(8,128)(2,1)S(1)}, u32[]{:S(2)}, u32[]{:S(2)}) collective-permute-start(bf16[2080,256]{1,0:T(8,128)(2,1)S(1)} %get-tuple-element.13.refs_4_), channel_id=1, source_target_pairs={{64,0},{17,1},{66,2},{19,3},{68,4},{21,5},{70,6},{23,7},{72,8},{25... | collective-permute-start | bytes 3194888 | tf_op jit(solution)/shard_map/ppermute | solution.py:60
  43.8 0.2 collective-permute-start.13
  44.0 5.5 %collective-permute-done.10.refs_3_ = bf16[1040,256]{1,0:T(8,128)(2,1)S(1)} collective-permute-done((bf16[1040,256]{1,0:T(8,128)(2,1)S(1)}, bf16[1040,256]{1,0:T(8,128)(2,1)S(1)}, u32[]{:S(2)}, u32[]{:S(2)}) %collective-permute-start.10) | collective-permute-done | bytes 532512 | tf_op jit(solution)/shard_map/ppermute | solution.py:60
  49.5 1.6 %collective-permute-start.11 = (bf16[1040,256]{1,0:T(8,128)(2,1)S(1)}, bf16[1040,256]{1,0:T(8,128)(2,1)S(1)}, u32[]{:S(2)}, u32[]{:S(2)}) collective-permute-start(bf16[1040,256]{1,0:T(8,128)(2,1)S(1)} %collective-permute-done.10.refs_3_), channel_id=1, source_target_pairs={{2,0},{15,1},{4,2},{1,3},{6,4},{3,5},{8,6},{5,7},{10,8},{7,9},{12,... | collective-permute-start | bytes 1597448 | tf_op jit(solution)/shard_map/ppermute | solution.py:60
  51.2 4.0 %collective-permute-done.8.refs_5_ = bf16[2080,256]{1,0:T(8,128)(2,1)S(1)} collective-permute-done((bf16[2080,256]{1,0:T(8,128)(2,1)S(1)}, bf16[2080,256]{1,0:T(8,128)(2,1)S(1)}, u32[]{:S(2)}, u32[]{:S(2)}) %collective-permute-start.8) | collective-permute-done | bytes 1064992 | tf_op jit(solution)/shard_map/ppermute | solution.py:60
  55.2 0.0 collective-permute-start.9
  55.2 2.7 %collective-permute-start.16 = (bf16[1040,256]{1,0:T(8,128)(2,1)S(1)}, bf16[1040,256]{1,0:T(8,128)(2,1)S(1)}, u32[]{:S(2)}, u32[]{:S(2)}) collective-permute-start(bf16[1040,256]{1,0:T(8,128)(2,1)S(1)} %collective-permute-done.10.refs_3_), channel_id=1, source_target_pairs={{64,0},{17,1},{66,2},{19,3},{68,4},{21,5},{70,6},{23,7},{72,8},{25... | collective-permute-start | bytes 1597448 | tf_op jit(solution)/shard_map/ppermute | solution.py:60
  57.9 3.0 %collective-permute-done.13.refs_6_ = bf16[1040,256]{1,0:T(8,128)(2,1)S(1)} collective-permute-done((bf16[1040,256]{1,0:T(8,128)(2,1)S(1)}, bf16[1040,256]{1,0:T(8,128)(2,1)S(1)}, u32[]{:S(2)}, u32[]{:S(2)}) %collective-permute-start.13) | collective-permute-done | bytes 532512 | tf_op jit(solution)/shard_map/ppermute | solution.py:60
  60.9 2.8 %collective-permute-start.14 = (bf16[1040,256]{1,0:T(8,128)(2,1)S(1)}, bf16[1040,256]{1,0:T(8,128)(2,1)S(1)}, u32[]{:S(2)}, u32[]{:S(2)}) collective-permute-start(bf16[1040,256]{1,0:T(8,128)(2,1)S(1)} %collective-permute-done.13.refs_6_), channel_id=1, source_target_pairs={{14,0},{3,1},{0,2},{5,3},{2,4},{7,5},{4,6},{9,7},{6,8},{11,9},{8,1... | collective-permute-start | bytes 1597448 | tf_op jit(solution)/shard_map/ppermute | solution.py:60
  63.7 0.0 collective-permute-done.11.refs_4_
  63.7 1.5 %collective-permute-start.12 = (bf16[1040,256]{1,0:T(8,128)(2,1)S(1)}, bf16[1040,256]{1,0:T(8,128)(2,1)S(1)}, u32[]{:S(2)}, u32[]{:S(2)}) collective-permute-start(bf16[1040,256]{1,0:T(8,128)(2,1)S(1)} %collective-permute-done.11.refs_4_), channel_id=1, source_target_pairs={{64,0},{17,1},{66,2},{19,3},{68,4},{21,5},{70,6},{23,7},{72,8},{25... | collective-permute-start | bytes 1597448 | tf_op jit(solution)/shard_map/ppermute | solution.py:60
  65.2 2.1 %shard_map.86.refs_9_ = f32[4096,256]{1,0:T(8,128)S(1)} custom-call(s32[17]{0:T(128)S(1)} %get-tuple-element.11.base.refs_0_, s32[304]{0:T(512)S(1)} %get-tuple-element.12.slots.refs_1_, bf16[76,4,128,128]{3,2,1,0:T(8,128)(2,1)S(1)} %shard_map.83.packed.refs_2_, bf16[1040,256]{1,0:T(8,128)(2,1)S(1)} %shard_map.84.a.refs_3_, ...), custom_call_target="tpu_custom_call" | custom-call | flops 400000000 | bytes 8000000 | tf_op jit(solution)/shard_map/pallas_call | solution.py:281
  67.3 0.0 collective-permute-done.16.refs_8_
  67.3 0.0 collective-permute-done.15.refs_7_
  67.3 3.7 %shard_map.87.refs_6_ = f32[4096,256]{1,0:T(8,128)S(1)} custom-call(s32[17]{0:T(128)S(1)} %get-tuple-element.11.base.refs_0_, s32[304]{0:T(512)S(1)} %get-tuple-element.12.slots.refs_1_, bf16[76,4,128,128]{3,2,1,0:T(8,128)(2,1)S(1)} %shard_map.83.packed.refs_2_, bf16[1040,256]{1,0:T(8,128)(2,1)S(1)} %collective-permute-done.10.refs_3_, ...), custom_call_target="tpu_custom_call" | custom-call | flops 400000000 | bytes 8000000 | tf_op jit(solution)/shard_map/pallas_call | solution.py:281
  71.0 0.0 copy-start.3
  71.0 0.0 copy-start.2
  71.1 1.3 %collective-permute-done.12.refs_4_ = bf16[1040,256]{1,0:T(8,128)(2,1)S(1)} collective-permute-done((bf16[1040,256]{1,0:T(8,128)(2,1)S(1)}, bf16[1040,256]{1,0:T(8,128)(2,1)S(1)}, u32[]{:S(2)}, u32[]{:S(2)}) %collective-permute-start.12) | collective-permute-done | bytes 532512 | tf_op jit(solution)/shard_map/ppermute | solution.py:60
  72.4 3.1 %shard_map.88 = (bf16[2048,256]{1,0:T(8,128)(2,1)}, f32[2048,256]{1,0:T(8,128)S(1)}) custom-call(s32[17]{0:T(128)S(1)} %get-tuple-element.11.base.refs_0_, s32[304]{0:T(512)S(1)} %get-tuple-element.12.slots.refs_1_, bf16[76,4,128,128]{3,2,1,0:T(8,128)(2,1)S(1)} %shard_map.83.packed.refs_2_, bf16[2080,256]{1,0:T(8,128)(2,1)S(1)} %collective-permute-done.9.refs_3_, ...), custom_call_target="tpu_custom_call" | custom-call | flops 400000000 | bytes 8000000 | tf_op jit(solution)/shard_map/pallas_call | solution.py:281
  75.5 2.0 %collective-permute-start.17 = (bf16[2048,256]{1,0:T(8,128)(2,1)}, bf16[2048,256]{1,0:T(8,128)(2,1)S(1)}, u32[]{:S(2)}, u32[]{:S(2)}) collective-permute-start(bf16[2048,256]{1,0:T(8,128)(2,1)} %get-tuple-element.16), channel_id=1, source_target_pairs={{0,1},{1,0},{2,3},{3,2},{4,5},{5,4},{6,7},{7,6},{8,9},{9,8},{10,11... | collective-permute-start | bytes 3145736 | tf_op jit(solution)/shard_map/ppermute | solution.py:391
  77.5 2.5 %collective-permute-done.17.received = bf16[2048,256]{1,0:T(8,128)(2,1)S(1)} collective-permute-done((bf16[2048,256]{1,0:T(8,128)(2,1)}, bf16[2048,256]{1,0:T(8,128)(2,1)S(1)}, u32[]{:S(2)}, u32[]{:S(2)}) %collective-permute-start.17) | collective-permute-done | bytes 1048608 | tf_op jit(solution)/shard_map/ppermute | solution.py:391
  80.0 1.3 %shard_map.89 = bf16[2048,256]{1,0:T(8,128)(2,1)} custom-call(f32[2048,256]{1,0:T(8,128)S(1)} %get-tuple-element.15.kept, bf16[2048,256]{1,0:T(8,128)(2,1)S(1)} %collective-permute-done.17.received, f32[16,128]{1,0:T(8,128)S(1)} %dynamic-slice_bitcast_fusion.scale, bf16[256,256]{1,0:T(8,128)(2,1)S(1)} %copy-done.2, f32[1,256]{1,0:T(1,128)S(1)} %bitcast.19), custom_call_target="tpu_custom_call" | custom-call | flops 300000000 | bytes 6000000 | tf_op jit(solution)/shard_map/pallas_call | solution.py:315
  (15 shorter events, 0.1 us)
Async XLA Ops:
  0.0 77.5 %copy-start = (f32[4096]{0:T(1024)S(1)}, f32[4096]{0:T(1024)}, u32[]{:S(2)}) copy-start(f32[4096]{0:T(1024)} %param.10) | copy-start | bytes 49156
  0.0 23.8 %collective-permute-start = (s32[128,128,128]{2,1,0:T(8,128)}, s32[128,128,128]{2,1,0:T(8,128)}, u32[]{:S(2)}, u32[]{:S(2)}) collective-permute-start(s32[128,128,128]{2,1,0:T(8,128)} %bitcast.17), channel_id=1, source_target_pairs={{0,1},{1,0},{2,3},{3,2},{4,5},{5,4},{6,7},{7,6},{8,9},{9,8},{10,11... | collective-permute-start | bytes 25165832 | tf_op jit(solution)/shard_map/ppermute | solution.py:367
  4.8 18.0 %collective-permute-start.1 = (bf16[272,256]{1,0:T(8,128)(2,1)S(1)}, bf16[272,256]{1,0:T(8,128)(2,1)S(1)}, u32[]{:S(2)}, u32[]{:S(2)}) collective-permute-start(bf16[272,256]{1,0:T(8,128)(2,1)S(1)} %pad_maximum_fusion.own), channel_id=1, source_target_pairs={{4,0},{12,1},{6,2},{14,3},{0,4},{8,5},{2,6},{10,7},{5,8},{13,9},{7... | collective-permute-start | bytes 417800 | tf_op jit(solution)/shard_map/ppermute | solution.py:60
  9.1 13.7 %collective-permute-start.2 = (bf16[272,256]{1,0:T(8,128)(2,1)S(1)}, bf16[272,256]{1,0:T(8,128)(2,1)S(1)}, u32[]{:S(2)}, u32[]{:S(2)}) collective-permute-start(bf16[272,256]{1,0:T(8,128)(2,1)S(1)} %pad_maximum_fusion.own), channel_id=1, source_target_pairs={{6,0},{14,1},{0,2},{8,3},{2,4},{10,5},{4,6},{12,7},{7,8},{15,9},{1... | collective-permute-start | bytes 417800 | tf_op jit(solution)/shard_map/ppermute | solution.py:60
  10.2 12.6 %collective-permute-start.3 = (bf16[272,256]{1,0:T(8,128)(2,1)S(1)}, bf16[272,256]{1,0:T(8,128)(2,1)S(1)}, u32[]{:S(2)}, u32[]{:S(2)}) collective-permute-start(bf16[272,256]{1,0:T(8,128)(2,1)S(1)} %pad_maximum_fusion.own), channel_id=1, source_target_pairs={{2,0},{10,1},{4,2},{12,3},{6,4},{14,5},{0,6},{8,7},{3,8},{11,9},{5... | collective-permute-start | bytes 417800 | tf_op jit(solution)/shard_map/ppermute | solution.py:60
  12.0 11.7 %collective-permute-start.4 = (bf16[272,256]{1,0:T(8,128)(2,1)S(1)}, bf16[272,256]{1,0:T(8,128)(2,1)S(1)}, u32[]{:S(2)}, u32[]{:S(2)}) collective-permute-start(bf16[272,256]{1,0:T(8,128)(2,1)S(1)} %pad_maximum_fusion.own), channel_id=1, source_target_pairs={{8,1},{10,3},{12,5},{14,7},{1,8},{3,10},{5,12},{7,14},{24,17},{26,... | collective-permute-start | bytes 417800 | tf_op jit(solution)/shard_map/ppermute | solution.py:60
  23.8 4.4 %copy-start.1 = (s32[1,1,128,128,128]{4,3,2,1,0:T(8,128)S(1)}, s32[1,1,128,128,128]{4,3,2,1,0:T(8,128)}, u32[]{:S(2)}) copy-start(s32[1,1,128,128,128]{4,3,2,1,0:T(8,128)} %param.13) | copy-start | bytes 25165828
  23.8 13.6 %collective-permute-start.5 = (bf16[1040,256]{1,0:T(8,128)(2,1)S(1)}, bf16[1040,256]{1,0:T(8,128)(2,1)S(1)}, u32[]{:S(2)}, u32[]{:S(2)}) collective-permute-start(bf16[1040,256]{1,0:T(8,128)(2,1)S(1)} %shard_map.84.a.refs_3_), channel_id=1, source_target_pairs={{32,0},{129,1},{34,2},{131,3},{36,4},{133,5},{38,6},{135,7},{40,8}... | collective-permute-start | bytes 1597448 | tf_op jit(solution)/shard_map/ppermute | solution.py:60
  26.7 13.0 %collective-permute-start.6 = (bf16[1040,256]{1,0:T(8,128)(2,1)S(1)}, bf16[1040,256]{1,0:T(8,128)(2,1)S(1)}, u32[]{:S(2)}, u32[]{:S(2)}) collective-permute-start(bf16[1040,256]{1,0:T(8,128)(2,1)S(1)} %shard_map.84.a.refs_3_), channel_id=1, source_target_pairs={{16,0},{65,1},{18,2},{67,3},{20,4},{69,5},{22,6},{71,7},{24,8},{73... | collective-permute-start | bytes 1597448 | tf_op jit(solution)/shard_map/ppermute | solution.py:60
  27.5 12.2 %collective-permute-start.7 = (bf16[1040,256]{1,0:T(8,128)(2,1)S(1)}, bf16[1040,256]{1,0:T(8,128)(2,1)S(1)}, u32[]{:S(2)}, u32[]{:S(2)}) collective-permute-start(bf16[1040,256]{1,0:T(8,128)(2,1)S(1)} %shard_map.84.a.refs_3_), channel_id=1, source_target_pairs={{48,0},{193,1},{50,2},{195,3},{52,4},{197,5},{54,6},{199,7},{56,8}... | collective-permute-start | bytes 1597448 | tf_op jit(solution)/shard_map/ppermute | solution.py:60
  39.8 15.4 %collective-permute-start.8 = (bf16[2080,256]{1,0:T(8,128)(2,1)S(1)}, bf16[2080,256]{1,0:T(8,128)(2,1)S(1)}, u32[]{:S(2)}, u32[]{:S(2)}) collective-permute-start(bf16[2080,256]{1,0:T(8,128)(2,1)S(1)} %get-tuple-element.13.refs_4_), channel_id=1, source_target_pairs={{192,0},{49,1},{194,2},{51,3},{196,4},{53,5},{198,6},{55,7},{200,8... | collective-permute-start | bytes 3194888 | tf_op jit(solution)/shard_map/ppermute | solution.py:60
  40.9 8.6 %collective-permute-start.10 = (bf16[1040,256]{1,0:T(8,128)(2,1)S(1)}, bf16[1040,256]{1,0:T(8,128)(2,1)S(1)}, u32[]{:S(2)}, u32[]{:S(2)}) collective-permute-start(bf16[1040,256]{1,0:T(8,128)(2,1)S(1)} %get-tuple-element.14), channel_id=1, source_target_pairs={{64,0},{17,1},{66,2},{19,3},{68,4},{21,5},{70,6},{23,7},{72,8},{25... | collective-permute-start | bytes 1597448 | tf_op jit(solution)/shard_map/ppermute | solution.py:60
  42.6 24.7 %collective-permute-start.15 = (bf16[2080,256]{1,0:T(8,128)(2,1)S(1)}, bf16[2080,256]{1,0:T(8,128)(2,1)S(1)}, u32[]{:S(2)}, u32[]{:S(2)}) collective-permute-start(bf16[2080,256]{1,0:T(8,128)(2,1)S(1)} %get-tuple-element.13.refs_4_), channel_id=1, source_target_pairs={{64,0},{17,1},{66,2},{19,3},{68,4},{21,5},{70,6},{23,7},{72,8},{25... | collective-permute-start | bytes 3194888 | tf_op jit(solution)/shard_map/ppermute | solution.py:60
  43.8 17.1 %collective-permute-start.13 = (bf16[1040,256]{1,0:T(8,128)(2,1)S(1)}, bf16[1040,256]{1,0:T(8,128)(2,1)S(1)}, u32[]{:S(2)}, u32[]{:S(2)}) collective-permute-start(bf16[1040,256]{1,0:T(8,128)(2,1)S(1)} %get-tuple-element.14), channel_id=1, source_target_pairs={{192,0},{49,1},{194,2},{51,3},{196,4},{53,5},{198,6},{55,7},{200,8... | collective-permute-start | bytes 1597448 | tf_op jit(solution)/shard_map/ppermute | solution.py:60
  49.5 14.2 %collective-permute-start.11 = (bf16[1040,256]{1,0:T(8,128)(2,1)S(1)}, bf16[1040,256]{1,0:T(8,128)(2,1)S(1)}, u32[]{:S(2)}, u32[]{:S(2)}) collective-permute-start(bf16[1040,256]{1,0:T(8,128)(2,1)S(1)} %collective-permute-done.10.refs_3_), channel_id=1, source_target_pairs={{2,0},{15,1},{4,2},{1,3},{6,4},{3,5},{8,6},{5,7},{10,8},{7,9},{12,... | collective-permute-start | bytes 1597448 | tf_op jit(solution)/shard_map/ppermute | solution.py:60
  55.2 17.1 %collective-permute-start.9 = (bf16[2080,256]{1,0:T(8,128)(2,1)S(1)}, bf16[2080,256]{1,0:T(8,128)(2,1)S(1)}, u32[]{:S(2)}, u32[]{:S(2)}) collective-permute-start(bf16[2080,256]{1,0:T(8,128)(2,1)S(1)} %collective-permute-done.8.refs_5_), channel_id=1, source_target_pairs={{192,0},{49,1},{194,2},{51,3},{196,4},{53,5},{198,6},{55,7},{200,8... | collective-permute-start | bytes 3194888 | tf_op jit(solution)/shard_map/ppermute | solution.py:60
  55.2 12.0 %collective-permute-start.16 = (bf16[1040,256]{1,0:T(8,128)(2,1)S(1)}, bf16[1040,256]{1,0:T(8,128)(2,1)S(1)}, u32[]{:S(2)}, u32[]{:S(2)}) collective-permute-start(bf16[1040,256]{1,0:T(8,128)(2,1)S(1)} %collective-permute-done.10.refs_3_), channel_id=1, source_target_pairs={{64,0},{17,1},{66,2},{19,3},{68,4},{21,5},{70,6},{23,7},{72,8},{25... | collective-permute-start | bytes 1597448 | tf_op jit(solution)/shard_map/ppermute | solution.py:60
  60.9 10.1 %collective-permute-start.14 = (bf16[1040,256]{1,0:T(8,128)(2,1)S(1)}, bf16[1040,256]{1,0:T(8,128)(2,1)S(1)}, u32[]{:S(2)}, u32[]{:S(2)}) collective-permute-start(bf16[1040,256]{1,0:T(8,128)(2,1)S(1)} %collective-permute-done.13.refs_6_), channel_id=1, source_target_pairs={{14,0},{3,1},{0,2},{5,3},{2,4},{7,5},{4,6},{9,7},{6,8},{11,9},{8,1... | collective-permute-start | bytes 1597448 | tf_op jit(solution)/shard_map/ppermute | solution.py:60
  63.7 8.6 %collective-permute-start.12 = (bf16[1040,256]{1,0:T(8,128)(2,1)S(1)}, bf16[1040,256]{1,0:T(8,128)(2,1)S(1)}, u32[]{:S(2)}, u32[]{:S(2)}) collective-permute-start(bf16[1040,256]{1,0:T(8,128)(2,1)S(1)} %collective-permute-done.11.refs_4_), channel_id=1, source_target_pairs={{64,0},{17,1},{66,2},{19,3},{68,4},{21,5},{70,6},{23,7},{72,8},{25... | collective-permute-start | bytes 1597448 | tf_op jit(solution)/shard_map/ppermute | solution.py:60
  71.0 6.5 %copy-start.3 = (bf16[256]{0:T(256)(128)(2,1)S(1)}, bf16[256]{0:T(256)(128)(2,1)}, u32[]{:S(2)}) copy-start(bf16[256]{0:T(256)(128)(2,1)} %param.15) | copy-start | bytes 1540
  71.0 9.0 %copy-start.2 = (bf16[256,256]{1,0:T(8,128)(2,1)S(1)}, bf16[256,256]{1,0:T(8,128)(2,1)}, u32[]{:S(2)}) copy-start(bf16[256,256]{1,0:T(8,128)(2,1)} %weight.1) | copy-start | bytes 393220
  75.5 4.5 %collective-permute-start.17 = (bf16[2048,256]{1,0:T(8,128)(2,1)}, bf16[2048,256]{1,0:T(8,128)(2,1)S(1)}, u32[]{:S(2)}, u32[]{:S(2)}) collective-permute-start(bf16[2048,256]{1,0:T(8,128)(2,1)} %get-tuple-element.16), channel_id=1, source_target_pairs={{0,1},{1,0},{2,3},{3,2},{4,5},{5,4},{6,7},{7,6},{8,9},{9,8},{10,11... | collective-permute-start | bytes 3145736 | tf_op jit(solution)/shard_map/ppermute | solution.py:391

commit v5 on v4

--- a/solution.py
+++ b/solution.py
@@ -217,36 +217,41 @@
     )(odd, lines[2], lines[0], lines[1], lines[3], packed)
 
 
-def sum_kernel(ids, before, *refs):
+def sum_kernel(ids, before, last, *refs):
     base, slots, packed = refs[:3]
     pieces = refs[3 : 3 + len(ids)]
     refs = refs[3 + len(ids) :]
     if before:
         earlier, refs = refs[0], refs[1:]
-    if len(refs) > 2:
-        sent, kept, norm, total = refs
+    if last:
+        sent, kept, norm, low = refs
+        low[...] = earlier[pl.ds(0, HALF), :]
+        kept[...] = earlier[pl.ds(HALF, HALF), :]
+        parts = [(i, k, low, 0) for i, k in enumerate(ids)]
+        parts += [(i, UPPER[k], kept, HALF) for i, k in enumerate(ids)]
     else:
         total, norm = refs
-    if before:
-        total[...] = earlier[...]
-    else:
-        total[...] = jnp.zeros_like(total)
+        if before:
+            total[...] = earlier[...]
+        else:
+            total[...] = jnp.zeros_like(total)
+        parts = [(i, k, total, 0) for i, k in enumerate(ids)]
     for i, piece in enumerate(pieces):
         for line in range(piece.shape[0] // LINE):
             for half in range(2):
                 rows = piece[pl.ds(line * LINE + 8 * BLOCK, 16), pl.ds(half * BLOCK, BLOCK)]
                 norm[pl.ds(32 * i + 16 * half + 8 * line, 8), :] = rows.astype(jnp.float32)[:8]
-    for i, (k, piece) in enumerate(zip(ids, pieces)):
-        first, last = base[k], base[k + 1]
-
-        def add(g, groups, i=i, piece=piece):
+    for i, k, total, first_row in parts:
+        first, end = base[k], base[k + 1]
+
+        def add(g, groups, i=i, piece=pieces[i], total=total, first_row=first_row):
             found = []
             for u in range(UNROLL * groups):
                 code = slots[UNROLL * g + u]
                 scale = norm[pl.ds(32 * i + ((code >> 21) & 31), 1), :]
                 row = pl.multiple_of(((code >> 13) & 255) * 16, 16)
                 found.append((
-                    pl.multiple_of(((code >> 8) & 31) * BLOCK, BLOCK),
+                    pl.multiple_of(jnp.maximum(((code >> 8) & 31) * BLOCK - first_row, 0), BLOCK),
                     jnp.dot(
                         packed[g + u // UNROLL, u % UNROLL] * scale.astype(jnp.bfloat16),
                         piece[pl.ds(row, BLOCK), :], preferred_element_type=jnp.float32,
@@ -259,15 +264,14 @@
             add(first + 2 * j, 2)
             return carry
 
-        lax.fori_loop(0, (last - first) >> 1, pair, 0)
-
-        @pl.when(((last - first) & 1) == 1)
-        def _(last=last, add=add):
-            add(last - 1, 1)
-
-    if len(refs) > 2:
-        sent[...] = total[pl.ds(0, HALF), :].astype(sent.dtype)
-        kept[...] = total[pl.ds(HALF, HALF), :]
+        lax.fori_loop(0, (end - first) >> 1, pair, 0)
+
+        @pl.when(((end - first) & 1) == 1)
+        def _(end=end, add=add):
+            add(end - 1, 1)
+
+    if last:
+        sent[...] = low[...].astype(sent.dtype)
 
 
 def sum_tiles(lists, pieces, earlier=None, last=False):
@@ -279,11 +283,11 @@
     ends = tuple(jax.ShapeDtypeStruct((HALF, WIDTH), t) for t in (jnp.bfloat16, jnp.float32))
     norm = pltpu.VMEM((32 * len(ids), BLOCK), jnp.float32)
     return pl.pallas_call(
-        functools.partial(sum_kernel, ids, bool(before)),
+        functools.partial(sum_kernel, ids, bool(before), last),
         out_shape=ends if last else whole,
         in_specs=[smem] * 2 + [vmem] * (1 + len(ids) + len(before)),
         out_specs=(vmem, vmem) if last else vmem,
-        scratch_shapes=[norm] + ([pltpu.VMEM(whole.shape, whole.dtype)] if last else []),
+        scratch_shapes=[norm] + ([pltpu.VMEM((HALF, WIDTH), jnp.float32)] if last else []),
         compiler_params=pltpu.CompilerParams(vmem_limit_bytes=8 * MIB),
         cost_estimate=pl.CostEstimate(flops=4 * 10**8, bytes_accessed=8 * 10**6, transcendentals=0),
     )(*lists, *pieces.values(), *before)
@@ -327,6 +331,7 @@
 UP, UP_12, UP_Z = 4, 5, 6
 FAR, FAR_12, FAR_Z = 8, 9, 10
 DOWN, DOWN_12, DOWN_Z = 12, 13, 14
+UPPER = {FAR_12: 3, FAR_Z: 7, DOWN_Z: 11}
 
 
 def encode(src, dst, place):
@@ -342,6 +347,9 @@
     own_kind = jnp.where(double, 1, jnp.where(da == 0, 0, 2))
     far_kind = jnp.where(double, 1, jnp.where(beside, 2, 0))
     segment = db * 4 + jnp.where(db == 0, own_kind, far_kind)
+    d = (dst + 16 * (1 - rep)) & 31
+    for low, high in UPPER.items():
+        segment = jnp.where((segment == low) & (d >= 16), high, segment)
     line = jnp.where(da == 2, 1, 0)
     z_of = jnp.where(beside, jnp.where((rep == 0) == (db != 3), z + 1, z - 1), z)
     shard = (pz - z_of) & 3

time: 81.8 us -> 82.8 us (1.012)
  Pallas kernels: 23 us -> 24.6 us
  waiting for transfers between devices: 19.6 us -> 18.4 us
    ppermute x16, waiting for transfers between devices: 17.1 us -> 15.9 us  [move(): return lax.ppermute(value, ('col', 'rep'), pairs)]
    pallas_call x1, Pallas kernels: 9.26 us -> 10.2 us  [pack_tiles(): pl.pallas_call(pack_kernel, out_shape=jax.ShapeDtypeStruct((PACKED // UNR...]
  transfers between devices with their start and end apart: 18 -> 18, of which waited for: 7 -> 8; matrix products, arithmetic and copies ran while one was open for 4% -> 4% of each run, Pallas kernels for 22% -> 23%
where the time goes in v5:
time: 82.8 us; the launch traced here: 82.7 us
  starting transfers between devices  34.4 us (42%)
  Pallas kernels  24.6 us (30%)
  waiting for transfers between devices  18.4 us (22%)
  other arithmetic  2.38 us (3%)
  blocking collectives  1.77 us (2%)
    ppermute x16, starting transfers between devices, move(): return lax.ppermute(value, ('col', 'rep'), pairs)  28.7 us
    ppermute x16, waiting for transfers between devices, move(): return lax.ppermute(value, ('col', 'rep'), pairs)  15.9 us
    pallas_call x1, Pallas kernels, pack_tiles(): pl.pallas_call(pack_kernel, out_shape=jax.ShapeDtypeStruct((PACKED // UNR...  10.2 us
    pallas_call x3, Pallas kernels, sum_tiles(): pl.pallas_call(functools.partial(sum_kernel, ids, bool(before), last), ou...  9.6 us
    pallas_call x1, Pallas kernels, sort_codes(): pl.pallas_call(sort_kernel, out_shape=(jax.ShapeDtypeStruct((SEGMENTS + 1...  3.27 us
    ppermute x1, starting transfers between devices, body(): other = lax.ppermute(own, 'rep', swap)  3.24 us
    ppermute x1, starting transfers between devices, body(): received = lax.ppermute(sent, 'rep', swap)  2.53 us
    ppermute x1, waiting for transfers between devices, body(): received = lax.ppermute(sent, 'rep', swap)  2.47 us
  transfers between devices with their start and end apart: 18, of which 8 were waited for; matrix products, arithmetic and copies ran while one was open for 4% of the time, Pallas kernels for 23%

profile of v5, /device:TPU:1, one launch (start us, length us, event | category | flops | bytes accessed | tf_op | source)
XLA Modules:
  0.0 82.7 jit_solution(12131760000108926920)
XLA Ops:
  0.0 3.2 %collective-permute-start = (s32[128,128,128]{2,1,0:T(8,128)}, s32[128,128,128]{2,1,0:T(8,128)}, u32[]{:S(2)}, u32[]{:S(2)}) collective-permute-start(s32[128,128,128]{2,1,0:T(8,128)} %bitcast.17), channel_id=1, source_target_pairs={{0,1},{1,0},{2,3},{3,2},{4,5},{5,4},{6,7},{7,6},{8,9},{9,8},{10,11... | collective-permute-start | bytes 25165832 | tf_op jit(solution)/shard_map/ppermute | solution.py:375
  3.2 0.7 broadcast_in_dim.41
  3.9 0.9 %pad_maximum_fusion.own = bf16[272,256]{1,0:T(8,128)(2,1)S(1)} fusion(bf16[16,256]{1,0:T(8,128)(2,1)S(1)} %broadcast_in_dim.41, bf16[256,256]{1,0:T(8,128)(2,1)} %param.8), kind=kLoop, calls=%fused_computation | loop fusion | flops 278528 | bytes 278528 | tf_op jit(solution)/shard_map/concatenate | solution.py:365
  4.8 4.3 %collective-permute-start.1 = (bf16[272,256]{1,0:T(8,128)(2,1)S(1)}, bf16[272,256]{1,0:T(8,128)(2,1)S(1)}, u32[]{:S(2)}, u32[]{:S(2)}) collective-permute-start(bf16[272,256]{1,0:T(8,128)(2,1)S(1)} %pad_maximum_fusion.own), channel_id=1, source_target_pairs={{4,0},{12,1},{6,2},{14,3},{0,4},{8,5},{2,6},{10,7},{5,8},{13,9},{7... | collective-permute-start | bytes 417800 | tf_op jit(solution)/shard_map/ppermute | solution.py:60
  9.1 1.1 %collective-permute-start.2 = (bf16[272,256]{1,0:T(8,128)(2,1)S(1)}, bf16[272,256]{1,0:T(8,128)(2,1)S(1)}, u32[]{:S(2)}, u32[]{:S(2)}) collective-permute-start(bf16[272,256]{1,0:T(8,128)(2,1)S(1)} %pad_maximum_fusion.own), channel_id=1, source_target_pairs={{6,0},{14,1},{0,2},{8,3},{2,4},{10,5},{4,6},{12,7},{7,8},{15,9},{1... | collective-permute-start | bytes 417800 | tf_op jit(solution)/shard_map/ppermute | solution.py:60
  10.2 1.9 %collective-permute-start.3 = (bf16[272,256]{1,0:T(8,128)(2,1)S(1)}, bf16[272,256]{1,0:T(8,128)(2,1)S(1)}, u32[]{:S(2)}, u32[]{:S(2)}) collective-permute-start(bf16[272,256]{1,0:T(8,128)(2,1)S(1)} %pad_maximum_fusion.own), channel_id=1, source_target_pairs={{2,0},{10,1},{4,2},{12,3},{6,4},{14,5},{0,6},{8,7},{3,8},{11,9},{5... | collective-permute-start | bytes 417800 | tf_op jit(solution)/shard_map/ppermute | solution.py:60
  12.0 4.2 %collective-permute-start.4 = (bf16[272,256]{1,0:T(8,128)(2,1)S(1)}, bf16[272,256]{1,0:T(8,128)(2,1)S(1)}, u32[]{:S(2)}, u32[]{:S(2)}) collective-permute-start(bf16[272,256]{1,0:T(8,128)(2,1)S(1)} %pad_maximum_fusion.own), channel_id=1, source_target_pairs={{8,1},{10,3},{12,5},{14,7},{1,8},{3,10},{5,12},{7,14},{24,17},{26,... | collective-permute-start | bytes 417800 | tf_op jit(solution)/shard_map/ppermute | solution.py:60
  16.3 0.7 add_bitcast_fusion
  17.0 1.8 %all-gather.1 = s32[2,2,128]{2,1,0:T(2,128)S(1)} all-gather(s32[1,2,128]{2,1,0:T(2,128)S(1)} %add_bitcast_fusion), channel_id=2, replica_groups=mesh['col'=128,'rep'=2] {'rep'}, dimensions={0}, use_global_device_ids=true | all-gather | bytes 3072 | tf_op jit(solution)/shard_map/all_gather | solution.py:377
  18.7 0.7 pad_add_fusion
  19.5 3.3 %shard_map.82 = (s32[17]{0:T(128)S(1)}, s32[304]{0:T(512)S(1)}) custom-call(s32[256]{0:T(256)S(1)} %or_or_fusion.codes), custom_call_target="tpu_custom_call" | custom-call | tf_op jit(solution)/shard_map/pallas_call | solution.py:127
  22.8 0.0 collective-permute-done.1.c
  22.8 0.0 collective-permute-done.2.d
  22.9 0.0 collective-permute-done.3.b
  22.9 0.9 %collective-permute-done.4.a = bf16[272,256]{1,0:T(8,128)(2,1)S(1)} collective-permute-done((bf16[272,256]{1,0:T(8,128)(2,1)S(1)}, bf16[272,256]{1,0:T(8,128)(2,1)S(1)}, u32[]{:S(2)}, u32[]{:S(2)}) %collective-permute-start.4) | collective-permute-done | bytes 139296 | tf_op jit(solution)/shard_map/ppermute | solution.py:60
  23.8 0.0 collective-permute-done.other.swapped
  23.8 2.8 %collective-permute-start.5 = (bf16[1040,256]{1,0:T(8,128)(2,1)S(1)}, bf16[1040,256]{1,0:T(8,128)(2,1)S(1)}, u32[]{:S(2)}, u32[]{:S(2)}) collective-permute-start(bf16[1040,256]{1,0:T(8,128)(2,1)S(1)} %shard_map.84.a.refs_3_), channel_id=1, source_target_pairs={{32,0},{129,1},{34,2},{131,3},{36,4},{133,5},{38,6},{135,7},{40,8}... | collective-permute-start | bytes 1597448 | tf_op jit(solution)/shard_map/ppermute | solution.py:60
  26.7 0.9 %collective-permute-start.6 = (bf16[1040,256]{1,0:T(8,128)(2,1)S(1)}, bf16[1040,256]{1,0:T(8,128)(2,1)S(1)}, u32[]{:S(2)}, u32[]{:S(2)}) collective-permute-start(bf16[1040,256]{1,0:T(8,128)(2,1)S(1)} %shard_map.84.a.refs_3_), channel_id=1, source_target_pairs={{16,0},{65,1},{18,2},{67,3},{20,4},{69,5},{22,6},{71,7},{24,8},{73... | collective-permute-start | bytes 1597448 | tf_op jit(solution)/shard_map/ppermute | solution.py:60
  27.5 0.6 collective-permute-start.7
  28.1 10.2 %shard_map.83.packed.refs_2_ = bf16[76,4,128,128]{3,2,1,0:T(8,128)(2,1)S(1)} custom-call(s32[17]{0:T(128)S(1)} %get-tuple-element.11.base.refs_0_, s32[304]{0:T(512)S(1)} %get-tuple-element.12.slots.refs_1_, s32[128,128,128]{2,1,0:T(8,128)S(1)} %bitcast.18, s32[128,128,128]{2,1,0:T(8,128)} %collective-permute-done.other.swapped), custom_call_target="tpu_custom_call" | custom-call | flops 1000000 | bytes 20000000 | tf_op jit(solution)/shard_map/pallas_call | solution.py:185
  38.4 0.0 collective-permute-done.5.c
  38.4 1.3 %collective-permute-done.6.b = bf16[1040,256]{1,0:T(8,128)(2,1)S(1)} collective-permute-done((bf16[1040,256]{1,0:T(8,128)(2,1)S(1)}, bf16[1040,256]{1,0:T(8,128)(2,1)S(1)}, u32[]{:S(2)}, u32[]{:S(2)}) %collective-permute-start.6) | collective-permute-done | bytes 532512 | tf_op jit(solution)/shard_map/ppermute | solution.py:60
  39.7 0.0 collective-permute-done.7.d.refs_5_
  39.7 0.1 shard_map.85
  39.8 1.2 %collective-permute-start.8 = (bf16[2080,256]{1,0:T(8,128)(2,1)S(1)}, bf16[2080,256]{1,0:T(8,128)(2,1)S(1)}, u32[]{:S(2)}, u32[]{:S(2)}) collective-permute-start(bf16[2080,256]{1,0:T(8,128)(2,1)S(1)} %get-tuple-element.13.refs_4_), channel_id=1, source_target_pairs={{192,0},{49,1},{194,2},{51,3},{196,4},{53,5},{198,6},{55,7},{200,8... | collective-permute-start | bytes 3194888 | tf_op jit(solution)/shard_map/ppermute | solution.py:60
  41.0 1.5 %collective-permute-start.10 = (bf16[1040,256]{1,0:T(8,128)(2,1)S(1)}, bf16[1040,256]{1,0:T(8,128)(2,1)S(1)}, u32[]{:S(2)}, u32[]{:S(2)}) collective-permute-start(bf16[1040,256]{1,0:T(8,128)(2,1)S(1)} %get-tuple-element.14), channel_id=1, source_target_pairs={{64,0},{17,1},{66,2},{19,3},{68,4},{21,5},{70,6},{23,7},{72,8},{25... | collective-permute-start | bytes 1597448 | tf_op jit(solution)/shard_map/ppermute | solution.py:60
  42.6 1.2 %collective-permute-start.15 = (bf16[2080,256]{1,0:T(8,128)(2,1)S(1)}, bf16[2080,256]{1,0:T(8,128)(2,1)S(1)}, u32[]{:S(2)}, u32[]{:S(2)}) collective-permute-start(bf16[2080,256]{1,0:T(8,128)(2,1)S(1)} %get-tuple-element.13.refs_4_), channel_id=1, source_target_pairs={{64,0},{17,1},{66,2},{19,3},{68,4},{21,5},{70,6},{23,7},{72,8},{25... | collective-permute-start | bytes 3194888 | tf_op jit(solution)/shard_map/ppermute | solution.py:60
  43.8 0.2 collective-permute-start.13
  44.0 5.4 %collective-permute-done.10.refs_3_ = bf16[1040,256]{1,0:T(8,128)(2,1)S(1)} collective-permute-done((bf16[1040,256]{1,0:T(8,128)(2,1)S(1)}, bf16[1040,256]{1,0:T(8,128)(2,1)S(1)}, u32[]{:S(2)}, u32[]{:S(2)}) %collective-permute-start.10) | collective-permute-done | bytes 532512 | tf_op jit(solution)/shard_map/ppermute | solution.py:60
  49.4 1.8 %collective-permute-start.11 = (bf16[1040,256]{1,0:T(8,128)(2,1)S(1)}, bf16[1040,256]{1,0:T(8,128)(2,1)S(1)}, u32[]{:S(2)}, u32[]{:S(2)}) collective-permute-start(bf16[1040,256]{1,0:T(8,128)(2,1)S(1)} %collective-permute-done.10.refs_3_), channel_id=1, source_target_pairs={{2,0},{15,1},{4,2},{1,3},{6,4},{3,5},{8,6},{5,7},{10,8},{7,9},{12,... | collective-permute-start | bytes 1597448 | tf_op jit(solution)/shard_map/ppermute | solution.py:60
  51.3 4.0 %collective-permute-done.8.refs_5_ = bf16[2080,256]{1,0:T(8,128)(2,1)S(1)} collective-permute-done((bf16[2080,256]{1,0:T(8,128)(2,1)S(1)}, bf16[2080,256]{1,0:T(8,128)(2,1)S(1)}, u32[]{:S(2)}, u32[]{:S(2)}) %collective-permute-start.8) | collective-permute-done | bytes 1064992 | tf_op jit(solution)/shard_map/ppermute | solution.py:60
  55.2 0.0 collective-permute-start.9
  55.2 2.7 %collective-permute-start.16 = (bf16[1040,256]{1,0:T(8,128)(2,1)S(1)}, bf16[1040,256]{1,0:T(8,128)(2,1)S(1)}, u32[]{:S(2)}, u32[]{:S(2)}) collective-permute-start(bf16[1040,256]{1,0:T(8,128)(2,1)S(1)} %collective-permute-done.10.refs_3_), channel_id=1, source_target_pairs={{64,0},{17,1},{66,2},{19,3},{68,4},{21,5},{70,6},{23,7},{72,8},{25... | collective-permute-start | bytes 1597448 | tf_op jit(solution)/shard_map/ppermute | solution.py:60
  57.9 3.0 %collective-permute-done.13.refs_6_ = bf16[1040,256]{1,0:T(8,128)(2,1)S(1)} collective-permute-done((bf16[1040,256]{1,0:T(8,128)(2,1)S(1)}, bf16[1040,256]{1,0:T(8,128)(2,1)S(1)}, u32[]{:S(2)}, u32[]{:S(2)}) %collective-permute-start.13) | collective-permute-done | bytes 532512 | tf_op jit(solution)/shard_map/ppermute | solution.py:60
  60.9 2.8 %collective-permute-start.14 = (bf16[1040,256]{1,0:T(8,128)(2,1)S(1)}, bf16[1040,256]{1,0:T(8,128)(2,1)S(1)}, u32[]{:S(2)}, u32[]{:S(2)}) collective-permute-start(bf16[1040,256]{1,0:T(8,128)(2,1)S(1)} %collective-permute-done.13.refs_6_), channel_id=1, source_target_pairs={{14,0},{3,1},{0,2},{5,3},{2,4},{7,5},{4,6},{9,7},{6,8},{11,9},{8,1... | collective-permute-start | bytes 1597448 | tf_op jit(solution)/shard_map/ppermute | solution.py:60
  63.7 0.0 collective-permute-done.11.refs_4_
  63.7 1.5 %collective-permute-start.12 = (bf16[1040,256]{1,0:T(8,128)(2,1)S(1)}, bf16[1040,256]{1,0:T(8,128)(2,1)S(1)}, u32[]{:S(2)}, u32[]{:S(2)}) collective-permute-start(bf16[1040,256]{1,0:T(8,128)(2,1)S(1)} %collective-permute-done.11.refs_4_), channel_id=1, source_target_pairs={{64,0},{17,1},{66,2},{19,3},{68,4},{21,5},{70,6},{23,7},{72,8},{25... | collective-permute-start | bytes 1597448 | tf_op jit(solution)/shard_map/ppermute | solution.py:60
  65.2 2.0 %shard_map.86.refs_9_ = f32[4096,256]{1,0:T(8,128)S(1)} custom-call(s32[17]{0:T(128)S(1)} %get-tuple-element.11.base.refs_0_, s32[304]{0:T(512)S(1)} %get-tuple-element.12.slots.refs_1_, bf16[76,4,128,128]{3,2,1,0:T(8,128)(2,1)S(1)} %shard_map.83.packed.refs_2_, bf16[1040,256]{1,0:T(8,128)(2,1)S(1)} %shard_map.84.a.refs_3_, ...), custom_call_target="tpu_custom_call" | custom-call | flops 400000000 | bytes 8000000 | tf_op jit(solution)/shard_map/pallas_call | solution.py:285
  67.2 0.0 collective-permute-done.16.refs_8_
  67.2 3.8 %shard_map.87.refs_6_ = f32[4096,256]{1,0:T(8,128)S(1)} custom-call(s32[17]{0:T(128)S(1)} %get-tuple-element.11.base.refs_0_, s32[304]{0:T(512)S(1)} %get-tuple-element.12.slots.refs_1_, bf16[76,4,128,128]{3,2,1,0:T(8,128)(2,1)S(1)} %shard_map.83.packed.refs_2_, bf16[1040,256]{1,0:T(8,128)(2,1)S(1)} %collective-permute-done.10.refs_3_, ...), custom_call_target="tpu_custom_call" | custom-call | flops 400000000 | bytes 8000000 | tf_op jit(solution)/shard_map/pallas_call | solution.py:285
  71.0 0.0 copy-start.3
  71.0 0.0 copy-start.2
  71.0 1.2 %collective-permute-done.12.refs_4_ = bf16[1040,256]{1,0:T(8,128)(2,1)S(1)} collective-permute-done((bf16[1040,256]{1,0:T(8,128)(2,1)S(1)}, bf16[1040,256]{1,0:T(8,128)(2,1)S(1)}, u32[]{:S(2)}, u32[]{:S(2)}) %collective-permute-start.12) | collective-permute-done | bytes 532512 | tf_op jit(solution)/shard_map/ppermute | solution.py:60
  72.3 0.1 collective-permute-done.9.refs_3_
  72.3 3.8 %shard_map.88 = (bf16[2048,256]{1,0:T(8,128)(2,1)}, f32[2048,256]{1,0:T(8,128)S(1)}) custom-call(s32[17]{0:T(128)S(1)} %get-tuple-element.11.base.refs_0_, s32[304]{0:T(512)S(1)} %get-tuple-element.12.slots.refs_1_, bf16[76,4,128,128]{3,2,1,0:T(8,128)(2,1)S(1)} %shard_map.83.packed.refs_2_, bf16[2080,256]{1,0:T(8,128)(2,1)S(1)} %collective-permute-done.9.refs_3_, ...), custom_call_target="tpu_custom_call" | custom-call | flops 400000000 | bytes 8000000 | tf_op jit(solution)/shard_map/pallas_call | solution.py:285
  76.2 2.5 %collective-permute-start.17 = (bf16[2048,256]{1,0:T(8,128)(2,1)}, bf16[2048,256]{1,0:T(8,128)(2,1)S(1)}, u32[]{:S(2)}, u32[]{:S(2)}) collective-permute-start(bf16[2048,256]{1,0:T(8,128)(2,1)} %get-tuple-element.16), channel_id=1, source_target_pairs={{0,1},{1,0},{2,3},{3,2},{4,5},{5,4},{6,7},{7,6},{8,9},{9,8},{10,11... | collective-permute-start | bytes 3145736 | tf_op jit(solution)/shard_map/ppermute | solution.py:399
  78.7 2.5 %collective-permute-done.17.received = bf16[2048,256]{1,0:T(8,128)(2,1)S(1)} collective-permute-done((bf16[2048,256]{1,0:T(8,128)(2,1)}, bf16[2048,256]{1,0:T(8,128)(2,1)S(1)}, u32[]{:S(2)}, u32[]{:S(2)}) %collective-permute-start.17) | collective-permute-done | bytes 1048608 | tf_op jit(solution)/shard_map/ppermute | solution.py:399
  81.2 1.3 %shard_map.89 = bf16[2048,256]{1,0:T(8,128)(2,1)} custom-call(f32[2048,256]{1,0:T(8,128)S(1)} %get-tuple-element.15.kept, bf16[2048,256]{1,0:T(8,128)(2,1)S(1)} %collective-permute-done.17.received, f32[16,128]{1,0:T(8,128)S(1)} %dynamic-slice_bitcast_fusion.scale, bf16[256,256]{1,0:T(8,128)(2,1)S(1)} %copy-done.2, f32[1,256]{1,0:T(1,128)S(1)} %bitcast.19), custom_call_target="tpu_custom_call" | custom-call | flops 300000000 | bytes 6000000 | tf_op jit(solution)/shard_map/pallas_call | solution.py:319
  (17 shorter events, 0.2 us)
Async XLA Ops:
  0.0 78.7 %copy-start = (f32[4096]{0:T(1024)S(1)}, f32[4096]{0:T(1024)}, u32[]{:S(2)}) copy-start(f32[4096]{0:T(1024)} %param.10) | copy-start | bytes 49156
  0.0 23.8 %collective-permute-start = (s32[128,128,128]{2,1,0:T(8,128)}, s32[128,128,128]{2,1,0:T(8,128)}, u32[]{:S(2)}, u32[]{:S(2)}) collective-permute-start(s32[128,128,128]{2,1,0:T(8,128)} %bitcast.17), channel_id=1, source_target_pairs={{0,1},{1,0},{2,3},{3,2},{4,5},{5,4},{6,7},{7,6},{8,9},{9,8},{10,11... | collective-permute-start | bytes 25165832 | tf_op jit(solution)/shard_map/ppermute | solution.py:375
  4.8 18.0 %collective-permute-start.1 = (bf16[272,256]{1,0:T(8,128)(2,1)S(1)}, bf16[272,256]{1,0:T(8,128)(2,1)S(1)}, u32[]{:S(2)}, u32[]{:S(2)}) collective-permute-start(bf16[272,256]{1,0:T(8,128)(2,1)S(1)} %pad_maximum_fusion.own), channel_id=1, source_target_pairs={{4,0},{12,1},{6,2},{14,3},{0,4},{8,5},{2,6},{10,7},{5,8},{13,9},{7... | collective-permute-start | bytes 417800 | tf_op jit(solution)/shard_map/ppermute | solution.py:60
  9.1 13.8 %collective-permute-start.2 = (bf16[272,256]{1,0:T(8,128)(2,1)S(1)}, bf16[272,256]{1,0:T(8,128)(2,1)S(1)}, u32[]{:S(2)}, u32[]{:S(2)}) collective-permute-start(bf16[272,256]{1,0:T(8,128)(2,1)S(1)} %pad_maximum_fusion.own), channel_id=1, source_target_pairs={{6,0},{14,1},{0,2},{8,3},{2,4},{10,5},{4,6},{12,7},{7,8},{15,9},{1... | collective-permute-start | bytes 417800 | tf_op jit(solution)/shard_map/ppermute | solution.py:60
  10.2 12.7 %collective-permute-start.3 = (bf16[272,256]{1,0:T(8,128)(2,1)S(1)}, bf16[272,256]{1,0:T(8,128)(2,1)S(1)}, u32[]{:S(2)}, u32[]{:S(2)}) collective-permute-start(bf16[272,256]{1,0:T(8,128)(2,1)S(1)} %pad_maximum_fusion.own), channel_id=1, source_target_pairs={{2,0},{10,1},{4,2},{12,3},{6,4},{14,5},{0,6},{8,7},{3,8},{11,9},{5... | collective-permute-start | bytes 417800 | tf_op jit(solution)/shard_map/ppermute | solution.py:60
  12.0 11.7 %collective-permute-start.4 = (bf16[272,256]{1,0:T(8,128)(2,1)S(1)}, bf16[272,256]{1,0:T(8,128)(2,1)S(1)}, u32[]{:S(2)}, u32[]{:S(2)}) collective-permute-start(bf16[272,256]{1,0:T(8,128)(2,1)S(1)} %pad_maximum_fusion.own), channel_id=1, source_target_pairs={{8,1},{10,3},{12,5},{14,7},{1,8},{3,10},{5,12},{7,14},{24,17},{26,... | collective-permute-start | bytes 417800 | tf_op jit(solution)/shard_map/ppermute | solution.py:60
  23.8 4.4 %copy-start.1 = (s32[1,1,128,128,128]{4,3,2,1,0:T(8,128)S(1)}, s32[1,1,128,128,128]{4,3,2,1,0:T(8,128)}, u32[]{:S(2)}) copy-start(s32[1,1,128,128,128]{4,3,2,1,0:T(8,128)} %param.13) | copy-start | bytes 25165828
  23.8 14.5 %collective-permute-start.5 = (bf16[1040,256]{1,0:T(8,128)(2,1)S(1)}, bf16[1040,256]{1,0:T(8,128)(2,1)S(1)}, u32[]{:S(2)}, u32[]{:S(2)}) collective-permute-start(bf16[1040,256]{1,0:T(8,128)(2,1)S(1)} %shard_map.84.a.refs_3_), channel_id=1, source_target_pairs={{32,0},{129,1},{34,2},{131,3},{36,4},{133,5},{38,6},{135,7},{40,8}... | collective-permute-start | bytes 1597448 | tf_op jit(solution)/shard_map/ppermute | solution.py:60
  26.7 13.0 %collective-permute-start.6 = (bf16[1040,256]{1,0:T(8,128)(2,1)S(1)}, bf16[1040,256]{1,0:T(8,128)(2,1)S(1)}, u32[]{:S(2)}, u32[]{:S(2)}) collective-permute-start(bf16[1040,256]{1,0:T(8,128)(2,1)S(1)} %shard_map.84.a.refs_3_), channel_id=1, source_target_pairs={{16,0},{65,1},{18,2},{67,3},{20,4},{69,5},{22,6},{71,7},{24,8},{73... | collective-permute-start | bytes 1597448 | tf_op jit(solution)/shard_map/ppermute | solution.py:60
  27.5 12.2 %collective-permute-start.7 = (bf16[1040,256]{1,0:T(8,128)(2,1)S(1)}, bf16[1040,256]{1,0:T(8,128)(2,1)S(1)}, u32[]{:S(2)}, u32[]{:S(2)}) collective-permute-start(bf16[1040,256]{1,0:T(8,128)(2,1)S(1)} %shard_map.84.a.refs_3_), channel_id=1, source_target_pairs={{48,0},{193,1},{50,2},{195,3},{52,4},{197,5},{54,6},{199,7},{56,8}... | collective-permute-start | bytes 1597448 | tf_op jit(solution)/shard_map/ppermute | solution.py:60
  39.8 15.4 %collective-permute-start.8 = (bf16[2080,256]{1,0:T(8,128)(2,1)S(1)}, bf16[2080,256]{1,0:T(8,128)(2,1)S(1)}, u32[]{:S(2)}, u32[]{:S(2)}) collective-permute-start(bf16[2080,256]{1,0:T(8,128)(2,1)S(1)} %get-tuple-element.13.refs_4_), channel_id=1, source_target_pairs={{192,0},{49,1},{194,2},{51,3},{196,4},{53,5},{198,6},{55,7},{200,8... | collective-permute-start | bytes 3194888 | tf_op jit(solution)/shard_map/ppermute | solution.py:60
  41.0 8.4 %collective-permute-start.10 = (bf16[1040,256]{1,0:T(8,128)(2,1)S(1)}, bf16[1040,256]{1,0:T(8,128)(2,1)S(1)}, u32[]{:S(2)}, u32[]{:S(2)}) collective-permute-start(bf16[1040,256]{1,0:T(8,128)(2,1)S(1)} %get-tuple-element.14), channel_id=1, source_target_pairs={{64,0},{17,1},{66,2},{19,3},{68,4},{21,5},{70,6},{23,7},{72,8},{25... | collective-permute-start | bytes 1597448 | tf_op jit(solution)/shard_map/ppermute | solution.py:60
  42.6 24.7 %collective-permute-start.15 = (bf16[2080,256]{1,0:T(8,128)(2,1)S(1)}, bf16[2080,256]{1,0:T(8,128)(2,1)S(1)}, u32[]{:S(2)}, u32[]{:S(2)}) collective-permute-start(bf16[2080,256]{1,0:T(8,128)(2,1)S(1)} %get-tuple-element.13.refs_4_), channel_id=1, source_target_pairs={{64,0},{17,1},{66,2},{19,3},{68,4},{21,5},{70,6},{23,7},{72,8},{25... | collective-permute-start | bytes 3194888 | tf_op jit(solution)/shard_map/ppermute | solution.py:60
  43.8 17.1 %collective-permute-start.13 = (bf16[1040,256]{1,0:T(8,128)(2,1)S(1)}, bf16[1040,256]{1,0:T(8,128)(2,1)S(1)}, u32[]{:S(2)}, u32[]{:S(2)}) collective-permute-start(bf16[1040,256]{1,0:T(8,128)(2,1)S(1)} %get-tuple-element.14), channel_id=1, source_target_pairs={{192,0},{49,1},{194,2},{51,3},{196,4},{53,5},{198,6},{55,7},{200,8... | collective-permute-start | bytes 1597448 | tf_op jit(solution)/shard_map/ppermute | solution.py:60
  49.4 14.3 %collective-permute-start.11 = (bf16[1040,256]{1,0:T(8,128)(2,1)S(1)}, bf16[1040,256]{1,0:T(8,128)(2,1)S(1)}, u32[]{:S(2)}, u32[]{:S(2)}) collective-permute-start(bf16[1040,256]{1,0:T(8,128)(2,1)S(1)} %collective-permute-done.10.refs_3_), channel_id=1, source_target_pairs={{2,0},{15,1},{4,2},{1,3},{6,4},{3,5},{8,6},{5,7},{10,8},{7,9},{12,... | collective-permute-start | bytes 1597448 | tf_op jit(solution)/shard_map/ppermute | solution.py:60
  55.2 17.1 %collective-permute-start.9 = (bf16[2080,256]{1,0:T(8,128)(2,1)S(1)}, bf16[2080,256]{1,0:T(8,128)(2,1)S(1)}, u32[]{:S(2)}, u32[]{:S(2)}) collective-permute-start(bf16[2080,256]{1,0:T(8,128)(2,1)S(1)} %collective-permute-done.8.refs_5_), channel_id=1, source_target_pairs={{192,0},{49,1},{194,2},{51,3},{196,4},{53,5},{198,6},{55,7},{200,8... | collective-permute-start | bytes 3194888 | tf_op jit(solution)/shard_map/ppermute | solution.py:60
  55.2 12.0 %collective-permute-start.16 = (bf16[1040,256]{1,0:T(8,128)(2,1)S(1)}, bf16[1040,256]{1,0:T(8,128)(2,1)S(1)}, u32[]{:S(2)}, u32[]{:S(2)}) collective-permute-start(bf16[1040,256]{1,0:T(8,128)(2,1)S(1)} %collective-permute-done.10.refs_3_), channel_id=1, source_target_pairs={{64,0},{17,1},{66,2},{19,3},{68,4},{21,5},{70,6},{23,7},{72,8},{25... | collective-permute-start | bytes 1597448 | tf_op jit(solution)/shard_map/ppermute | solution.py:60
  60.9 10.1 %collective-permute-start.14 = (bf16[1040,256]{1,0:T(8,128)(2,1)S(1)}, bf16[1040,256]{1,0:T(8,128)(2,1)S(1)}, u32[]{:S(2)}, u32[]{:S(2)}) collective-permute-start(bf16[1040,256]{1,0:T(8,128)(2,1)S(1)} %collective-permute-done.13.refs_6_), channel_id=1, source_target_pairs={{14,0},{3,1},{0,2},{5,3},{2,4},{7,5},{4,6},{9,7},{6,8},{11,9},{8,1... | collective-permute-start | bytes 1597448 | tf_op jit(solution)/shard_map/ppermute | solution.py:60
  63.7 8.5 %collective-permute-start.12 = (bf16[1040,256]{1,0:T(8,128)(2,1)S(1)}, bf16[1040,256]{1,0:T(8,128)(2,1)S(1)}, u32[]{:S(2)}, u32[]{:S(2)}) collective-permute-start(bf16[1040,256]{1,0:T(8,128)(2,1)S(1)} %collective-permute-done.11.refs_4_), channel_id=1, source_target_pairs={{64,0},{17,1},{66,2},{19,3},{68,4},{21,5},{70,6},{23,7},{72,8},{25... | collective-permute-start | bytes 1597448 | tf_op jit(solution)/shard_map/ppermute | solution.py:60
  71.0 7.7 %copy-start.3 = (bf16[256]{0:T(256)(128)(2,1)S(1)}, bf16[256]{0:T(256)(128)(2,1)}, u32[]{:S(2)}) copy-start(bf16[256]{0:T(256)(128)(2,1)} %param.15) | copy-start | bytes 1540
  71.0 10.2 %copy-start.2 = (bf16[256,256]{1,0:T(8,128)(2,1)S(1)}, bf16[256,256]{1,0:T(8,128)(2,1)}, u32[]{:S(2)}) copy-start(bf16[256,256]{1,0:T(8,128)(2,1)} %weight.1) | copy-start | bytes 393220
  76.2 5.0 %collective-permute-start.17 = (bf16[2048,256]{1,0:T(8,128)(2,1)}, bf16[2048,256]{1,0:T(8,128)(2,1)S(1)}, u32[]{:S(2)}, u32[]{:S(2)}) collective-permute-start(bf16[2048,256]{1,0:T(8,128)(2,1)} %get-tuple-element.16), channel_id=1, source_target_pairs={{0,1},{1,0},{2,3},{3,2},{4,5},{5,4},{6,7},{7,6},{8,9},{9,8},{10,11... | collective-permute-start | bytes 3145736 | tf_op jit(solution)/shard_map/ppermute | solution.py:399
